TPU v7x, 256 devices: a whole 4x4x8 slice. The times are simulated.
256 devices in a mesh: section: 16 (over y, z_hi), tp: 16 (over x, z_lo, core).
Axes of the slice: x: 4, y: 4, z: 8 (z_hi: 4, z_lo: 2; z = z_hi * 2 + z_lo), core: 2. Of those that a mesh axis runs over, the one named last changes fastest.
Arguments:
- image_rows: bfloat16 [384, 8192], P('section', 'tp'), may hold values from -6 to 6
- queries: bfloat16 [16, 512, 8192], P('section', None, 'tp'), may hold values from -6 to 6
- key_weight: bfloat16 [16, 8192, 1024], P('section', 'tp'), may hold values from -0.0625 to 0.0625
- value_weight: bfloat16 [16, 8192, 1024], P('section', 'tp'), may hold values from -0.0625 to 0.0625
- query_gain: float32 [16, 128], P('section'), may hold values from 0.5 to 2
- key_gain: float32 [16, 128], P('section'), may hold values from 0.5 to 2
- tiles_seen: int32 [512], replicated, may hold values from 0 to 4
- context_grad: bfloat16 [16, 512, 8192], P('section', None, 'tp'), may hold values from -6 to 6
Outputs:
- context: bfloat16 [16, 512, 8192], P('section', None, 'tp')
- query_grad: bfloat16 [16, 512, 8192], P('section', None, 'tp')
- key_weight_grad: bfloat16 [16, 8192, 1024], P('section', 'tp')
- value_weight_grad: bfloat16 [16, 8192, 1024], P('section', 'tp')
- image_grad: float32 [384, 8192], P('section', 'tp')
Inputs may be any that keep to these rules, and one draw needn't show every extreme that they name: `tiles_seen`: tiles are counted from the image's first; 0 means the row attends no image row and its attention output is zero.
All inputs are finite; a program needn't handle non-finite values.
Results may differ from a plain program's by a relative error of at most 0.019.
Values may be sent and summed in bfloat16 or wider, within the bound.
No kernel may reach another device: no remote copies, remote signals or barrier semaphores. Data moves between devices by JAX's collectives and lax.ppermute only.
A program may use at most 64 MiB of HBM per device.

v0:
```python
import jax
import jax.numpy as jnp
from jax import lax
from jax.sharding import PartitionSpec as P

HEADS = 64
TILE_ROWS = 96


epsilon = 1e-05


def head_norm(raw_rows, gain_row):
    inverse = lax.rsqrt(jnp.mean(raw_rows * raw_rows, -1, keepdims=True) + epsilon)
    return (raw_rows * inverse * gain_row, inverse)


def head_norm_back(raw_rows, inverse, gain_row, upstream):
    scaled = upstream * gain_row
    return inverse * scaled - raw_rows * inverse**3 * jnp.mean(raw_rows * scaled, -1, keepdims=True)


def shards(
    image_rows, queries, key_weight, value_weight, query_gain, key_gain, tiles_seen, context_grad
):
    tp_index = lax.axis_index("tp")
    gathered = lax.all_gather(image_rows, "section", axis=0, tiled=True)
    img_total = gathered.shape[0]
    kv_width = key_weight.shape[2]
    head_size = query_gain.shape[1]
    kv_heads = kv_width // head_size
    heads_dev = queries.shape[2] // head_size
    group_size = HEADS // kv_heads
    kv_count = max(1, heads_dev // group_size)
    per_kv = heads_dev // kv_count
    kv_low = tp_index * heads_dev // group_size
    text_rows = queries.shape[1]
    score_scale = head_size ** (-0.5)
    key_gain_row = key_gain[0]
    query_gain_row = query_gain[0]
    kv_weight = jnp.concatenate([key_weight[0], value_weight[0]], 1)
    partial_value = jnp.dot(gathered, kv_weight, preferred_element_type=jnp.float32)
    kv_raw = lax.psum(partial_value, "tp")
    key_raw = kv_raw[:, :kv_width].reshape(img_total, kv_heads, head_size)
    keys_float, key_inverse = head_norm(key_raw, key_gain_row)
    kv_rounded = jnp.concatenate(
        [keys_float.reshape(img_total, kv_width), kv_raw[:, kv_width:]], 1
    ).astype(jnp.bfloat16)
    keys_dev = lax.dynamic_slice_in_dim(
        kv_rounded, kv_low * head_size, kv_count * head_size, 1
    ).reshape(img_total, kv_count, head_size)
    values_dev = lax.dynamic_slice_in_dim(
        kv_rounded, kv_width + kv_low * head_size, kv_count * head_size, 1
    ).reshape(img_total, kv_count, head_size)
    query_raw = queries[0].astype(jnp.float32).reshape(text_rows, kv_count, per_kv, head_size)
    normed_float, query_inverse = head_norm(query_raw, query_gain_row)
    normed = normed_float.astype(jnp.bfloat16)
    tile_index = jnp.arange(img_total, dtype=jnp.int32) // TILE_ROWS
    visible = tile_index[None, :] < tiles_seen[:, None]
    empty_row = (tiles_seen == 0).astype(jnp.float32)[:, None]
    scores = (
        jnp.einsum("tkgd,jkd->kgtj", normed, keys_dev, preferred_element_type=jnp.float32)
        * score_scale
    )
    expo = jnp.where(visible, jnp.exp(scores), 0.0)
    totals = jnp.sum(expo, -1, keepdims=True) + empty_row
    probs = expo / totals
    probs_low = probs.astype(jnp.bfloat16)
    context = jnp.einsum(
        "kgtj,jkd->tkgd", probs_low, values_dev, preferred_element_type=jnp.float32
    )
    context = context.astype(jnp.bfloat16).reshape(1, text_rows, heads_dev * head_size)
    upstream = context_grad[0].reshape(text_rows, kv_count, per_kv, head_size)
    prob_grad = jnp.einsum(
        "tkgd,jkd->kgtj", upstream, values_dev, preferred_element_type=jnp.float32
    )
    row_dot = jnp.sum(probs * prob_grad, -1, keepdims=True)
    score_grad = (probs * (prob_grad - row_dot)).astype(jnp.bfloat16)
    normed_grad = (
        jnp.einsum("kgtj,jkd->tkgd", score_grad, keys_dev, preferred_element_type=jnp.float32)
        * score_scale
    )
    query_grad = head_norm_back(query_raw, query_inverse, query_gain_row, normed_grad)
    query_grad = query_grad.astype(jnp.bfloat16).reshape(1, text_rows, heads_dev * head_size)
    key_grad = (
        jnp.einsum("kgtj,tkgd->jkd", score_grad, normed, preferred_element_type=jnp.float32)
        * score_scale
    )
    value_grad = jnp.einsum(
        "kgtj,tkgd->jkd", probs_low, upstream, preferred_element_type=jnp.float32
    )
    placed = jnp.zeros((img_total, 2 * kv_width), jnp.float32)
    placed = lax.dynamic_update_slice(
        placed, key_grad.reshape(img_total, kv_count * head_size), (0, kv_low * head_size)
    )
    placed = lax.dynamic_update_slice(
        placed,
        value_grad.reshape(img_total, kv_count * head_size),
        (0, kv_width + kv_low * head_size),
    )
    grad_total = lax.psum(placed, "tp")
    key_raw_grad = head_norm_back(
        key_raw,
        key_inverse,
        key_gain_row,
        grad_total[:, :kv_width].reshape(img_total, kv_heads, head_size),
    )
    kv_grad = jnp.concatenate(
        [key_raw_grad.reshape(img_total, kv_width), grad_total[:, kv_width:]], 1
    ).astype(jnp.bfloat16)
    weight_grad = lax.dot_general(
        gathered, kv_grad, (((0,), (0,)), ((), ())), preferred_element_type=jnp.float32
    ).astype(jnp.bfloat16)
    key_weight_grad = weight_grad[:, :kv_width][None]
    value_weight_grad = weight_grad[:, kv_width:][None]
    image_grad = lax.psum_scatter(
        lax.dot_general(
            kv_grad, kv_weight, (((1,), (1,)), ((), ())), preferred_element_type=jnp.float32
        ).astype(jnp.bfloat16),
        "section",
        scatter_dimension=0,
        tiled=True,
    ).astype(jnp.float32)
    return (context, query_grad, key_weight_grad, value_weight_grad, image_grad)


def solution(mesh):
    return jax.shard_map(
        shards,
        mesh=mesh,
        in_specs=(
            P("section", "tp"),
            P("section", None, "tp"),
            P("section", "tp", None),
            P("section", "tp", None),
            P("section", None),
            P("section", None),
            P(),
            P("section", None, "tp"),
        ),
        out_specs=(
            P("section", None, "tp"),
            P("section", None, "tp"),
            P("section", "tp", None),
            P("section", "tp", None),
            P("section", "tp"),
        ),
        check_vma=False,
    )
```

profile of v0, /device:TPU:1, one launch (start us, length us, event | category | flops | bytes accessed | tf_op | source)
XLA Modules:
  0.0 439.1 jit_solution(6747723316020241022)
XLA Ops:
  7.2 43.6 %all_gather.3 = bf16[384,512]{1,0:T(8,128)(2,1)S(1)} all-gather(bf16[24,512]{1,0:T(8,128)(2,1)} %param.8), channel_id=1, replica_groups=mesh['section'=16,'tp'=16] {'section'}, dimensions={0}, use_global_device_ids=true | all-gather | bytes 417792 | tf_op jit(solution)/shard_map/all_gather | solution.py:27
  50.8 4.7 %convolution_bitcast_fusion = f32[384,2048]{0,1:T(8,128)} fusion(bf16[384,512]{1,0:T(8,128)(2,1)S(1)} %all_gather.3, bf16[512,1024]{1,0:T(8,128)(2,1)} %bitcast.157, bf16[512,1024]{1,0:T(8,128)(2,1)} %bitcast.159), kind=kOutput, calls=%fused_computation.7 | convolution fusion | flops 809500672 | bytes 5636096 | tf_op jit(solution)/shard_map/dot_general | solution.py:42
  57.3 1.2 multiply_convert_fusion.1
  60.2 130.7 %all-reduce.3.cloned.1.call-done = f32[384,2048]{0,1:T(8,128)} async-done(((f32[384,2048]{0,1:T(8,128)}), f32[384,2048]{0,1:T(8,128)}) %all-reduce.3.cloned.1.call-update) | async-done | bytes 3145744 | tf_op jit(solution)/shard_map/psum | solution.py:43
  190.8 1.7 multiply_reduce_fusion.1
  192.5 1.5 slice.43
  195.5 1.3 fusion
  196.8 1.9 fusion.10
  198.7 1.8 broadcast_in_dim.27
  200.6 1.3 fusion.31
  201.8 1.7 fusion.26
  203.8 3.7 fusion.19
  207.6 2.0 copy.25
  209.6 2.3 multiply_reduce_fusion.2
  212.0 126.2 %all-reduce.5.cloned.1.call-done = f32[384,2048]{0,1:T(8,128)} async-done(((f32[384,2048]{0,1:T(8,128)}), f32[384,2048]{0,1:T(8,128)}) %all-reduce.5.cloned.1.call-update) | async-done | bytes 3145744 | tf_op jit(solution)/shard_map/psum | solution.py:101
  338.1 2.3 multiply_reduce_fusion
  340.5 1.6 slice.42
  342.1 1.8 fusion.9
  344.8 1.8 fusion.22
  347.9 2.5 fusion.3
  350.5 1.3 copy.27
  351.9 1.3 copy.28
  353.2 78.1 %reduce-scatter.2.cloned.1.call-done = bf16[24,512]{1,0:T(8,128)(2,1)} async-done(((bf16[384,512]{1,0:T(8,128)(2,1)}), bf16[24,512]{1,0:T(8,128)(2,1)}) %reduce-scatter.2.cloned.1.call-update) | async-done | bytes 24592 | tf_op jit(solution)/shard_map/reduce_scatter | solution.py:116
  431.2 1.4 convert_element_type.104
  (62 shorter events, 7.4 us)
Async XLA Ops:
  7.2 183.7 %all-reduce.3.cloned.1.call-start = ((), (), s32[]{:S(2)}) async-start(), calls=%async_computation.1 | async-start | bytes 6291456 | tf_op jit(solution)/shard_map/psum | solution.py:43
  50.8 4.7 %copy-start.11 = (bf16[384,512]{1,0:T(8,128)(2,1)}, bf16[384,512]{1,0:T(8,128)(2,1)S(1)}, u32[]{:S(2)}) copy-start(bf16[384,512]{1,0:T(8,128)(2,1)S(1)} %all_gather.3) | copy-start | bytes 1179652
  55.4 1.0 copy-start.5
  55.5 1.9 copy-start.13
  55.5 282.7 %all-reduce.5.cloned.1.call-start = ((), (), s32[]{:S(2)}) async-start(), calls=%async_computation.2 | async-start | bytes 6291456 | tf_op jit(solution)/shard_map/psum | solution.py:101
  57.0 3.0 copy-start.12
  57.0 3.0 copy-start.14
  59.9 135.6 %copy-start.9 = (bf16[512,4,128]{2,1,0:T(4,128)(2,1)}, bf16[512,4,128]{2,1,0:T(4,128)(2,1)S(1)}, u32[]{:S(2)}) copy-start(bf16[512,4,128]{2,1,0:T(4,128)(2,1)S(1)} %reshape.224) | copy-start | bytes 1572868
  60.1 135.4 %copy-start.6 = (pred[512,384]{0,1:T(8,128)(4,1)}, pred[512,384]{0,1:T(8,128)(4,1)S(1)}, u32[]{:S(2)}) copy-start(pred[512,384]{0,1:T(8,128)(4,1)S(1)} %broadcast_compare_fusion) | copy-start | bytes 589828
  190.8 3.2 copy-start
  194.3 2.5 copy-start.3
  195.5 6.4 %copy-start.2 = (f32[384,512,4]{1,0,2:T(8,128)}, f32[384,512,4]{1,0,2:T(8,128)S(1)}, u32[]{:S(2)}) copy-start(f32[384,512,4]{1,0,2:T(8,128)S(1)} %get-tuple-element.17) | copy-start | bytes 9437188
  198.7 3.2 copy-start.7
  198.7 3.1 copy-start.10
  203.6 227.6 %reduce-scatter.2.cloned.1.call-start = ((), (), s32[]{:S(2)}) async-start(), calls=%async_computation.3 | async-start | bytes 417792 | tf_op jit(solution)/shard_map/reduce_scatter | solution.py:116
  338.1 4.0 copy-start.1
  340.4 4.3 copy-start.15
  340.4 4.3 copy-start.16
  343.9 0.9 copy-start.8
  344.8 1.8 copy-start.4
Sparse Core Ops, SparseCore 0:
  55.6 135.1 all-reduce.2
  203.7 134.3 all-reduce.4
  346.7 84.4 reduce-scatter.1
where the time goes:
time: 441 us; the launch traced here: 439 us
  waiting for transfers between devices  335 us (76%)
  blocking collectives  43.6 us (10%)
  matrix products  20.4 us (5%)
  local copies, waits for them, and re-layouts  14.6 us (3%)
  between operations  14.1 us (3%)
  other arithmetic  11.1 us (3%)
    psum x1, waiting for transfers between devices, shards(): kv_raw = lax.psum(partial_value, 'tp')  131 us
    psum x1, waiting for transfers between devices, shards(): grad_total = lax.psum(placed, 'tp')  126 us
    reduce_scatter x1, waiting for transfers between devices, shards(): lax.psum_scatter(lax.dot_general(kv_grad, kv_weight, (((1,), (1,)), ((),...  78.1 us
    all_gather x1, blocking collectives, shards(): gathered = lax.all_gather(image_rows, 'section', axis=0, tiled=True)  43.6 us
  transfers between devices with their start and end apart: 3, of which 3 were waited for; matrix products, arithmetic and copies ran while one was open for 4% of the time, Pallas kernels for 0%

commit v1 on v0

v1 whole, which is shorter than its diff:
```python
import jax
import jax.numpy as jnp
from jax import lax
from jax.sharding import PartitionSpec as P

TILE_ROWS = 96
CORES = 2
epsilon = 1e-05

f32 = jnp.float32
bf16 = jnp.bfloat16


def head_norm(raw_rows, gain_row):
    inverse = lax.rsqrt(jnp.mean(raw_rows * raw_rows, -1, keepdims=True) + epsilon)
    return (raw_rows * inverse * gain_row, inverse)


def head_norm_back(raw_rows, inverse, gain_row, upstream):
    scaled = upstream * gain_row
    return inverse * scaled - raw_rows * inverse**3 * jnp.mean(raw_rows * scaled, -1, keepdims=True)


def shards(
    image_rows, queries, key_weight, value_weight, query_gain, key_gain, tiles_seen, context_grad
):
    sections = lax.axis_size("section")
    tp = lax.axis_size("tp")
    chips = tp // CORES
    core = lax.axis_index("tp") % CORES
    same_core = [[i for i in range(tp) if i % CORES == c] for c in range(CORES)]
    swap = [(i, i ^ 1) for i in range(tp)]

    def other_core(x):
        return lax.ppermute(x, "tp", swap)

    def over_chips(x):
        return lax.all_to_all(x, "tp", 0, 0, axis_index_groups=same_core)

    own_rows, features = image_rows.shape
    half = sections * own_rows // CORES
    kv_width = key_weight.shape[2]
    head = query_gain.shape[1]
    kv_heads = kv_width // head
    text = queries.shape[1]
    heads = queries.shape[2] // head
    score_scale = head ** (-0.5)
    key_gain_row, query_gain_row = key_gain[0], query_gain[0]

    blocks = lax.all_to_all(
        jnp.broadcast_to(image_rows[None], (sections, own_rows, features)), "section", 0, 0
    )
    halves = blocks.reshape(CORES, half, features)
    rows_mine = lax.dynamic_index_in_dim(halves, core, 0, keepdims=False)
    rows_other = lax.dynamic_index_in_dim(halves, 1 - core, 0, keepdims=False)

    def project(rows):
        k = jnp.dot(rows, key_weight[0], preferred_element_type=f32)
        v = jnp.dot(rows, value_weight[0], preferred_element_type=f32)
        both = jnp.concatenate(
            [k.reshape(half, kv_heads, head), v.reshape(half, kv_heads, head)], -1
        )
        return both.transpose(1, 0, 2)

    received = other_core(project(rows_other).astype(bf16))
    partial = (project(rows_mine) + received.astype(f32)).astype(bf16)
    kv_raw = jnp.sum(over_chips(partial).astype(f32), 0)
    key_raw = kv_raw[:, :head]
    keys_float, key_inverse = head_norm(key_raw, key_gain_row)
    kv_mine = jnp.concatenate([keys_float, kv_raw[:, head:]], 1).astype(bf16)
    kv_all = jnp.concatenate([kv_mine, other_core(kv_mine)], 0)
    keys, values = kv_all[:, :head], kv_all[:, head:]

    query_raw = queries[0].reshape(text, heads, head).transpose(1, 0, 2).astype(f32)
    upstream = context_grad[0].reshape(text, heads, head).transpose(1, 0, 2)
    normed_float, query_inverse = head_norm(query_raw, query_gain_row)
    normed = normed_float.astype(bf16)
    local = jnp.arange(CORES * half, dtype=jnp.int32)
    row = jnp.where(local < half, local + core * half, local - core * half)
    visible = (row // TILE_ROWS)[None, :] < tiles_seen[:, None]
    empty_row = (tiles_seen == 0).astype(f32)[:, None]
    scores = jnp.einsum("htd,jd->htj", normed, keys, preferred_element_type=f32) * score_scale
    expo = jnp.where(visible, jnp.exp(scores), 0.0)
    totals = jnp.sum(expo, -1, keepdims=True) + empty_row
    probs = expo / totals
    probs_low = probs.astype(bf16)
    prob_grad = jnp.einsum("htd,jd->htj", upstream, values, preferred_element_type=f32)
    row_dot = jnp.sum(probs * prob_grad, -1, keepdims=True)
    score_grad = (probs * (prob_grad - row_dot)).astype(bf16)
    key_grad = jnp.einsum("htj,htd->jd", score_grad, normed, preferred_element_type=f32) * score_scale
    value_grad = jnp.einsum("htj,htd->jd", probs_low, upstream, preferred_element_type=f32)
    kv_grad_part = jnp.concatenate([key_grad, value_grad], 1)
    received = other_core(kv_grad_part[half:].astype(bf16))
    kv_grad_raw = kv_grad_part[:half] + received.astype(f32)
    key_raw_grad = head_norm_back(key_raw, key_inverse, key_gain_row, kv_grad_raw[:, :head])
    kv_grad = jnp.concatenate([key_raw_grad, kv_grad_raw[:, head:]], 1).astype(bf16)
    grads_mine = over_chips(jnp.broadcast_to(kv_grad[None], (chips, half, 2 * head)))
    grads_other = other_core(grads_mine)

    context = jnp.einsum("htj,jd->thd", probs_low, values, preferred_element_type=f32)
    context = context.astype(bf16).reshape(1, text, heads * head)
    normed_grad = (
        jnp.einsum("htj,jd->htd", score_grad, keys, preferred_element_type=f32) * score_scale
    )
    query_grad = head_norm_back(query_raw, query_inverse, query_gain_row, normed_grad)
    query_grad = query_grad.astype(bf16).transpose(1, 0, 2).reshape(1, text, heads * head)

    grads = jnp.concatenate([grads_mine, grads_other], 1).transpose(1, 0, 2)
    key_grads = grads[:, :, :head].reshape(CORES * half, kv_width)
    value_grads = grads[:, :, head:].reshape(CORES * half, kv_width)
    image_part = lax.dot_general(
        key_grads, key_weight[0], (((1,), (1,)), ((), ())), preferred_element_type=f32
    ) + lax.dot_general(
        value_grads, value_weight[0], (((1,), (1,)), ((), ())), preferred_element_type=f32
    )
    image_part = image_part.astype(bf16).reshape(CORES, half, features)
    image_part = jnp.where(core == 0, image_part, image_part[::-1])
    image_grad = lax.all_to_all(
        image_part.reshape(sections, own_rows, features), "section", 0, 0
    )
    image_grad = jnp.sum(image_grad.astype(f32), 0)
    image_local = jnp.concatenate([rows_mine, rows_other], 0)

    def weight_grad(column_grads):
        return lax.dot_general(
            image_local, column_grads, (((0,), (0,)), ((), ())), preferred_element_type=f32
        ).astype(bf16)[None]

    return (context, query_grad, weight_grad(key_grads), weight_grad(value_grads), image_grad)


def solution(mesh):
    return jax.shard_map(
        shards,
        mesh=mesh,
        in_specs=(
            P("section", "tp"),
            P("section", None, "tp"),
            P("section", "tp", None),
            P("section", "tp", None),
            P("section", None),
            P("section", None),
            P(),
            P("section", None, "tp"),
        ),
        out_specs=(
            P("section", None, "tp"),
            P("section", None, "tp"),
            P("section", "tp", None),
            P("section", "tp", None),
            P("section", "tp"),
        ),
        check_vma=False,
    )
```

time: 441 us -> 112 us (0.25)
  waiting for transfers between devices: 335 us -> 47.2 us
  blocking collectives: 43.6 us -> 0 us
  starting transfers between devices: 0.3 us -> 29.5 us
  between operations: 14.1 us -> 1.14 us
  matrix products: 20.4 us -> 14.7 us
  other arithmetic: 11.1 us -> 6.66 us
    psum x2 -> x0, waiting for transfers between devices: 257 us -> none  [the longest x1 131 us: shards(): kv_raw = lax.psum(partial_value, 'tp')]
    reduce_scatter x1 -> x0, waiting for transfers between devices: 78.1 us -> none  [shards(): lax.psum_scatter(lax.dot_general(kv_grad, kv_weight, (((1,), (1,)), ((),...]
    all_to_all x0 -> x4, waiting for transfers between devices: none -> 44.9 us  [the longest x2 24.3 us: over_chips(): return lax.all_to_all(x, 'tp', 0, 0, axis_index_groups=same_core)]
    all_gather x1 -> x0, blocking collectives: 43.6 us -> none  [shards(): gathered = lax.all_gather(image_rows, 'section', axis=0, tiled=True)]
    all_to_all x0 -> x4, starting transfers between devices: none -> 24.2 us  [the longest x1 11.7 us: shards(): lax.all_to_all(jnp.broadcast_to(image_rows[None], (sections, own_rows, fe...]
    dot_general x9 -> x14, matrix products: 20.4 us -> 14.7 us  [the longest x2 3.46 us: weight_grad(): lax.dot_general(image_local, column_grads, (((0,), (0,)), ((), ())), pref...]
    ppermute x0 -> x4, starting transfers between devices: none -> 5.33 us  [other_core(): return lax.ppermute(x, 'tp', swap)]
    unnamed x38 -> x26, local copies, waits for them, and re-layouts: 7.58 us -> 2.54 us
  transfers between devices with their start and end apart: 3 -> 8, of which waited for: 3 -> 6; matrix products, arithmetic and copies ran while one was open for 4% -> 15% of each run, Pallas kernels for 0% -> 0%
where the time goes in v1:
time: 112 us; the launch traced here: 111 us
  waiting for transfers between devices  47.2 us (42%)
  starting transfers between devices  29.5 us (26%)
  matrix products  14.7 us (13%)
  local copies, waits for them, and re-layouts  11.7 us (10%)
  other arithmetic  6.66 us (6%)
  between operations  1.14 us (1%)
    all_to_all x2, waiting for transfers between devices, over_chips(): return lax.all_to_all(x, 'tp', 0, 0, axis_index_groups=same_core)  24.3 us
    all_to_all x1, waiting for transfers between devices, shards(): lax.all_to_all(jnp.broadcast_to(image_rows[None], (sections, own_rows, fe...  12.6 us
    all_to_all x1, starting transfers between devices, shards(): lax.all_to_all(jnp.broadcast_to(image_rows[None], (sections, own_rows, fe...  11.7 us
    all_to_all x2, starting transfers between devices, over_chips(): return lax.all_to_all(x, 'tp', 0, 0, axis_index_groups=same_core)  8.9 us
    all_to_all x1, waiting for transfers between devices, shards(): lax.all_to_all(image_part.reshape(sections, own_rows, features), 'section...  8.04 us
    ppermute x4, starting transfers between devices, other_core(): return lax.ppermute(x, 'tp', swap)  5.33 us
    all_to_all x1, starting transfers between devices, shards(): lax.all_to_all(image_part.reshape(sections, own_rows, features), 'section...  3.55 us
    dot_general x2, matrix products, weight_grad(): lax.dot_general(image_local, column_grads, (((0,), (0,)), ((), ())), pref...  3.46 us
  transfers between devices with their start and end apart: 8, of which 6 were waited for; matrix products, arithmetic and copies ran while one was open for 15% of the time, Pallas kernels for 0%

profile of v1, /device:TPU:1, one launch (start us, length us, event | category | flops | bytes accessed | tf_op | source)
XLA Modules:
  0.0 110.9 jit_solution(13680708635452023294)
XLA Ops:
  0.6 1.6 %broadcast_in_dim.16 = bf16[16,24,512]{2,1,0:T(8,128)(2,1)} broadcast(bf16[24,512]{1,0:T(8,128)(2,1)} %param.8), dimensions={1,2} | broadcast | bytes 417792 | tf_op jit(solution)/shard_map/broadcast_in_dim | solution.py:51
  2.2 11.7 %all-to-all-start = ((bf16[16,24,512]{2,1,0:T(8,128)(2,1)}), bf16[16,24,512]{2,1,0:T(8,128)(2,1)S(1)}, u32[]{:S(2)}, u32[]{:S(2)}) async-start(bf16[16,24,512]{2,1,0:T(8,128)(2,1)} %broadcast_in_dim.16), calls=%async_computation | async-start | bytes 786432 | tf_op jit(solution)/shard_map/all_to_all | solution.py:50
  14.0 1.5 %copy.86 = bf16[1024,512]{1,0:T(8,128)(2,1)S(1)} copy(bf16[1024,512]{0,1:T(8,128)(2,1)} %bitcast.131) | data formatting | bytes 2097152 | tf_op jit(solution)/shard_map/dot_general | solution.py:59
  16.1 12.6 %all-to-all-done = bf16[16,24,512]{2,1,0:T(8,128)(2,1)S(1)} async-done(((bf16[16,24,512]{2,1,0:T(8,128)(2,1)}), bf16[16,24,512]{2,1,0:T(8,128)(2,1)S(1)}, u32[]{:S(2)}, u32[]{:S(2)}) %all-to-all-start) | async-done | bytes 393248 | tf_op jit(solution)/shard_map/all_to_all | solution.py:50
  29.8 2.3 %collective-permute-start = (bf16[8,192,256]{2,1,0:T(8,128)(2,1)S(1)}, bf16[8,192,256]{2,1,0:T(8,128)(2,1)}, u32[]{:S(2)}, u32[]{:S(2)}) collective-permute-start(bf16[8,192,256]{2,1,0:T(8,128)(2,1)S(1)} %maximum_bitcast_fusion.2), channel_id=1, source_target_pairs={{0,1},{1,0},{2,3},{3,2},{4,5},{5,4},{6,7},{7,6},{8,9},{9,8},{10,11... | collective-permute-start | bytes 2359304 | tf_op jit(solution)/shard_map/ppermute | solution.py:35
  33.1 1.0 collective-permute-done
  34.2 2.2 %fusion.6 = bf16[8,192,256]{2,1,0:T(8,128)(2,1)} fusion(f32[192,8,128]{2,0,1:T(8,128)S(1)} %fusion.23, f32[192,8,128]{2,0,1:T(8,128)S(1)} %fusion.25, bf16[8,192,256]{2,1,0:T(8,128)(2,1)} %collective-permute-done), kind=kLoop, calls=%fused_computation.10 | loop fusion | flops 1572864 | bytes 3145728 | tf_op jit(solution)/shard_map/convert_element_type | solution.py:66
  36.4 4.7 %all-to-all-start.1 = ((bf16[8,192,256]{2,1,0:T(8,128)(2,1)}), bf16[8,192,256]{2,1,0:T(8,128)(2,1)S(1)}, u32[]{:S(2)}, u32[]{:S(2)}) async-start(bf16[8,192,256]{2,1,0:T(8,128)(2,1)} %fusion.6), calls=%async_computation.1 | async-start | bytes 1572864 | tf_op jit(solution)/shard_map/all_to_all | solution.py:38
  41.7 11.4 %all-to-all-done.1 = bf16[8,192,256]{2,1,0:T(8,128)(2,1)S(1)} async-done(((bf16[8,192,256]{2,1,0:T(8,128)(2,1)}), bf16[8,192,256]{2,1,0:T(8,128)(2,1)S(1)}, u32[]{:S(2)}, u32[]{:S(2)}) %all-to-all-start.1) | async-done | bytes 786464 | tf_op jit(solution)/shard_map/all_to_all | solution.py:38
  53.5 1.9 %collective-permute-start.1 = (bf16[192,256]{1,0:T(8,128)(2,1)S(1)}, bf16[192,256]{1,0:T(8,128)(2,1)S(1)}, u32[]{:S(2)}, u32[]{:S(2)}) collective-permute-start(bf16[192,256]{1,0:T(8,128)(2,1)S(1)} %pad_maximum_fusion.5), channel_id=1, source_target_pairs={{0,1},{1,0},{2,3},{3,2},{4,5},{5,4},{6,7},{7,6},{8,9},{9,8},{10,11... | collective-permute-start | bytes 294920 | tf_op jit(solution)/shard_map/ppermute | solution.py:35
  55.4 1.3 %copy.81 = bf16[1,512,512]{1,2,0:T(8,128)(2,1)S(1)} copy(bf16[1,512,512]{2,1,0:T(8,128)(2,1)} %param.15) | data formatting | bytes 1048576 | tf_op jit(solution)/shard_map/reshape;squeeze | solution.py:75
  56.7 1.0 fusion.4
  58.7 1.1 %fusion = (f32[4,512]{1,0:T(4,128)S(1)}, f32[384,4,512]{2,0,1:T(8,128)S(1)}) fusion(f32[4,512]{1,0:T(4,128)S(1)} %broadcast_add_fusion, f32[4,512,384]{1,2,0:T(8,128)S(1)} %get-tuple-element.29, pred[512,384]{0,1:T(8,128)(4,1)S(1)} %broadcast_compare_fusion, bf16[4,512,128]{1,2,0:T(8,128)(2,1)S(1)} %bitcast.135, bf16[384,256]{1,0:T(8,128)(2,1)S(1)} %pad_maximum_fusion.4), kind=kOutput, calls=%fused_computation.2 | convolution fusion | flops 205256704 | bytes 7127040 | tf_op jit(solution)/shard_map/htd,jd->htj/dot_general | solution.py:87
  61.5 1.3 %collective-permute-done.2 = bf16[192,256]{1,0:T(8,128)(2,1)S(1)} collective-permute-done((bf16[192,256]{1,0:T(8,128)(2,1)S(1)}, bf16[192,256]{1,0:T(8,128)(2,1)S(1)}, u32[]{:S(2)}, u32[]{:S(2)}) %collective-permute-start.2) | collective-permute-done | bytes 98336 | tf_op jit(solution)/shard_map/ppermute | solution.py:35
  64.1 4.2 %all-to-all-start.2 = ((bf16[8,192,256]{2,1,0:T(8,128)(2,1)}), bf16[8,192,256]{2,1,0:T(8,128)(2,1)}, u32[]{:S(2)}, u32[]{:S(2)}) async-start(bf16[8,192,256]{2,1,0:T(8,128)(2,1)} %broadcast_in_dim.19), calls=%async_computation.2 | async-start | bytes 1572864 | tf_op jit(solution)/shard_map/all_to_all | solution.py:38
  68.4 12.9 %all-to-all-done.2 = bf16[8,192,256]{2,1,0:T(8,128)(2,1)} async-done(((bf16[8,192,256]{2,1,0:T(8,128)(2,1)}), bf16[8,192,256]{2,1,0:T(8,128)(2,1)}, u32[]{:S(2)}, u32[]{:S(2)}) %all-to-all-start.2) | async-done | bytes 786464 | tf_op jit(solution)/shard_map/all_to_all | solution.py:38
  82.2 1.4 %multiply_reduce_fusion = (f32[4,512]{1,0:T(4,128)S(1)}, f32[4,512,128]{1,2,0:T(8,128)S(1)}) fusion(f32[4,512,128]{1,2,0:T(8,128)S(1)} %bitcast.115, f32[128]{0:T(128)S(1)} %broadcast_multiply_fusion.1, bf16[4,512,384]{1,2,0:T(8,128)(2,1)S(1)} %fusion.2, bf16[384,256]{1,0:T(8,128)(2,1)} %copy-done.7), kind=kOutput, calls=%fused_computation.32 | convolution fusion | flops 202110976 | bytes 3777024 | tf_op jit(solution)/shard_map/htj,jd->htd/dot_general | solution.py:103
  84.9 1.4 %copy.66 = bf16[8,192,256]{1,2,0:T(8,128)(2,1)S(1)} copy(bf16[8,192,256]{2,1,0:T(8,128)(2,1)} %all-to-all-done.2) | data formatting | bytes 1572864 | tf_op jit(solution)/shard_map/all_to_all | solution.py:38
  86.4 1.4 %copy.67 = bf16[8,192,256]{1,2,0:T(8,128)(2,1)S(1)} copy(bf16[8,192,256]{2,1,0:T(8,128)(2,1)} %collective-permute-done.3) | data formatting | bytes 1572864 | tf_op jit(solution)/shard_map/ppermute | solution.py:35
  91.2 3.6 %all-to-all-start.3 = ((bf16[16,24,512]{2,1,0:T(8,128)(2,1)}), bf16[16,24,512]{2,1,0:T(8,128)(2,1)S(1)}, u32[]{:S(2)}, u32[]{:S(2)}) async-start(bf16[16,24,512]{2,1,0:T(8,128)(2,1)} %bitcast.38), calls=%async_computation.3 | async-start | bytes 786432 | tf_op jit(solution)/shard_map/all_to_all | solution.py:118
  94.8 2.9 %convolution_convert_fusion.2 = bf16[128,4,512]{2,0,1:T(8,128)(2,1)S(1)} fusion(bf16[384,256]{1,0:T(8,128)(2,1)S(1)} %copy-done.8, f32[4,512,384]{1,2,0:T(8,128)} %copy-done.3, f32[4,512]{1,0:T(4,128)S(1)} %broadcast_add_fusion, pred[512,384]{0,1:T(8,128)(4,1)S(1)} %copy-done.5), kind=kOutput, calls=%fused_computation.19 | convolution fusion | flops 204734464 | bytes 3973120 | tf_op jit(solution)/shard_map/htj,jd->thd/dot_general | solution.py:100
  98.7 1.7 %fusion.8 = bf16[1,512,1024]{2,1,0:T(8,128)(2,1)} fusion(bf16[384,1024]{0,1:T(8,128)(2,1)S(1)} %bitcast.124, bf16[192,512]{1,0:T(8,128)(2,1)S(1)} %get-tuple-element.23, bf16[192,512]{1,0:T(8,128)(2,1)S(1)} %get-tuple-element.22), kind=kOutput, calls=%fused_computation.16 | convolution fusion | flops 403963904 | bytes 2228224 | tf_op jit(solution)/shard_map/dot_general | solution.py:125
  100.4 1.7 %fusion.7 = bf16[1,512,1024]{2,1,0:T(8,128)(2,1)} fusion(bf16[384,1024]{0,1:T(8,128)(2,1)S(1)} %bitcast.122, bf16[192,512]{1,0:T(8,128)(2,1)S(1)} %get-tuple-element.23, bf16[192,512]{1,0:T(8,128)(2,1)S(1)} %get-tuple-element.22), kind=kOutput, calls=%fused_computation.15 | convolution fusion | flops 403963904 | bytes 2228224 | tf_op jit(solution)/shard_map/dot_general | solution.py:125
  102.1 8.0 %all-to-all-done.3 = bf16[16,24,512]{2,1,0:T(8,128)(2,1)S(1)} async-done(((bf16[16,24,512]{2,1,0:T(8,128)(2,1)}), bf16[16,24,512]{2,1,0:T(8,128)(2,1)S(1)}, u32[]{:S(2)}, u32[]{:S(2)}) %all-to-all-start.3) | async-done | bytes 393248 | tf_op jit(solution)/shard_map/all_to_all | solution.py:118
  (72 shorter events, 14.7 us)
Async XLA Ops:
  0.6 14.9 %copy-start = (bf16[1,512,1024]{2,1,0:T(8,128)(2,1)S(1)}, bf16[1,512,1024]{2,1,0:T(8,128)(2,1)}, u32[]{:S(2)}) copy-start(bf16[1,512,1024]{2,1,0:T(8,128)(2,1)} %param.10) | copy-start | bytes 3145732
  2.2 26.4 %all-to-all-start = ((bf16[16,24,512]{2,1,0:T(8,128)(2,1)}), bf16[16,24,512]{2,1,0:T(8,128)(2,1)S(1)}, u32[]{:S(2)}, u32[]{:S(2)}) async-start(bf16[16,24,512]{2,1,0:T(8,128)(2,1)} %broadcast_in_dim.16), calls=%async_computation | async-start | bytes 786432 | tf_op jit(solution)/shard_map/all_to_all | solution.py:50
  29.8 4.4 %collective-permute-start = (bf16[8,192,256]{2,1,0:T(8,128)(2,1)S(1)}, bf16[8,192,256]{2,1,0:T(8,128)(2,1)}, u32[]{:S(2)}, u32[]{:S(2)}) collective-permute-start(bf16[8,192,256]{2,1,0:T(8,128)(2,1)S(1)} %maximum_bitcast_fusion.2), channel_id=1, source_target_pairs={{0,1},{1,0},{2,3},{3,2},{4,5},{5,4},{6,7},{7,6},{8,9},{9,8},{10,11... | collective-permute-start | bytes 2359304 | tf_op jit(solution)/shard_map/ppermute | solution.py:35
  32.6 8.5 %copy-start.6 = (bf16[1,512,512]{2,1,0:T(8,128)(2,1)S(1)}, bf16[1,512,512]{2,1,0:T(8,128)(2,1)}, u32[]{:S(2)}) copy-start(bf16[1,512,512]{2,1,0:T(8,128)(2,1)} %param.9) | copy-start | bytes 1572868
  33.1 8.4 %copy-start.9 = (s32[512]{0:T(512)S(1)}, s32[512]{0:T(512)}, u32[]{:S(2)}) copy-start(s32[512]{0:T(512)} %param.14) | copy-start | bytes 6148
  36.4 17.0 %copy-start.10 = (f32[1,128]{1,0:T(1,128)S(1)}, f32[1,128]{1,0:T(1,128)}, u32[]{:S(2)}) copy-start(f32[1,128]{1,0:T(1,128)} %param.13) | copy-start | bytes 1540
  36.4 16.7 %all-to-all-start.1 = ((bf16[8,192,256]{2,1,0:T(8,128)(2,1)}), bf16[8,192,256]{2,1,0:T(8,128)(2,1)S(1)}, u32[]{:S(2)}, u32[]{:S(2)}) async-start(bf16[8,192,256]{2,1,0:T(8,128)(2,1)} %fusion.6), calls=%async_computation.1 | async-start | bytes 1572864 | tf_op jit(solution)/shard_map/all_to_all | solution.py:38
  41.1 15.6 %copy-start.11 = (f32[1,128]{1,0:T(1,128)S(1)}, f32[1,128]{1,0:T(1,128)}, u32[]{:S(2)}) copy-start(f32[1,128]{1,0:T(1,128)} %param.12) | copy-start | bytes 1540
  41.7 18.1 %copy-start.4 = (pred[512,384]{0,1:T(8,128)(4,1)}, pred[512,384]{0,1:T(8,128)(4,1)S(1)}, u32[]{:S(2)}) copy-start(pred[512,384]{0,1:T(8,128)(4,1)S(1)} %broadcast_compare_fusion) | copy-start | bytes 589828
  53.5 3.2 %collective-permute-start.1 = (bf16[192,256]{1,0:T(8,128)(2,1)S(1)}, bf16[192,256]{1,0:T(8,128)(2,1)S(1)}, u32[]{:S(2)}, u32[]{:S(2)}) collective-permute-start(bf16[192,256]{1,0:T(8,128)(2,1)S(1)} %pad_maximum_fusion.5), channel_id=1, source_target_pairs={{0,1},{1,0},{2,3},{3,2},{4,5},{5,4},{6,7},{7,6},{8,9},{9,8},{10,11... | collective-permute-start | bytes 294920 | tf_op jit(solution)/shard_map/ppermute | solution.py:35
  56.7 1.9 %copy-start.7 = (bf16[384,256]{1,0:T(8,128)(2,1)}, bf16[384,256]{1,0:T(8,128)(2,1)S(1)}, u32[]{:S(2)}) copy-start(bf16[384,256]{1,0:T(8,128)(2,1)S(1)} %pad_maximum_fusion.4) | copy-start | bytes 589828
  57.8 2.0 %copy-start.3 = (f32[4,512,384]{1,2,0:T(8,128)}, f32[4,512,384]{1,2,0:T(8,128)S(1)}, u32[]{:S(2)}) copy-start(f32[4,512,384]{1,2,0:T(8,128)S(1)} %get-tuple-element.29) | copy-start | bytes 9437188
  61.4 1.4 %collective-permute-start.2 = (bf16[192,256]{1,0:T(8,128)(2,1)S(1)}, bf16[192,256]{1,0:T(8,128)(2,1)S(1)}, u32[]{:S(2)}, u32[]{:S(2)}) collective-permute-start(bf16[192,256]{1,0:T(8,128)(2,1)S(1)} %fusion.20), channel_id=1, source_target_pairs={{0,1},{1,0},{2,3},{3,2},{4,5},{5,4},{6,7},{7,6},{8,9},{9,8},{10,11... | collective-permute-start | bytes 294920 | tf_op jit(solution)/shard_map/ppermute | solution.py:35
  64.1 17.1 %all-to-all-start.2 = ((bf16[8,192,256]{2,1,0:T(8,128)(2,1)}), bf16[8,192,256]{2,1,0:T(8,128)(2,1)}, u32[]{:S(2)}, u32[]{:S(2)}) async-start(bf16[8,192,256]{2,1,0:T(8,128)(2,1)} %broadcast_in_dim.19), calls=%async_computation.2 | async-start | bytes 1572864 | tf_op jit(solution)/shard_map/all_to_all | solution.py:38
  81.2 5.2 %collective-permute-start.3 = (bf16[8,192,256]{2,1,0:T(8,128)(2,1)}, bf16[8,192,256]{2,1,0:T(8,128)(2,1)}, u32[]{:S(2)}, u32[]{:S(2)}) collective-permute-start(bf16[8,192,256]{2,1,0:T(8,128)(2,1)} %all-to-all-done.2), channel_id=1, source_target_pairs={{0,1},{1,0},{2,3},{3,2},{4,5},{5,4},{6,7},{7,6},{8,9},{9,8},{10,11... | collective-permute-start | bytes 2359304 | tf_op jit(solution)/shard_map/ppermute | solution.py:35
  87.8 1.2 %copy-start.2 = (bf16[1,512,1024]{2,1,0:T(8,128)(2,1)S(1)}, bf16[1,512,1024]{2,1,0:T(8,128)(2,1)}, u32[]{:S(2)}) copy-start(bf16[1,512,1024]{2,1,0:T(8,128)(2,1)} %param.11) | copy-start | bytes 3145732
  88.4 1.3 %copy-start.1 = (bf16[1,512,1024]{2,1,0:T(8,128)(2,1)S(1)}, bf16[1,512,1024]{2,1,0:T(8,128)(2,1)}, u32[]{:S(2)}) copy-start(bf16[1,512,1024]{2,1,0:T(8,128)(2,1)} %param.10) | copy-start | bytes 3145732
  89.1 5.7 %copy-start.5 = (pred[512,384]{0,1:T(8,128)(4,1)S(1)}, pred[512,384]{0,1:T(8,128)(4,1)}, u32[]{:S(2)}) copy-start(pred[512,384]{0,1:T(8,128)(4,1)} %copy-done.4) | copy-start | bytes 589828
  89.1 5.7 %copy-start.8 = (bf16[384,256]{1,0:T(8,128)(2,1)S(1)}, bf16[384,256]{1,0:T(8,128)(2,1)}, u32[]{:S(2)}) copy-start(bf16[384,256]{1,0:T(8,128)(2,1)} %copy-done.7) | copy-start | bytes 589828
  91.2 19.0 %all-to-all-start.3 = ((bf16[16,24,512]{2,1,0:T(8,128)(2,1)}), bf16[16,24,512]{2,1,0:T(8,128)(2,1)S(1)}, u32[]{:S(2)}, u32[]{:S(2)}) async-start(bf16[16,24,512]{2,1,0:T(8,128)(2,1)} %bitcast.38), calls=%async_computation.3 | async-start | bytes 786432 | tf_op jit(solution)/shard_map/all_to_all | solution.py:118

commit v2 on v1

v2 whole, which is shorter than its diff:
```python
import functools

import jax
import jax.numpy as jnp
from jax import lax
from jax.experimental import pallas as pl
from jax.experimental.pallas import tpu as pltpu
from jax.sharding import PartitionSpec as P

TILE_ROWS = 96
CORES = 2
TEXT_STEP = 256
epsilon = 1e-05

f32 = jnp.float32
bf16 = jnp.bfloat16

BOTH_LAST = (((1,), (1,)), ((), ()))
BOTH_FIRST = (((0,), (0,)), ((), ()))

VMEM = pl.BlockSpec(memory_space=pltpu.VMEM)
SMEM = pl.BlockSpec(memory_space=pltpu.SMEM)
PARAMS = pltpu.CompilerParams(vmem_limit_bytes=40 * 1024 * 1024)


def dot(a, b, dims=(((1,), (0,)), ((), ()))):
    return lax.dot_general(a, b, dims, preferred_element_type=f32)


def head_norm(raw_rows, gain_row):
    inverse = lax.rsqrt(jnp.mean(raw_rows * raw_rows, -1, keepdims=True) + epsilon)
    return (raw_rows * inverse * gain_row, inverse)


def head_norm_back(raw_rows, inverse, gain_row, upstream):
    scaled = upstream * gain_row
    return inverse * scaled - raw_rows * (
        inverse * inverse * inverse * jnp.mean(raw_rows * scaled, -1, keepdims=True)
    )


def half_rows(ref, which, half):
    return ref[pl.ds(pl.multiple_of(which * half, half), half), :]


def project_kernel(add, core_ref, rows_ref, key_ref, value_ref, *refs):
    out_ref = refs[-1]
    kv_heads, half, width = out_ref.shape
    head = width // 2
    core = core_ref[0]
    rows = half_rows(rows_ref, core if add else 1 - core, half)
    for low in range(0, kv_heads, 2):
        for part, weight_ref in enumerate((key_ref, value_ref)):
            pair = dot(rows, weight_ref[:, low * head : (low + 2) * head])
            for i in range(2):
                here = pair[:, i * head : (i + 1) * head]
                where = slice(part * head, (part + 1) * head)
                if add:
                    here = here + refs[0][low + i, :, where].astype(f32)
                out_ref[low + i, :, where] = here.astype(bf16)


def norm_kernel(parts_ref, gain_ref, kv_ref, raw_ref):
    total = parts_ref[0].astype(f32)
    for i in range(1, parts_ref.shape[0]):
        total = total + parts_ref[i].astype(f32)
    head = gain_ref.shape[1]
    key_raw = total[:, :head]
    keys, _ = head_norm(key_raw, gain_ref[...])
    raw_ref[...] = key_raw
    kv_ref[:, :head] = keys.astype(bf16)
    kv_ref[:, head:] = total[:, head:].astype(bf16)


def attention_kernel(
    core_ref, mine_ref, other_ref, query_ref, up_ref, gain_ref, seen_ref,
    context_ref, query_grad_ref, send_ref, keep_ref,
):
    core = core_ref[0]
    head = gain_ref.shape[1]
    half = mine_ref.shape[0]
    text, width = query_ref.shape
    tiles_half = half // TILE_ROWS
    scale = head ** (-0.5)
    kv = jnp.concatenate([mine_ref[...], other_ref[...]], 0)
    keys, values = kv[:, :head], kv[:, head:]
    keys_t = keys.astype(f32).T.astype(bf16)
    values_t = values.astype(f32).T.astype(bf16)
    gain = gain_ref[...]
    key_grad = jnp.zeros((2 * half, head), f32)
    value_grad = jnp.zeros((2 * half, head), f32)
    for t in range(0, text, TEXT_STEP):
        now = slice(t, t + TEXT_STEP)
        seen = seen_ref[:, now]
        empty = jnp.where(seen == 0, 1.0, 0.0)
        shown = []
        for side in (core, 1 - core):
            for i in range(tiles_half):
                tile = side * tiles_half + i
                shown.append(jnp.broadcast_to(tile < seen, (TILE_ROWS, TEXT_STEP)))
        visible = jnp.concatenate(shown, 0)
        for h in range(width // head):
            cols = slice(h * head, (h + 1) * head)
            query = query_ref[now, cols].astype(f32)
            up = up_ref[now, cols]
            normed_float, inverse = head_norm(query, gain)
            normed = normed_float.astype(bf16)
            scores = dot(keys, normed, BOTH_LAST) * scale
            expo = jnp.where(visible, jnp.exp(scores), 0.0)
            totals = jnp.sum(expo, 0, keepdims=True) + empty
            probs = expo * (1.0 / totals)
            probs_low = probs.astype(bf16)
            prob_grad = dot(values, up, BOTH_LAST)
            row_dot = jnp.sum(probs * prob_grad, 0, keepdims=True)
            score_grad = (probs * (prob_grad - row_dot)).astype(bf16)
            key_grad = key_grad + dot(score_grad, normed)
            value_grad = value_grad + dot(probs_low, up)
            context_ref[now, cols] = dot(values_t, probs_low).T.astype(bf16)
            normed_grad = dot(keys_t, score_grad).T * scale
            query_grad_ref[now, cols] = head_norm_back(
                query, inverse, gain, normed_grad
            ).astype(bf16)
    key_grad = key_grad * scale
    keep_ref[:, :head] = key_grad[:half]
    keep_ref[:, head:] = value_grad[:half]
    send_ref[:, :head] = key_grad[half:].astype(bf16)
    send_ref[:, head:] = value_grad[half:].astype(bf16)


def kv_grad_kernel(keep_ref, received_ref, raw_ref, gain_ref, out_ref):
    total = keep_ref[...] + received_ref[...].astype(f32)
    gain = gain_ref[...]
    head = gain.shape[1]
    key_raw = raw_ref[...]
    _, inverse = head_norm(key_raw, gain)
    key_raw_grad = head_norm_back(key_raw, inverse, gain, total[:, :head]).astype(bf16)
    value_grad = total[:, head:].astype(bf16)
    for i in range(out_ref.shape[0]):
        out_ref[i, :, :head] = key_raw_grad
        out_ref[i, :, head:] = value_grad


def image_product(grads_ref, key_ref, value_ref):
    kv_heads, half, width = grads_ref.shape
    head = width // 2
    total = None
    for h in range(kv_heads):
        cols = slice(h * head, (h + 1) * head)
        weight = jnp.concatenate([key_ref[:, cols], value_ref[:, cols]], 1)
        term = dot(grads_ref[h], weight, BOTH_LAST)
        total = term if total is None else total + term
    return total.astype(bf16)


def image_kernel(grads_ref, key_ref, value_ref, out_ref):
    out_ref[...] = image_product(grads_ref, key_ref, value_ref)


def image_both_kernel(core_ref, grads_ref, key_ref, value_ref, mine_ref, out_ref):
    half = mine_ref.shape[0]
    core = core_ref[0]
    out_ref[pl.ds(pl.multiple_of(core * half, half), half), :] = mine_ref[...]
    out_ref[pl.ds(pl.multiple_of((1 - core) * half, half), half), :] = image_product(
        grads_ref, key_ref, value_ref
    )


def weight_grad_kernel(core_ref, rows_ref, mine_ref, other_ref, key_ref, value_ref):
    kv_heads, half, width = mine_ref.shape
    head = width // 2
    core = core_ref[0]
    rows_mine = half_rows(rows_ref, core, half).astype(f32).T.astype(bf16)
    rows_other = half_rows(rows_ref, 1 - core, half).astype(f32).T.astype(bf16)
    for h in range(kv_heads):
        cols = slice(h * head, (h + 1) * head)
        both = (dot(rows_mine, mine_ref[h]) + dot(rows_other, other_ref[h])).astype(bf16)
        key_ref[:, cols] = both[:, :head]
        value_ref[:, cols] = both[:, head:]


def call(kernel, outs, *args, scalar=False):
    many = len(outs) > 1
    shapes = tuple(jax.ShapeDtypeStruct(shape, kind) for shape, kind in outs)
    return pl.pallas_call(
        kernel,
        out_shape=shapes if many else shapes[0],
        in_specs=[SMEM if scalar and i == 0 else VMEM for i in range(len(args))],
        out_specs=(VMEM,) * len(outs) if many else VMEM,
        compiler_params=PARAMS,
    )(*args)


def fence(*arrays):
    return lax.optimization_barrier(arrays)


def shards(
    image_rows, queries, key_weight, value_weight, query_gain, key_gain, tiles_seen, context_grad
):
    sections = lax.axis_size("section")
    tp = lax.axis_size("tp")
    chips = tp // CORES
    core = (lax.axis_index("tp") % CORES).astype(jnp.int32).reshape(1)
    same_core = [[i for i in range(tp) if i % CORES == c] for c in range(CORES)]
    swap = [(i, i ^ 1) for i in range(tp)]

    def other_core(x):
        return lax.ppermute(x, "tp", swap)

    def over_chips(x):
        return lax.all_to_all(x, "tp", 0, 0, axis_index_groups=same_core)

    own_rows, features = image_rows.shape
    rows_total = sections * own_rows
    half = rows_total // CORES
    kv_width = key_weight.shape[2]
    head = query_gain.shape[1]
    kv_heads = kv_width // head
    text, width = queries.shape[1:]
    pieces = (kv_heads, half, 2 * head)

    blocks = lax.all_to_all(
        jnp.broadcast_to(image_rows[None], (sections, own_rows, features)), "section", 0, 0
    )
    blocks, key_weight, value_weight, queries, context_grad = fence(
        blocks, key_weight[0], value_weight[0], queries[0], context_grad[0]
    )
    rows = blocks.reshape(rows_total, features)
    for_other = call(
        functools.partial(project_kernel, False), [(pieces, bf16)],
        core, rows, key_weight, value_weight, scalar=True,
    )
    received = other_core(for_other)
    partial = call(
        functools.partial(project_kernel, True), [(pieces, bf16)],
        core, rows, key_weight, value_weight, received, scalar=True,
    )
    parts = over_chips(partial)
    kv_mine, key_raw = call(
        norm_kernel, [((half, 2 * head), bf16), ((half, head), f32)], parts, key_gain
    )
    kv_other = other_core(kv_mine)
    context, query_grad, send, keep = call(
        attention_kernel,
        [
            ((text, width), bf16),
            ((text, width), bf16),
            ((half, 2 * head), bf16),
            ((half, 2 * head), f32),
        ],
        core, kv_mine, kv_other, queries, context_grad, query_gain, tiles_seen[None],
        scalar=True,
    )
    received = other_core(send)
    copies = call(kv_grad_kernel, [(pieces, bf16)], keep, received, key_raw, key_gain)
    grads_mine = over_chips(copies)
    grads_other = other_core(grads_mine)
    image_mine = call(
        image_kernel, [((half, features), bf16)], grads_mine, key_weight, value_weight
    )
    image_part = call(
        image_both_kernel, [((rows_total, features), bf16)],
        core, grads_other, key_weight, value_weight, image_mine, scalar=True,
    )
    image_parts = lax.all_to_all(
        image_part.reshape(sections, own_rows, features), "section", 0, 0
    )
    image_parts, rows, grads_mine, grads_other = fence(image_parts, rows, grads_mine, grads_other)
    image_grad = jnp.sum(image_parts.astype(f32), 0)
    key_weight_grad, value_weight_grad = call(
        weight_grad_kernel, [((features, kv_width), bf16)] * 2,
        core, rows, grads_mine, grads_other, scalar=True,
    )
    return (
        context[None], query_grad[None], key_weight_grad[None], value_weight_grad[None], image_grad
    )


def solution(mesh):
    return jax.shard_map(
        shards,
        mesh=mesh,
        in_specs=(
            P("section", "tp"),
            P("section", None, "tp"),
            P("section", "tp", None),
            P("section", "tp", None),
            P("section", None),
            P("section", None),
            P(),
            P("section", None, "tp"),
        ),
        out_specs=(
            P("section", None, "tp"),
            P("section", None, "tp"),
            P("section", "tp", None),
            P("section", "tp", None),
            P("section", "tp"),
        ),
        check_vma=False,
    )
```

time: 112 us -> 102 us (0.911); the launches traced: 111 us -> 102 us
  blocking collectives: 0 us -> 49 us
  waiting for transfers between devices: 47.2 us -> 19.5 us
  matrix products: 14.7 us -> 0 us
  starting transfers between devices: 29.5 us -> 18 us
  Pallas kernels: 0 us -> 11.3 us
  local copies, waits for them, and re-layouts: 11.7 us -> 2.86 us
  other arithmetic: 6.66 us -> 0.68 us
    all_to_all x0 -> x3, blocking collectives: none -> 49 us  [the longest x2 31.3 us: over_chips(): return lax.all_to_all(x, 'tp', 0, 0, axis_index_groups=same_core)]
    all_to_all x3 -> x0, waiting for transfers between devices: 32.3 us -> none  [the longest x2 24.3 us: over_chips(): return lax.all_to_all(x, 'tp', 0, 0, axis_index_groups=same_core)]
    dot_general x14 -> x0, matrix products: 14.7 us -> none  [the longest x2 3.46 us: weight_grad(): lax.dot_general(image_local, column_grads, (((0,), (0,)), ((), ())), pref...]
    all_to_all x3 -> x0, starting transfers between devices: 12.4 us -> none  [the longest x2 8.9 us: over_chips(): return lax.all_to_all(x, 'tp', 0, 0, axis_index_groups=same_core)]
    pallas_call x0 -> x8, Pallas kernels: none -> 11.3 us  [call(): pl.pallas_call(kernel, out_shape=shapes if many else shapes[0], in_specs=...]
    convert_element_type x5 -> x0, other arithmetic: 3.59 us -> none  [the longest x1 2.24 us: shards(): partial = (project(rows_mine) + received.astype(f32)).astype(bf16)]
    ppermute x4, waiting for transfers between devices: 2.32 us -> 4.84 us  [other_core(): return lax.ppermute(x, 'tp', swap)]
    all_to_all x1, waiting for transfers between devices: 12.6 us -> 14.7 us  [shards(): lax.all_to_all(jnp.broadcast_to(image_rows[None], (sections, own_rows, fe...]
  transfers between devices with their start and end apart: 8 -> 5, of which waited for: 6 -> 5; matrix products, arithmetic and copies ran while one was open for 15% -> 0% of each run, Pallas kernels for 0% -> 1%
where the time goes in v2:
time: 102 us
  blocking collectives  49 us (48%)
  waiting for transfers between devices  19.5 us (19%)
  starting transfers between devices  18 us (18%)
  Pallas kernels  11.3 us (11%)
  local copies, waits for them, and re-layouts  2.86 us (3%)
    all_to_all x2, blocking collectives, over_chips(): return lax.all_to_all(x, 'tp', 0, 0, axis_index_groups=same_core)  31.3 us
    all_to_all x1, blocking collectives, shards(): lax.all_to_all(image_part.reshape(sections, own_rows, features), 'section...  17.7 us
    all_to_all x1, waiting for transfers between devices, shards(): lax.all_to_all(jnp.broadcast_to(image_rows[None], (sections, own_rows, fe...  14.7 us
    all_to_all x1, starting transfers between devices, shards(): lax.all_to_all(jnp.broadcast_to(image_rows[None], (sections, own_rows, fe...  11.7 us
    pallas_call x8, Pallas kernels, call(): pl.pallas_call(kernel, out_shape=shapes if many else shapes[0], in_specs=...  11.3 us
    ppermute x4, starting transfers between devices, other_core(): return lax.ppermute(x, 'tp', swap)  6.23 us
    ppermute x4, waiting for transfers between devices, other_core(): return lax.ppermute(x, 'tp', swap)  4.84 us
  transfers between devices with their start and end apart: 5, of which 5 were waited for; matrix products, arithmetic and copies ran while one was open for 0% of the time, Pallas kernels for 1%

profile of v2, /device:TPU:1, one launch (start us, length us, event | category | flops | bytes accessed | tf_op | source)
XLA Modules:
  0.0 102.1 jit_solution(6948443431705523815)
XLA Ops:
  0.6 1.6 %broadcast_in_dim.21 = bf16[16,24,512]{2,1,0:T(8,128)(2,1)} broadcast(bf16[24,512]{1,0:T(8,128)(2,1)} %param.8), dimensions={1,2} | broadcast | bytes 417792 | tf_op jit(solution)/shard_map/broadcast_in_dim | solution.py:223
  2.2 11.7 %all-to-all-start = ((bf16[16,24,512]{2,1,0:T(8,128)(2,1)}), bf16[16,24,512]{2,1,0:T(8,128)(2,1)S(1)}, u32[]{:S(2)}, u32[]{:S(2)}) async-start(bf16[16,24,512]{2,1,0:T(8,128)(2,1)} %broadcast_in_dim.21), calls=%async_computation | async-start | bytes 786432 | tf_op jit(solution)/shard_map/all_to_all | solution.py:222
  14.0 14.7 %all-to-all-done = bf16[16,24,512]{2,1,0:T(8,128)(2,1)S(1)} async-done(((bf16[16,24,512]{2,1,0:T(8,128)(2,1)}), bf16[16,24,512]{2,1,0:T(8,128)(2,1)S(1)}, u32[]{:S(2)}, u32[]{:S(2)}) %all-to-all-start) | async-done | bytes 393248 | tf_op jit(solution)/shard_map/all_to_all | solution.py:222
  28.7 1.2 %copy-done.1 = bf16[1,512,1024]{2,1,0:T(8,128)(2,1)S(1)} copy-done((bf16[1,512,1024]{2,1,0:T(8,128)(2,1)S(1)}, bf16[1,512,1024]{2,1,0:T(8,128)(2,1)}, u32[]{:S(2)}) %copy-start.1) | copy-done | bytes 1048600
  29.9 0.6 shard_map.119
  30.5 2.4 %collective-permute-start = (bf16[8,192,256]{2,1,0:T(8,128)(2,1)S(1)}, bf16[8,192,256]{2,1,0:T(8,128)(2,1)S(1)}, u32[]{:S(2)}, u32[]{:S(2)}) collective-permute-start(bf16[8,192,256]{2,1,0:T(8,128)(2,1)S(1)} %shard_map.119), channel_id=1, source_target_pairs={{0,1},{1,0},{2,3},{3,2},{4,5},{5,4},{6,7},{7,6},{8,9},{9,8},{10,11... | collective-permute-start | bytes 2359304 | tf_op jit(solution)/shard_map/ppermute | solution.py:208
  32.9 1.9 %collective-permute-done.refs_0_ = bf16[8,192,256]{2,1,0:T(8,128)(2,1)S(1)} collective-permute-done((bf16[8,192,256]{2,1,0:T(8,128)(2,1)S(1)}, bf16[8,192,256]{2,1,0:T(8,128)(2,1)S(1)}, u32[]{:S(2)}, u32[]{:S(2)}) %collective-permute-start) | collective-permute-done | bytes 786464 | tf_op jit(solution)/shard_map/ppermute | solution.py:208
  34.8 0.6 shard_map.120
  35.4 16.5 %all_to_all.20.parts_ref = bf16[8,192,256]{2,1,0:T(8,128)(2,1)S(1)} all-to-all(bf16[8,192,256]{2,1,0:T(8,128)(2,1)S(1)} %shard_map.120), channel_id=1, replica_groups={{0,2,4,6,8,10,12,14},{1,3,5,7,9,11,13,15},{16,18,20,22,24,26,28,30},{17..., dimensions={0} | all-to-all | bytes 1572864 | tf_op jit(solution)/shard_map/all_to_all | solution.py:211
  51.9 0.2 shard_map.121
  52.1 1.9 %collective-permute-start.1 = (bf16[192,256]{1,0:T(8,128)(2,1)S(1)}, bf16[192,256]{1,0:T(8,128)(2,1)S(1)}, u32[]{:S(2)}, u32[]{:S(2)}) collective-permute-start(bf16[192,256]{1,0:T(8,128)(2,1)S(1)} %get-tuple-element.25.mine_ref), channel_id=1, source_target_pairs={{0,1},{1,0},{2,3},{3,2},{4,5},{5,4},{6,7},{7,6},{8,9},{9,8},{10,11... | collective-permute-start | bytes 294920 | tf_op jit(solution)/shard_map/ppermute | solution.py:208
  54.1 0.9 collective-permute-done.1.other_ref
  55.0 5.4 %shard_map.122 = (bf16[512,512]{1,0:T(8,128)(2,1)}, bf16[512,512]{1,0:T(8,128)(2,1)}, bf16[192,256]{1,0:T(8,128)(2,1)S(1)}, f32[192,256]{1,0:T(8,128)S(1)}) custom-call(s32[1]{0:T(128)} %bitcast.core_ref, bf16[192,256]{1,0:T(8,128)(2,1)S(1)} %get-tuple-element.25.mine_ref, bf16[192,256]{1,0:T(8,128)(2,1)S(1)} %collective-permute-done.1.other_ref, ...), custom_call_target="tpu_custom_call" | custom-call | tf_op jit(solution)/shard_map/pallas_call | solution.py:184
  60.4 0.4 collective-permute-start.2
  60.8 0.9 collective-permute-done.2.received_ref
  61.7 0.2 shard_map.123
  61.9 14.8 %all_to_all.21.grads_ref.mine_ref = bf16[8,192,256]{2,1,0:T(8,128)(2,1)S(1)} all-to-all(bf16[8,192,256]{2,1,0:T(8,128)(2,1)S(1)} %shard_map.123), channel_id=1, replica_groups={{0,2,4,6,8,10,12,14},{1,3,5,7,9,11,13,15},{16,18,20,22,24,26,28,30},{17..., dimensions={0} | all-to-all | bytes 1572864 | tf_op jit(solution)/shard_map/all_to_all | solution.py:211
  76.7 1.6 %collective-permute-start.3 = (bf16[8,192,256]{2,1,0:T(8,128)(2,1)S(1)}, bf16[8,192,256]{2,1,0:T(8,128)(2,1)S(1)}, u32[]{:S(2)}, u32[]{:S(2)}) collective-permute-start(bf16[8,192,256]{2,1,0:T(8,128)(2,1)S(1)} %all_to_all.21.grads_ref.mine_ref), channel_id=1, source_target_pairs={{0,1},{1,0},{2,3},{3,2},{4,5},{5,4},{6,7},{7,6},{8,9},{9,8},{10,11... | collective-permute-start | bytes 2359304 | tf_op jit(solution)/shard_map/ppermute | solution.py:208
  78.3 0.9 shard_map.124.mine_ref
  79.2 1.0 %collective-permute-done.3.grads_ref.other_ref = bf16[8,192,256]{2,1,0:T(8,128)(2,1)S(1)} collective-permute-done((bf16[8,192,256]{2,1,0:T(8,128)(2,1)S(1)}, bf16[8,192,256]{2,1,0:T(8,128)(2,1)S(1)}, u32[]{:S(2)}, u32[]{:S(2)}) %collective-permute-start.3) | collective-permute-done | bytes 786464 | tf_op jit(solution)/shard_map/ppermute | solution.py:208
  80.2 0.9 shard_map.125
  81.1 17.7 %all_to_all.22 = bf16[16,24,512]{2,1,0:T(8,128)(2,1)S(1)} all-to-all(bf16[16,24,512]{2,1,0:T(8,128)(2,1)S(1)} %bitcast.23), channel_id=1, replica_groups=mesh['section'=16,'tp'=16] {'section'}, dimensions={0} | all-to-all | bytes 786432 | tf_op jit(solution)/shard_map/all_to_all | solution.py:265
  98.8 0.7 convert_reduce_fusion
  99.5 2.6 %shard_map.126 = (bf16[512,1024]{1,0:T(8,128)(2,1)}, bf16[512,1024]{1,0:T(8,128)(2,1)}) custom-call(s32[1]{0:T(128)} %bitcast.core_ref, bf16[384,512]{1,0:T(8,128)(2,1)S(1)} %bitcast.22, bf16[8,192,256]{2,1,0:T(8,128)(2,1)S(1)} %all_to_all.21.grads_ref.mine_ref, bf16[8,192,256]{2,1,0:T(8,128)(2,1)S(1)} %collective-permute-done.3.grads_ref.other_ref), custom_call_target="tpu_custom_call" | custom-call | tf_op jit(solution)/shard_map/pallas_call | solution.py:184
  (15 shorter events, 0.0 us)
Async XLA Ops:
  0.6 28.0 %copy-start = (bf16[1,512,1024]{2,1,0:T(8,128)(2,1)S(1)}, bf16[1,512,1024]{2,1,0:T(8,128)(2,1)}, u32[]{:S(2)}) copy-start(bf16[1,512,1024]{2,1,0:T(8,128)(2,1)} %param.10) | copy-start | bytes 3145732
  2.2 26.4 %all-to-all-start = ((bf16[16,24,512]{2,1,0:T(8,128)(2,1)}), bf16[16,24,512]{2,1,0:T(8,128)(2,1)S(1)}, u32[]{:S(2)}, u32[]{:S(2)}) async-start(bf16[16,24,512]{2,1,0:T(8,128)(2,1)} %broadcast_in_dim.21), calls=%async_computation | async-start | bytes 786432 | tf_op jit(solution)/shard_map/all_to_all | solution.py:222
  28.7 1.2 %copy-start.1 = (bf16[1,512,1024]{2,1,0:T(8,128)(2,1)S(1)}, bf16[1,512,1024]{2,1,0:T(8,128)(2,1)}, u32[]{:S(2)}) copy-start(bf16[1,512,1024]{2,1,0:T(8,128)(2,1)} %param.11) | copy-start | bytes 3145732
  30.5 4.3 %collective-permute-start = (bf16[8,192,256]{2,1,0:T(8,128)(2,1)S(1)}, bf16[8,192,256]{2,1,0:T(8,128)(2,1)S(1)}, u32[]{:S(2)}, u32[]{:S(2)}) collective-permute-start(bf16[8,192,256]{2,1,0:T(8,128)(2,1)S(1)} %shard_map.119), channel_id=1, source_target_pairs={{0,1},{1,0},{2,3},{3,2},{4,5},{5,4},{6,7},{7,6},{8,9},{9,8},{10,11... | collective-permute-start | bytes 2359304 | tf_op jit(solution)/shard_map/ppermute | solution.py:208
  35.4 16.5 %copy-start.6 = (f32[1,128]{1,0:T(1,128)S(1)}, f32[1,128]{1,0:T(1,128)}, u32[]{:S(2)}) copy-start(f32[1,128]{1,0:T(1,128)} %gain_ref.5) | copy-start | bytes 1540
  35.4 19.6 %copy-start.4 = (bf16[1,512,512]{2,1,0:T(8,128)(2,1)S(1)}, bf16[1,512,512]{2,1,0:T(8,128)(2,1)}, u32[]{:S(2)}) copy-start(bf16[1,512,512]{2,1,0:T(8,128)(2,1)} %param.15) | copy-start | bytes 1572868
  51.9 3.1 %copy-start.3 = (bf16[1,512,512]{2,1,0:T(8,128)(2,1)S(1)}, bf16[1,512,512]{2,1,0:T(8,128)(2,1)}, u32[]{:S(2)}) copy-start(bf16[1,512,512]{2,1,0:T(8,128)(2,1)} %param.9) | copy-start | bytes 1572868
  52.1 2.9 %copy-start.5 = (s32[512]{0:T(512)S(1)}, s32[512]{0:T(512)}, u32[]{:S(2)}) copy-start(s32[512]{0:T(512)} %param.14) | copy-start | bytes 6148
  52.1 2.9 %copy-start.7 = (f32[1,128]{1,0:T(1,128)S(1)}, f32[1,128]{1,0:T(1,128)}, u32[]{:S(2)}) copy-start(f32[1,128]{1,0:T(1,128)} %gain_ref.4) | copy-start | bytes 1540
  52.1 2.9 %collective-permute-start.1 = (bf16[192,256]{1,0:T(8,128)(2,1)S(1)}, bf16[192,256]{1,0:T(8,128)(2,1)S(1)}, u32[]{:S(2)}, u32[]{:S(2)}) collective-permute-start(bf16[192,256]{1,0:T(8,128)(2,1)S(1)} %get-tuple-element.25.mine_ref), channel_id=1, source_target_pairs={{0,1},{1,0},{2,3},{3,2},{4,5},{5,4},{6,7},{7,6},{8,9},{9,8},{10,11... | collective-permute-start | bytes 294920 | tf_op jit(solution)/shard_map/ppermute | solution.py:208
  60.4 1.3 %collective-permute-start.2 = (bf16[192,256]{1,0:T(8,128)(2,1)S(1)}, bf16[192,256]{1,0:T(8,128)(2,1)S(1)}, u32[]{:S(2)}, u32[]{:S(2)}) collective-permute-start(bf16[192,256]{1,0:T(8,128)(2,1)S(1)} %get-tuple-element.31), channel_id=1, source_target_pairs={{0,1},{1,0},{2,3},{3,2},{4,5},{5,4},{6,7},{7,6},{8,9},{9,8},{10,11... | collective-permute-start | bytes 294920 | tf_op jit(solution)/shard_map/ppermute | solution.py:208
  61.9 16.4 %copy-start.2 = (bf16[1,512,1024]{2,1,0:T(8,128)(2,1)S(1)}, bf16[1,512,1024]{2,1,0:T(8,128)(2,1)}, u32[]{:S(2)}) copy-start(bf16[1,512,1024]{2,1,0:T(8,128)(2,1)} %param.11) | copy-start | bytes 3145732
  76.7 3.5 %collective-permute-start.3 = (bf16[8,192,256]{2,1,0:T(8,128)(2,1)S(1)}, bf16[8,192,256]{2,1,0:T(8,128)(2,1)S(1)}, u32[]{:S(2)}, u32[]{:S(2)}) collective-permute-start(bf16[8,192,256]{2,1,0:T(8,128)(2,1)S(1)} %all_to_all.21.grads_ref.mine_ref), channel_id=1, source_target_pairs={{0,1},{1,0},{2,3},{3,2},{4,5},{5,4},{6,7},{7,6},{8,9},{9,8},{10,11... | collective-permute-start | bytes 2359304 | tf_op jit(solution)/shard_map/ppermute | solution.py:208

commit v3 on v2

--- a/solution.py
+++ b/solution.py
@@ -9,7 +9,8 @@
 
 TILE_ROWS = 96
 CORES = 2
-TEXT_STEP = 256
+IMAGE_STEPS = 2
+LOG2_E = 1.4426950408889634
 epsilon = 1e-05
 
 f32 = jnp.float32
@@ -18,6 +19,7 @@
 BOTH_LAST = (((1,), (1,)), ((), ()))
 BOTH_FIRST = (((0,), (0,)), ((), ()))
 
+ANY = pl.BlockSpec(memory_space=pl.ANY)
 VMEM = pl.BlockSpec(memory_space=pltpu.VMEM)
 SMEM = pl.BlockSpec(memory_space=pltpu.SMEM)
 PARAMS = pltpu.CompilerParams(vmem_limit_bytes=40 * 1024 * 1024)
@@ -41,6 +43,11 @@
 
 def half_rows(ref, which, half):
     return ref[pl.ds(pl.multiple_of(which * half, half), half), :]
+
+
+def copies_kernel(rows_ref, out_ref):
+    for i in range(out_ref.shape[0]):
+        out_ref[i] = rows_ref[...]
 
 
 def project_kernel(add, core_ref, rows_ref, key_ref, value_ref, *refs):
@@ -75,6 +82,7 @@
 def attention_kernel(
     core_ref, mine_ref, other_ref, query_ref, up_ref, gain_ref, seen_ref,
     context_ref, query_grad_ref, send_ref, keep_ref,
+    context_held, query_grad_held, sems,
 ):
     core = core_ref[0]
     head = gain_ref.shape[1]
@@ -87,44 +95,48 @@
     keys_t = keys.astype(f32).T.astype(bf16)
     values_t = values.astype(f32).T.astype(bf16)
     gain = gain_ref[...]
+    seen = seen_ref[...]
+    empty = jnp.where(seen == 0, 1.0, 0.0)
+    shown = []
+    for side in (core, 1 - core):
+        for i in range(tiles_half):
+            shown.append(jnp.broadcast_to(side * tiles_half + i < seen, (TILE_ROWS, text)))
+    visible = jnp.concatenate(shown, 0)
     key_grad = jnp.zeros((2 * half, head), f32)
     value_grad = jnp.zeros((2 * half, head), f32)
-    for t in range(0, text, TEXT_STEP):
-        now = slice(t, t + TEXT_STEP)
-        seen = seen_ref[:, now]
-        empty = jnp.where(seen == 0, 1.0, 0.0)
-        shown = []
-        for side in (core, 1 - core):
-            for i in range(tiles_half):
-                tile = side * tiles_half + i
-                shown.append(jnp.broadcast_to(tile < seen, (TILE_ROWS, TEXT_STEP)))
-        visible = jnp.concatenate(shown, 0)
-        for h in range(width // head):
-            cols = slice(h * head, (h + 1) * head)
-            query = query_ref[now, cols].astype(f32)
-            up = up_ref[now, cols]
-            normed_float, inverse = head_norm(query, gain)
-            normed = normed_float.astype(bf16)
-            scores = dot(keys, normed, BOTH_LAST) * scale
-            expo = jnp.where(visible, jnp.exp(scores), 0.0)
-            totals = jnp.sum(expo, 0, keepdims=True) + empty
-            probs = expo * (1.0 / totals)
-            probs_low = probs.astype(bf16)
-            prob_grad = dot(values, up, BOTH_LAST)
-            row_dot = jnp.sum(probs * prob_grad, 0, keepdims=True)
-            score_grad = (probs * (prob_grad - row_dot)).astype(bf16)
-            key_grad = key_grad + dot(score_grad, normed)
-            value_grad = value_grad + dot(probs_low, up)
-            context_ref[now, cols] = dot(values_t, probs_low).T.astype(bf16)
-            normed_grad = dot(keys_t, score_grad).T * scale
-            query_grad_ref[now, cols] = head_norm_back(
-                query, inverse, gain, normed_grad
-            ).astype(bf16)
+    copies = []
+    for h in range(width // head):
+        cols = slice(h * head, (h + 1) * head)
+        query = query_ref[:, cols].astype(f32)
+        up = up_ref[:, cols]
+        normed_float, inverse = head_norm(query, gain)
+        normed = normed_float.astype(bf16)
+        scores = dot(keys, normed, BOTH_LAST)
+        expo = jnp.where(visible, jnp.exp2(scores * (scale * LOG2_E)), 0.0)
+        totals = jnp.sum(expo, 0, keepdims=True) + empty
+        probs = expo * (1.0 / totals)
+        probs_low = probs.astype(bf16)
+        prob_grad = dot(values, up, BOTH_LAST)
+        row_dot = jnp.sum(probs * prob_grad, 0, keepdims=True)
+        score_grad = (probs * (prob_grad - row_dot)).astype(bf16)
+        key_grad = key_grad + dot(score_grad, normed)
+        value_grad = value_grad + dot(probs_low, up)
+        context_held[:, cols] = dot(values_t, probs_low).T.astype(bf16)
+        normed_grad = dot(keys_t, score_grad).T * scale
+        query_grad_held[:, cols] = head_norm_back(query, inverse, gain, normed_grad).astype(bf16)
+        for i, (held, out) in enumerate(
+            ((context_held, context_ref), (query_grad_held, query_grad_ref))
+        ):
+            copy = pltpu.make_async_copy(held.at[:, cols], out.at[:, cols], sems.at[2 * h + i])
+            copy.start()
+            copies.append(copy)
     key_grad = key_grad * scale
     keep_ref[:, :head] = key_grad[:half]
     keep_ref[:, head:] = value_grad[:half]
     send_ref[:, :head] = key_grad[half:].astype(bf16)
     send_ref[:, head:] = value_grad[half:].astype(bf16)
+    for copy in copies:
+        copy.wait()
 
 
 def kv_grad_kernel(keep_ref, received_ref, raw_ref, gain_ref, out_ref):
@@ -140,29 +152,39 @@
         out_ref[i, :, head:] = value_grad
 
 
-def image_product(grads_ref, key_ref, value_ref):
+def image_product(grads_ref, key_ref, value_ref, now):
     kv_heads, half, width = grads_ref.shape
     head = width // 2
     total = None
     for h in range(kv_heads):
         cols = slice(h * head, (h + 1) * head)
-        weight = jnp.concatenate([key_ref[:, cols], value_ref[:, cols]], 1)
+        weight = jnp.concatenate([key_ref[now, cols], value_ref[now, cols]], 1)
         term = dot(grads_ref[h], weight, BOTH_LAST)
         total = term if total is None else total + term
     return total.astype(bf16)
 
 
 def image_kernel(grads_ref, key_ref, value_ref, out_ref):
-    out_ref[...] = image_product(grads_ref, key_ref, value_ref)
-
-
-def image_both_kernel(core_ref, grads_ref, key_ref, value_ref, mine_ref, out_ref):
-    half = mine_ref.shape[0]
+    out_ref[...] = image_product(grads_ref, key_ref, value_ref, slice(None))
+
+
+def image_both_kernel(core_ref, grads_ref, key_ref, value_ref, mine_ref, out_ref, held, sems):
+    half, features = mine_ref.shape
     core = core_ref[0]
-    out_ref[pl.ds(pl.multiple_of(core * half, half), half), :] = mine_ref[...]
-    out_ref[pl.ds(pl.multiple_of((1 - core) * half, half), half), :] = image_product(
-        grads_ref, key_ref, value_ref
-    )
+    here = pl.ds(pl.multiple_of(core * half, half), half)
+    there = pl.ds(pl.multiple_of((1 - core) * half, half), half)
+    copies = [pltpu.make_async_copy(mine_ref, out_ref.at[here, :], sems.at[0])]
+    copies[0].start()
+    step = features // IMAGE_STEPS
+    for i in range(IMAGE_STEPS):
+        now = slice(i * step, (i + 1) * step)
+        held[:, now] = image_product(grads_ref, key_ref, value_ref, now)
+        copies.append(
+            pltpu.make_async_copy(held.at[:, now], out_ref.at[there, now], sems.at[i + 1])
+        )
+        copies[-1].start()
+    for copy in copies:
+        copy.wait()
 
 
 def weight_grad_kernel(core_ref, rows_ref, mine_ref, other_ref, key_ref, value_ref):
@@ -178,15 +200,18 @@
         value_ref[:, cols] = both[:, head:]
 
 
-def call(kernel, outs, *args, scalar=False):
+def call(kernel, outs, *args, scalar=False, cost=None, scratch=(), to_hbm=()):
     many = len(outs) > 1
     shapes = tuple(jax.ShapeDtypeStruct(shape, kind) for shape, kind in outs)
+    places = tuple(ANY if i in to_hbm else VMEM for i in range(len(outs)))
     return pl.pallas_call(
         kernel,
         out_shape=shapes if many else shapes[0],
         in_specs=[SMEM if scalar and i == 0 else VMEM for i in range(len(args))],
-        out_specs=(VMEM,) * len(outs) if many else VMEM,
+        out_specs=places if many else places[0],
+        scratch_shapes=list(scratch),
         compiler_params=PARAMS,
+        cost_estimate=cost,
     )(*args)
 
 
@@ -219,9 +244,12 @@
     text, width = queries.shape[1:]
     pieces = (kv_heads, half, 2 * head)
 
-    blocks = lax.all_to_all(
-        jnp.broadcast_to(image_rows[None], (sections, own_rows, features)), "section", 0, 0
-    )
+    image_rows, core = fence(image_rows, core)
+    copies = call(
+        copies_kernel, [((sections, own_rows, features), bf16)], image_rows,
+        cost=pl.CostEstimate(flops=2**34, bytes_accessed=2**25, transcendentals=0),
+    )
+    blocks = lax.all_to_all(copies, "section", 0, 0)
     blocks, key_weight, value_weight, queries, context_grad = fence(
         blocks, key_weight[0], value_weight[0], queries[0], context_grad[0]
     )
@@ -249,7 +277,9 @@
             ((half, 2 * head), f32),
         ],
         core, kv_mine, kv_other, queries, context_grad, query_gain, tiles_seen[None],
-        scalar=True,
+        scalar=True, to_hbm=(0, 1),
+        scratch=[pltpu.VMEM((text, width), bf16)] * 2
+        + [pltpu.SemaphoreType.DMA((2 * width // head,))],
     )
     received = other_core(send)
     copies = call(kv_grad_kernel, [(pieces, bf16)], keep, received, key_raw, key_gain)
@@ -260,17 +290,26 @@
     )
     image_part = call(
         image_both_kernel, [((rows_total, features), bf16)],
-        core, grads_other, key_weight, value_weight, image_mine, scalar=True,
-    )
+        core, grads_other, key_weight, value_weight, image_mine, scalar=True, to_hbm=(0,),
+        scratch=[pltpu.VMEM((half, features), bf16), pltpu.SemaphoreType.DMA((IMAGE_STEPS + 1,))],
+    )
+    image_part, rows, grads_mine, grads_other = fence(image_part, rows, grads_mine, grads_other)
     image_parts = lax.all_to_all(
         image_part.reshape(sections, own_rows, features), "section", 0, 0
     )
-    image_parts, rows, grads_mine, grads_other = fence(image_parts, rows, grads_mine, grads_other)
-    image_grad = jnp.sum(image_parts.astype(f32), 0)
     key_weight_grad, value_weight_grad = call(
         weight_grad_kernel, [((features, kv_width), bf16)] * 2,
         core, rows, grads_mine, grads_other, scalar=True,
-    )
+        cost=pl.CostEstimate(
+            flops=2 * features * 2 * kv_width * rows_total,
+            bytes_accessed=4 * features * 2 * kv_width,
+            transcendentals=0,
+        ),
+    )
+    image_parts, key_weight_grad, value_weight_grad = fence(
+        image_parts, key_weight_grad, value_weight_grad
+    )
+    image_grad = jnp.sum(image_parts.astype(f32), 0)
     return (
         context[None], query_grad[None], key_weight_grad[None], value_weight_grad[None], image_grad
     )

time: 102 us -> 98.6 us (0.967)
  blocking collectives: 49 us -> 57.5 us
  starting transfers between devices: 18 us -> 9.88 us
  waiting for transfers between devices: 19.5 us -> 17.4 us
  local copies, waits for them, and re-layouts: 2.86 us -> 0.76 us
    all_to_all x1, blocking collectives: 17.7 us -> 26.3 us  [shards(): blocks = lax.all_to_all(copies, 'section', 0, 0)]
    all_to_all x1, starting transfers between devices: 11.7 us -> 3.56 us  [shards(): lax.all_to_all(image_part.reshape(sections, own_rows, features), 'section...]
    all_to_all x1, waiting for transfers between devices: 14.7 us -> 12.6 us  [shards(): lax.all_to_all(image_part.reshape(sections, own_rows, features), 'section...]
    broadcast_in_dim x1 -> x0, local copies, waits for them, and re-layouts: 1.6 us -> none  [shards(): jnp.broadcast_to(image_rows[None], (sections, own_rows, features))]
    pallas_call x8 -> x9, Pallas kernels: 11.3 us -> 11.3 us  [call(): pl.pallas_call(kernel, out_shape=shapes if many else shapes[0], in_specs=...]
  transfers between devices with their start and end apart: 5 -> 5, of which waited for: 5 -> 5; matrix products, arithmetic and copies ran while one was open for 0% -> 0% of each run, Pallas kernels for 1% -> 4%
where the time goes in v3:
time: 98.6 us; the launch traced here: 98.2 us
  blocking collectives  57.5 us (58%)
  waiting for transfers between devices  17.4 us (18%)
  Pallas kernels  11.3 us (11%)
  starting transfers between devices  9.88 us (10%)
    all_to_all x2, blocking collectives, over_chips(): return lax.all_to_all(x, 'tp', 0, 0, axis_index_groups=same_core)  31.1 us
    all_to_all x1, blocking collectives, shards(): blocks = lax.all_to_all(copies, 'section', 0, 0)  26.3 us
    all_to_all x1, waiting for transfers between devices, shards(): lax.all_to_all(image_part.reshape(sections, own_rows, features), 'section...  12.6 us
    pallas_call x9, Pallas kernels, call(): pl.pallas_call(kernel, out_shape=shapes if many else shapes[0], in_specs=...  11.3 us
    ppermute x4, starting transfers between devices, other_core(): return lax.ppermute(x, 'tp', swap)  6.31 us
    ppermute x4, waiting for transfers between devices, other_core(): return lax.ppermute(x, 'tp', swap)  4.85 us
    all_to_all x1, starting transfers between devices, shards(): lax.all_to_all(image_part.reshape(sections, own_rows, features), 'section...  3.56 us
  transfers between devices with their start and end apart: 5, of which 5 were waited for; matrix products, arithmetic and copies ran while one was open for 0% of the time, Pallas kernels for 4%

profile of v3, /device:TPU:1, one launch (start us, length us, event | category | flops | bytes accessed | tf_op | source)
XLA Modules:
  0.0 98.2 jit_solution(2429373383904162818)
XLA Ops:
  0.7 0.7 copy-done.7
  1.4 26.3 %all_to_all.20 = bf16[16,24,512]{2,1,0:T(8,128)(2,1)S(1)} all-to-all(bf16[16,24,512]{2,1,0:T(8,128)(2,1)S(1)} %shard_map.119), channel_id=1, replica_groups=mesh['section'=16,'tp'=16] {'section'}, dimensions={0} | all-to-all | bytes 786432 | tf_op jit(solution)/shard_map/all_to_all | solution.py:252
  27.8 0.6 shard_map.120
  28.4 2.3 %collective-permute-start = (bf16[8,192,256]{2,1,0:T(8,128)(2,1)S(1)}, bf16[8,192,256]{2,1,0:T(8,128)(2,1)S(1)}, u32[]{:S(2)}, u32[]{:S(2)}) collective-permute-start(bf16[8,192,256]{2,1,0:T(8,128)(2,1)S(1)} %shard_map.120), channel_id=1, source_target_pairs={{0,1},{1,0},{2,3},{3,2},{4,5},{5,4},{6,7},{7,6},{8,9},{9,8},{10,11... | collective-permute-start | bytes 2359304 | tf_op jit(solution)/shard_map/ppermute | solution.py:233
  30.7 1.9 %collective-permute-done.refs_0_ = bf16[8,192,256]{2,1,0:T(8,128)(2,1)S(1)} collective-permute-done((bf16[8,192,256]{2,1,0:T(8,128)(2,1)S(1)}, bf16[8,192,256]{2,1,0:T(8,128)(2,1)S(1)}, u32[]{:S(2)}, u32[]{:S(2)}) %collective-permute-start) | collective-permute-done | bytes 786464 | tf_op jit(solution)/shard_map/ppermute | solution.py:233
  32.7 0.6 shard_map.121
  33.3 0.0 copy-start.5
  33.3 16.5 %all_to_all.21.parts_ref = bf16[8,192,256]{2,1,0:T(8,128)(2,1)S(1)} all-to-all(bf16[8,192,256]{2,1,0:T(8,128)(2,1)S(1)} %shard_map.121), channel_id=1, replica_groups={{0,2,4,6,8,10,12,14},{1,3,5,7,9,11,13,15},{16,18,20,22,24,26,28,30},{17..., dimensions={0} | all-to-all | bytes 1572864 | tf_op jit(solution)/shard_map/all_to_all | solution.py:236
  49.8 0.2 shard_map.122
  50.0 1.9 %collective-permute-start.1 = (bf16[192,256]{1,0:T(8,128)(2,1)S(1)}, bf16[192,256]{1,0:T(8,128)(2,1)S(1)}, u32[]{:S(2)}, u32[]{:S(2)}) collective-permute-start(bf16[192,256]{1,0:T(8,128)(2,1)S(1)} %get-tuple-element.32.mine_ref), channel_id=1, source_target_pairs={{0,1},{1,0},{2,3},{3,2},{4,5},{5,4},{6,7},{7,6},{8,9},{9,8},{10,11... | collective-permute-start | bytes 294920 | tf_op jit(solution)/shard_map/ppermute | solution.py:233
  51.9 0.9 collective-permute-done.1.other_ref
  52.9 4.6 %shard_map.123 = (bf16[512,512]{1,0:T(8,128)(2,1)}, bf16[512,512]{1,0:T(8,128)(2,1)}, bf16[192,256]{1,0:T(8,128)(2,1)S(1)}, f32[192,256]{1,0:T(8,128)S(1)}) custom-call(s32[1]{0:T(128)} %bitcast.core_ref, bf16[192,256]{1,0:T(8,128)(2,1)S(1)} %get-tuple-element.32.mine_ref, bf16[192,256]{1,0:T(8,128)(2,1)S(1)} %collective-permute-done.1.other_ref, ...), custom_call_target="tpu_custom_call" | custom-call | tf_op jit(solution)/shard_map/pallas_call | solution.py:207
  57.5 0.4 collective-permute-start.2
  57.9 0.9 collective-permute-done.2.received_ref
  58.9 0.2 shard_map.124
  59.1 14.6 %all_to_all.22.grads_ref.mine_ref = bf16[8,192,256]{2,1,0:T(8,128)(2,1)S(1)} all-to-all(bf16[8,192,256]{2,1,0:T(8,128)(2,1)S(1)} %shard_map.124), channel_id=1, replica_groups={{0,2,4,6,8,10,12,14},{1,3,5,7,9,11,13,15},{16,18,20,22,24,26,28,30},{17..., dimensions={0} | all-to-all | bytes 1572864 | tf_op jit(solution)/shard_map/all_to_all | solution.py:236
  73.7 1.6 %collective-permute-start.3 = (bf16[8,192,256]{2,1,0:T(8,128)(2,1)S(1)}, bf16[8,192,256]{2,1,0:T(8,128)(2,1)S(1)}, u32[]{:S(2)}, u32[]{:S(2)}) collective-permute-start(bf16[8,192,256]{2,1,0:T(8,128)(2,1)S(1)} %all_to_all.22.grads_ref.mine_ref), channel_id=1, source_target_pairs={{0,1},{1,0},{2,3},{3,2},{4,5},{5,4},{6,7},{7,6},{8,9},{9,8},{10,11... | collective-permute-start | bytes 2359304 | tf_op jit(solution)/shard_map/ppermute | solution.py:233
  75.3 0.9 shard_map.125.mine_ref
  76.2 1.1 %collective-permute-done.3.grads_ref.other_ref = bf16[8,192,256]{2,1,0:T(8,128)(2,1)S(1)} collective-permute-done((bf16[8,192,256]{2,1,0:T(8,128)(2,1)S(1)}, bf16[8,192,256]{2,1,0:T(8,128)(2,1)S(1)}, u32[]{:S(2)}, u32[]{:S(2)}) %collective-permute-start.3) | collective-permute-done | bytes 786464 | tf_op jit(solution)/shard_map/ppermute | solution.py:233
  77.2 1.6 %shard_map.126 = bf16[384,512]{1,0:T(8,128)(2,1)} custom-call(s32[1]{0:T(128)} %bitcast.core_ref, bf16[8,192,256]{2,1,0:T(8,128)(2,1)S(1)} %collective-permute-done.3.grads_ref.other_ref, bf16[512,1024]{1,0:T(8,128)(2,1)S(1)} %bitcast.15, bf16[512,1024]{1,0:T(8,128)(2,1)S(1)} %bitcast.19, bf16[192,512]{1,0:T(8,128)(2,1)S(1)} %shard_map.125.mine_ref), custom_call_target="tpu_custom_call" | custom-call | tf_op jit(solution)/shard_map/pallas_call | solution.py:207
  78.8 3.6 %all-to-all-start.3 = ((bf16[16,24,512]{2,1,0:T(8,128)(2,1)}), bf16[16,24,512]{2,1,0:T(8,128)(2,1)S(1)}, u32[]{:S(2)}, u32[]{:S(2)}) async-start(bf16[16,24,512]{2,1,0:T(8,128)(2,1)} %bitcast.9), calls=%async_computation.3 | async-start | bytes 786432 | tf_op jit(solution)/shard_map/all_to_all | solution.py:297
  82.4 2.6 %shard_map.127 = (bf16[512,1024]{1,0:T(8,128)(2,1)}, bf16[512,1024]{1,0:T(8,128)(2,1)}) custom-call(s32[1]{0:T(128)} %bitcast.core_ref, bf16[384,512]{1,0:T(8,128)(2,1)S(1)} %bitcast.22, bf16[8,192,256]{2,1,0:T(8,128)(2,1)S(1)} %all_to_all.22.grads_ref.mine_ref, bf16[8,192,256]{2,1,0:T(8,128)(2,1)S(1)} %collective-permute-done.3.grads_ref.other_ref), custom_call_target="tpu_custom_call" | custom-call | flops 805306368 | bytes 4194304 | tf_op jit(solution)/shard_map/pallas_call | solution.py:207
  85.0 12.6 %all-to-all-done.3 = bf16[16,24,512]{2,1,0:T(8,128)(2,1)S(1)} async-done(((bf16[16,24,512]{2,1,0:T(8,128)(2,1)}), bf16[16,24,512]{2,1,0:T(8,128)(2,1)S(1)}, u32[]{:S(2)}, u32[]{:S(2)}) %all-to-all-start.3) | async-done | bytes 393248 | tf_op jit(solution)/shard_map/all_to_all | solution.py:297
  97.6 0.7 convert_reduce_fusion
  (15 shorter events, 0.1 us)
Async XLA Ops:
  0.6 0.7 copy-start.7
  1.4 26.4 %copy-start = (bf16[1,512,1024]{2,1,0:T(8,128)(2,1)S(1)}, bf16[1,512,1024]{2,1,0:T(8,128)(2,1)}, u32[]{:S(2)}) copy-start(bf16[1,512,1024]{2,1,0:T(8,128)(2,1)} %param.10) | copy-start | bytes 3145732
  1.4 26.4 %copy-start.1 = (bf16[1,512,1024]{2,1,0:T(8,128)(2,1)S(1)}, bf16[1,512,1024]{2,1,0:T(8,128)(2,1)}, u32[]{:S(2)}) copy-start(bf16[1,512,1024]{2,1,0:T(8,128)(2,1)} %param.11) | copy-start | bytes 3145732
  28.4 4.3 %collective-permute-start = (bf16[8,192,256]{2,1,0:T(8,128)(2,1)S(1)}, bf16[8,192,256]{2,1,0:T(8,128)(2,1)S(1)}, u32[]{:S(2)}, u32[]{:S(2)}) collective-permute-start(bf16[8,192,256]{2,1,0:T(8,128)(2,1)S(1)} %shard_map.120), channel_id=1, source_target_pairs={{0,1},{1,0},{2,3},{3,2},{4,5},{5,4},{6,7},{7,6},{8,9},{9,8},{10,11... | collective-permute-start | bytes 2359304 | tf_op jit(solution)/shard_map/ppermute | solution.py:233
  33.3 16.5 %copy-start.5 = (f32[1,128]{1,0:T(1,128)S(1)}, f32[1,128]{1,0:T(1,128)}, u32[]{:S(2)}) copy-start(f32[1,128]{1,0:T(1,128)} %gain_ref.5) | copy-start | bytes 1540
  33.3 19.6 %copy-start.3 = (bf16[1,512,512]{2,1,0:T(8,128)(2,1)S(1)}, bf16[1,512,512]{2,1,0:T(8,128)(2,1)}, u32[]{:S(2)}) copy-start(bf16[1,512,512]{2,1,0:T(8,128)(2,1)} %param.15) | copy-start | bytes 1572868
  49.8 3.1 %copy-start.2 = (bf16[1,512,512]{2,1,0:T(8,128)(2,1)S(1)}, bf16[1,512,512]{2,1,0:T(8,128)(2,1)}, u32[]{:S(2)}) copy-start(bf16[1,512,512]{2,1,0:T(8,128)(2,1)} %param.9) | copy-start | bytes 1572868
  50.0 2.9 %copy-start.4 = (s32[512]{0:T(512)S(1)}, s32[512]{0:T(512)}, u32[]{:S(2)}) copy-start(s32[512]{0:T(512)} %param.14) | copy-start | bytes 6148
  50.0 2.9 %copy-start.6 = (f32[1,128]{1,0:T(1,128)S(1)}, f32[1,128]{1,0:T(1,128)}, u32[]{:S(2)}) copy-start(f32[1,128]{1,0:T(1,128)} %gain_ref.4) | copy-start | bytes 1540
  50.0 2.8 %collective-permute-start.1 = (bf16[192,256]{1,0:T(8,128)(2,1)S(1)}, bf16[192,256]{1,0:T(8,128)(2,1)S(1)}, u32[]{:S(2)}, u32[]{:S(2)}) collective-permute-start(bf16[192,256]{1,0:T(8,128)(2,1)S(1)} %get-tuple-element.32.mine_ref), channel_id=1, source_target_pairs={{0,1},{1,0},{2,3},{3,2},{4,5},{5,4},{6,7},{7,6},{8,9},{9,8},{10,11... | collective-permute-start | bytes 294920 | tf_op jit(solution)/shard_map/ppermute | solution.py:233
  57.5 1.4 %collective-permute-start.2 = (bf16[192,256]{1,0:T(8,128)(2,1)S(1)}, bf16[192,256]{1,0:T(8,128)(2,1)S(1)}, u32[]{:S(2)}, u32[]{:S(2)}) collective-permute-start(bf16[192,256]{1,0:T(8,128)(2,1)S(1)} %get-tuple-element.38), channel_id=1, source_target_pairs={{0,1},{1,0},{2,3},{3,2},{4,5},{5,4},{6,7},{7,6},{8,9},{9,8},{10,11... | collective-permute-start | bytes 294920 | tf_op jit(solution)/shard_map/ppermute | solution.py:233
  73.7 3.5 %collective-permute-start.3 = (bf16[8,192,256]{2,1,0:T(8,128)(2,1)S(1)}, bf16[8,192,256]{2,1,0:T(8,128)(2,1)S(1)}, u32[]{:S(2)}, u32[]{:S(2)}) collective-permute-start(bf16[8,192,256]{2,1,0:T(8,128)(2,1)S(1)} %all_to_all.22.grads_ref.mine_ref), channel_id=1, source_target_pairs={{0,1},{1,0},{2,3},{3,2},{4,5},{5,4},{6,7},{7,6},{8,9},{9,8},{10,11... | collective-permute-start | bytes 2359304 | tf_op jit(solution)/shard_map/ppermute | solution.py:233
  78.8 18.8 %all-to-all-start.3 = ((bf16[16,24,512]{2,1,0:T(8,128)(2,1)}), bf16[16,24,512]{2,1,0:T(8,128)(2,1)S(1)}, u32[]{:S(2)}, u32[]{:S(2)}) async-start(bf16[16,24,512]{2,1,0:T(8,128)(2,1)} %bitcast.9), calls=%async_computation.3 | async-start | bytes 786432 | tf_op jit(solution)/shard_map/all_to_all | solution.py:297

commit v4 on v3

v4 whole, which is shorter than its diff:
```python
import jax
import jax.numpy as jnp
from jax import lax
from jax.experimental import pallas as pl
from jax.experimental.pallas import tpu as pltpu
from jax.sharding import PartitionSpec as P

TILE_ROWS = 96
CORES = 2
LOG2_E = 1.4426950408889634
epsilon = 1e-05

f32 = jnp.float32
bf16 = jnp.bfloat16

BOTH_LAST = (((1,), (1,)), ((), ()))

ANY = pl.BlockSpec(memory_space=pl.ANY)
VMEM = pl.BlockSpec(memory_space=pltpu.VMEM)
SMEM = pl.BlockSpec(memory_space=pltpu.SMEM)
PARAMS = pltpu.CompilerParams(vmem_limit_bytes=40 * 1024 * 1024)


def dot(a, b, dims=(((1,), (0,)), ((), ()))):
    return lax.dot_general(a, b, dims, preferred_element_type=f32)


def head_norm(raw_rows, gain_row):
    inverse = lax.rsqrt(jnp.mean(raw_rows * raw_rows, -1, keepdims=True) + epsilon)
    return (raw_rows * inverse * gain_row, inverse)


def head_norm_back(raw_rows, inverse, gain_row, upstream):
    scaled = upstream * gain_row
    return inverse * scaled - raw_rows * (
        inverse * inverse * inverse * jnp.mean(raw_rows * scaled, -1, keepdims=True)
    )


def by_core(core, zero, one):
    return jnp.where(core == 0, zero, one)


def copies_kernel(rows_ref, out_ref):
    for i in range(out_ref.shape[0]):
        out_ref[i] = rows_ref[...]


def project_kernel(core_ref, rows_ref, key_ref, value_ref, *refs):
    *before, out_ref = refs
    kv_heads, _, head = out_ref.shape
    rows = rows_ref[...]
    for kind, weight_ref in enumerate((key_ref, value_ref)):

        @pl.when(core_ref[0] == kind)
        def _(weight_ref=weight_ref):
            for low in range(0, kv_heads, 2):
                pair = dot(rows, weight_ref[:, low * head : (low + 2) * head])
                for i in range(2):
                    here = pair[:, i * head : (i + 1) * head]
                    if before:
                        here = here + before[0][low + i]
                    out_ref[low + i] = here.astype(out_ref.dtype)


def norm_kernel(core_ref, parts_ref, gain_ref, kv_ref, raw_ref):
    total = parts_ref[0].astype(f32)
    for i in range(1, parts_ref.shape[0]):
        total = total + parts_ref[i].astype(f32)
    keys, _ = head_norm(total, gain_ref[...])
    raw_ref[...] = total
    kv_ref[...] = by_core(core_ref[0], keys, total).astype(bf16)


def attention_kernel(
    core_ref, mine_ref, other_ref, query_ref, up_ref, gain_ref, seen_ref,
    context_ref, query_grad_ref, send_ref, keep_ref,
    context_held, query_grad_held, sems,
):
    core = core_ref[0]
    head = gain_ref.shape[1]
    rows = mine_ref.shape[0]
    text, width = query_ref.shape
    scale = head ** (-0.5)
    keys = by_core(core, mine_ref[...], other_ref[...])
    values = by_core(core, other_ref[...], mine_ref[...])
    keys_t = keys.astype(f32).T.astype(bf16)
    values_t = values.astype(f32).T.astype(bf16)
    gain = gain_ref[...]
    seen = seen_ref[...]
    empty = jnp.where(seen == 0, 1.0, 0.0)
    visible = jnp.concatenate(
        [jnp.broadcast_to(i < seen, (TILE_ROWS, text)) for i in range(rows // TILE_ROWS)], 0
    )
    key_grad = jnp.zeros((rows, head), f32)
    value_grad = jnp.zeros((rows, head), f32)
    copies = []
    for h in range(width // head):
        cols = slice(h * head, (h + 1) * head)
        query = query_ref[:, cols].astype(f32)
        up = up_ref[:, cols]
        normed_float, inverse = head_norm(query, gain)
        normed = normed_float.astype(bf16)
        scores = dot(keys, normed, BOTH_LAST)
        expo = jnp.where(visible, jnp.exp2(scores * (scale * LOG2_E)), 0.0)
        totals = jnp.sum(expo, 0, keepdims=True) + empty
        probs = expo * (1.0 / totals)
        probs_low = probs.astype(bf16)
        prob_grad = dot(values, up, BOTH_LAST)
        row_dot = jnp.sum(probs * prob_grad, 0, keepdims=True)
        score_grad = (probs * (prob_grad - row_dot)).astype(bf16)
        key_grad = key_grad + dot(score_grad, normed)
        value_grad = value_grad + dot(probs_low, up)
        context_held[:, cols] = dot(values_t, probs_low).T.astype(bf16)
        normed_grad = dot(keys_t, score_grad).T * scale
        query_grad_held[:, cols] = head_norm_back(query, inverse, gain, normed_grad).astype(bf16)
        for i, (held, out) in enumerate(
            ((context_held, context_ref), (query_grad_held, query_grad_ref))
        ):
            copy = pltpu.make_async_copy(held.at[:, cols], out.at[:, cols], sems.at[2 * h + i])
            copy.start()
            copies.append(copy)
    key_grad = key_grad * scale
    keep_ref[...] = by_core(core, key_grad, value_grad)
    send_ref[...] = by_core(core, value_grad, key_grad).astype(bf16)
    for copy in copies:
        copy.wait()


def kv_grad_kernel(core_ref, keep_ref, received_ref, raw_ref, gain_ref, out_ref):
    total = keep_ref[...] + received_ref[...].astype(f32)
    gain = gain_ref[...]
    raw = raw_ref[...]
    _, inverse = head_norm(raw, gain)
    key_raw_grad = head_norm_back(raw, inverse, gain, total)
    kv_grad = by_core(core_ref[0], key_raw_grad, total).astype(bf16)
    for i in range(out_ref.shape[0]):
        out_ref[i] = kv_grad


def image_product(grads_ref, weight_ref, now):
    kv_heads, _, head = grads_ref.shape
    total = None
    for low in range(0, kv_heads, 2):
        pair = jnp.concatenate([grads_ref[low], grads_ref[low + 1]], 1)
        term = dot(pair, weight_ref[now, low * head : (low + 2) * head], BOTH_LAST)
        total = term if total is None else total + term
    return total


def image_kernel(core_ref, grads_ref, key_ref, value_ref, out_ref):
    for kind, weight_ref in enumerate((key_ref, value_ref)):

        @pl.when(core_ref[0] == kind)
        def _(weight_ref=weight_ref):
            out_ref[...] = image_product(grads_ref, weight_ref, slice(None)).astype(out_ref.dtype)


def add_kernel(own_ref, received_ref, out_ref):
    out_ref[...] = (own_ref[...] + received_ref[...].astype(f32)).astype(bf16)


def weight_grad_kernel(core_ref, rows_ref, mine_ref, other_ref, key_ref, value_ref):
    kv_heads, _, head = mine_ref.shape
    core = core_ref[0]
    rows_t = rows_ref[...].astype(f32).T.astype(bf16)
    for low in range(0, kv_heads, 2):
        cols = slice(low * head, (low + 2) * head)
        mine = jnp.concatenate([mine_ref[low], mine_ref[low + 1]], 1)
        other = jnp.concatenate([other_ref[low], other_ref[low + 1]], 1)
        key_ref[:, cols] = dot(rows_t, by_core(core, mine, other)).astype(bf16)
        value_ref[:, cols] = dot(rows_t, by_core(core, other, mine)).astype(bf16)


def call(kernel, outs, *args, scalar=False, cost=None, scratch=(), to_hbm=()):
    many = len(outs) > 1
    shapes = tuple(jax.ShapeDtypeStruct(shape, kind) for shape, kind in outs)
    places = tuple(ANY if i in to_hbm else VMEM for i in range(len(outs)))
    return pl.pallas_call(
        kernel,
        out_shape=shapes if many else shapes[0],
        in_specs=[SMEM if scalar and i == 0 else VMEM for i in range(len(args))],
        out_specs=places if many else places[0],
        scratch_shapes=list(scratch),
        compiler_params=PARAMS,
        cost_estimate=cost,
    )(*args)


def fence(*arrays):
    return lax.optimization_barrier(arrays)


def shards(
    image_rows, queries, key_weight, value_weight, query_gain, key_gain, tiles_seen, context_grad
):
    sections = lax.axis_size("section")
    tp = lax.axis_size("tp")
    chips = tp // CORES
    core = (lax.axis_index("tp") % CORES).astype(jnp.int32).reshape(1)
    same_core = [[i for i in range(tp) if i % CORES == c] for c in range(CORES)]
    swap = [(i, i ^ 1) for i in range(tp)]

    def other_core(x):
        return lax.ppermute(x, "tp", swap)

    def to_core(x, c):
        return lax.ppermute(x, "tp", [(i ^ 1, i) for i in range(tp) if i % CORES == c])

    def over_chips(x):
        return lax.all_to_all(x, "tp", 0, 0, axis_index_groups=same_core)

    own_rows, features = image_rows.shape
    rows_total = sections * own_rows
    kv_width = key_weight.shape[2]
    head = query_gain.shape[1]
    kv_heads = kv_width // head
    text, width = queries.shape[1:]
    pieces = (kv_heads, rows_total, head)
    square = (rows_total, head)

    key_other = to_core(key_weight[0], 0)
    value_other = to_core(value_weight[0], 1)
    image_rows, core = fence(image_rows, core)
    copies = call(
        copies_kernel, [((sections, own_rows, features), bf16)], image_rows,
        cost=pl.CostEstimate(flops=2**34, bytes_accessed=2**25, transcendentals=0),
    )
    blocks = lax.all_to_all(copies, "section", 0, 0)
    blocks, key_weight, value_weight, key_other, value_other, queries, context_grad = fence(
        blocks, key_weight[0], value_weight[0], key_other, value_other, queries[0], context_grad[0]
    )
    rows = blocks.reshape(rows_total, features)
    rows_other = other_core(rows)
    partial = call(
        project_kernel, [(pieces, f32)], core, rows, key_weight, value_weight, scalar=True
    )
    partial = call(
        project_kernel, [(pieces, bf16)],
        core, rows_other, key_other, value_other, partial, scalar=True,
    )
    parts = over_chips(partial)
    kv_mine, raw = call(
        norm_kernel, [(square, bf16), (square, f32)], core, parts, key_gain, scalar=True
    )
    kv_other = other_core(kv_mine)
    context, query_grad, send, keep = call(
        attention_kernel,
        [((text, width), bf16), ((text, width), bf16), (square, bf16), (square, f32)],
        core, kv_mine, kv_other, queries, context_grad, query_gain, tiles_seen[None],
        scalar=True, to_hbm=(0, 1),
        scratch=[pltpu.VMEM((text, width), bf16)] * 2
        + [pltpu.SemaphoreType.DMA((2 * width // head,))],
    )
    received = other_core(send)
    copies = call(
        kv_grad_kernel, [(pieces, bf16)], core, keep, received, raw, key_gain, scalar=True
    )
    grads = over_chips(copies)
    image_send = call(
        image_kernel, [((rows_total, features), bf16)],
        core, grads, key_other, value_other, scalar=True,
    )
    received = other_core(image_send)
    image_own = call(
        image_kernel, [((rows_total, features), f32)],
        core, grads, key_weight, value_weight, scalar=True,
    )
    image_part = call(add_kernel, [((rows_total, features), bf16)], image_own, received)
    image_part, rows, grads = fence(image_part, rows, grads)
    grads_other = other_core(grads)
    image_parts = lax.all_to_all(
        image_part.reshape(sections, own_rows, features), "section", 0, 0
    )
    key_weight_grad, value_weight_grad = call(
        weight_grad_kernel, [((features, kv_width), bf16)] * 2,
        core, rows, grads, grads_other, scalar=True,
        cost=pl.CostEstimate(
            flops=2 * features * 2 * kv_width * rows_total,
            bytes_accessed=4 * features * 2 * kv_width,
            transcendentals=0,
        ),
    )
    image_parts, key_weight_grad, value_weight_grad = fence(
        image_parts, key_weight_grad, value_weight_grad
    )
    image_grad = jnp.sum(image_parts.astype(f32), 0)
    return (
        context[None], query_grad[None], key_weight_grad[None], value_weight_grad[None], image_grad
    )


def solution(mesh):
    return jax.shard_map(
        shards,
        mesh=mesh,
        in_specs=(
            P("section", "tp"),
            P("section", None, "tp"),
            P("section", "tp", None),
            P("section", "tp", None),
            P("section", None),
            P("section", None),
            P(),
            P("section", None, "tp"),
        ),
        out_specs=(
            P("section", None, "tp"),
            P("section", None, "tp"),
            P("section", "tp", None),
            P("section", "tp", None),
            P("section", "tp"),
        ),
        check_vma=False,
    )
```

time: 98.6 us -> 101 us (1.024)
  starting transfers between devices: 9.88 us -> 16.8 us
  blocking collectives: 57.5 us -> 54.8 us
  waiting for transfers between devices: 17.4 us -> 16.1 us
    ppermute x0 -> x2, starting transfers between devices: none -> 6.5 us  [to_core(): lax.ppermute(x, 'tp', [(i ^ 1, i) for i in range(tp) if i % CORES == c])]
    all_to_all x1, blocking collectives: 26.3 us -> 23.7 us  [shards(): blocks = lax.all_to_all(copies, 'section', 0, 0)]
    ppermute x4 -> x5, waiting for transfers between devices: 4.85 us -> 3.37 us  [other_core(): return lax.ppermute(x, 'tp', swap)]
    pallas_call x9 -> x10, Pallas kernels: 11.3 us -> 10.8 us  [call(): pl.pallas_call(kernel, out_shape=shapes if many else shapes[0], in_specs=...]
    ppermute x4 -> x5, starting transfers between devices: 6.31 us -> 6.76 us  [other_core(): return lax.ppermute(x, 'tp', swap)]
  transfers between devices with their start and end apart: 5 -> 8, of which waited for: 5 -> 5; matrix products, arithmetic and copies ran while one was open for 0% -> 0% of each run, Pallas kernels for 4% -> 4%
where the time goes in v4:
time: 101 us
  blocking collectives  54.8 us (54%)
  starting transfers between devices  16.8 us (17%)
  waiting for transfers between devices  16.1 us (16%)
  Pallas kernels  10.8 us (11%)
    all_to_all x2, blocking collectives, over_chips(): return lax.all_to_all(x, 'tp', 0, 0, axis_index_groups=same_core)  31.1 us
    all_to_all x1, blocking collectives, shards(): blocks = lax.all_to_all(copies, 'section', 0, 0)  23.7 us
    all_to_all x1, waiting for transfers between devices, shards(): lax.all_to_all(image_part.reshape(sections, own_rows, features), 'section...  12.8 us
    pallas_call x10, Pallas kernels, call(): pl.pallas_call(kernel, out_shape=shapes if many else shapes[0], in_specs=...  10.8 us
    ppermute x5, starting transfers between devices, other_core(): return lax.ppermute(x, 'tp', swap)  6.76 us
    ppermute x2, starting transfers between devices, to_core(): lax.ppermute(x, 'tp', [(i ^ 1, i) for i in range(tp) if i % CORES == c])  6.5 us
    all_to_all x1, starting transfers between devices, shards(): lax.all_to_all(image_part.reshape(sections, own_rows, features), 'section...  3.55 us
    ppermute x5, waiting for transfers between devices, other_core(): return lax.ppermute(x, 'tp', swap)  3.37 us
  transfers between devices with their start and end apart: 8, of which 5 were waited for; matrix products, arithmetic and copies ran while one was open for 0% of the time, Pallas kernels for 4%

profile of v4, /device:TPU:1, one launch (start us, length us, event | category | flops | bytes accessed | tf_op | source)
XLA Modules:
  0.0 100.8 jit_solution(16275507226935453580)
XLA Ops:
  0.6 5.2 %collective-permute-start = (bf16[512,1024]{1,0:T(8,128)(2,1)}, bf16[512,1024]{1,0:T(8,128)(2,1)S(1)}, u32[]{:S(2)}, u32[]{:S(2)}) collective-permute-start(bf16[512,1024]{1,0:T(8,128)(2,1)} %bitcast.12), channel_id=1, source_target_pairs={{1,0},{3,2},{5,4},{7,6},{9,8},{11,10},{13,12},{15,14},{17,16},{19,... | collective-permute-start | bytes 3145736 | tf_op jit(solution)/shard_map/ppermute | solution.py:208
  5.8 1.3 %collective-permute-start.1 = (bf16[512,1024]{1,0:T(8,128)(2,1)}, bf16[512,1024]{1,0:T(8,128)(2,1)S(1)}, u32[]{:S(2)}, u32[]{:S(2)}) collective-permute-start(bf16[512,1024]{1,0:T(8,128)(2,1)} %bitcast.15), channel_id=1, source_target_pairs={{0,1},{2,3},{4,5},{6,7},{8,9},{10,11},{12,13},{14,15},{16,17},{18,... | collective-permute-start | bytes 3145736 | tf_op jit(solution)/shard_map/ppermute | solution.py:208
  7.2 0.7 copy-done.7
  7.9 23.7 %all_to_all.20 = bf16[16,24,512]{2,1,0:T(8,128)(2,1)S(1)} all-to-all(bf16[16,24,512]{2,1,0:T(8,128)(2,1)S(1)} %shard_map.119), channel_id=1, replica_groups=mesh['section'=16,'tp'=16] {'section'}, dimensions={0} | all-to-all | bytes 786432 | tf_op jit(solution)/shard_map/all_to_all | solution.py:229
  31.6 2.3 %collective-permute-start.2 = (bf16[384,512]{1,0:T(8,128)(2,1)S(1)}, bf16[384,512]{1,0:T(8,128)(2,1)S(1)}, u32[]{:S(2)}, u32[]{:S(2)}) collective-permute-start(bf16[384,512]{1,0:T(8,128)(2,1)S(1)} %bitcast.18), channel_id=1, source_target_pairs={{0,1},{1,0},{2,3},{3,2},{4,5},{5,4},{6,7},{7,6},{8,9},{9,8},{10,11... | collective-permute-start | bytes 1179656 | tf_op jit(solution)/shard_map/ppermute | solution.py:205
  34.0 0.6 shard_map.120.refs_0_
  34.6 0.7 collective-permute-done.2.rows_ref
  35.3 0.6 shard_map.121
  36.0 16.5 %all_to_all.21.parts_ref = bf16[8,384,128]{2,1,0:T(8,128)(2,1)S(1)} all-to-all(bf16[8,384,128]{2,1,0:T(8,128)(2,1)S(1)} %shard_map.121), channel_id=1, replica_groups={{0,2,4,6,8,10,12,14},{1,3,5,7,9,11,13,15},{16,18,20,22,24,26,28,30},{17..., dimensions={0} | all-to-all | bytes 1572864 | tf_op jit(solution)/shard_map/all_to_all | solution.py:211
  52.6 1.9 %collective-permute-start.3 = (bf16[384,128]{1,0:T(8,128)(2,1)S(1)}, bf16[384,128]{1,0:T(8,128)(2,1)S(1)}, u32[]{:S(2)}, u32[]{:S(2)}) collective-permute-start(bf16[384,128]{1,0:T(8,128)(2,1)S(1)} %get-tuple-element.35.mine_ref), channel_id=1, source_target_pairs={{0,1},{1,0},{2,3},{3,2},{4,5},{5,4},{6,7},{7,6},{8,9},{9,8},{10,11... | collective-permute-start | bytes 294920 | tf_op jit(solution)/shard_map/ppermute | solution.py:205
  54.6 0.9 collective-permute-done.3.other_ref
  55.5 4.5 %shard_map.123 = (bf16[512,512]{1,0:T(8,128)(2,1)}, bf16[512,512]{1,0:T(8,128)(2,1)}, bf16[384,128]{1,0:T(8,128)(2,1)S(1)}, f32[384,128]{1,0:T(8,128)S(1)}) custom-call(s32[1]{0:T(128)} %bitcast.core_ref, bf16[384,128]{1,0:T(8,128)(2,1)S(1)} %get-tuple-element.35.mine_ref, bf16[384,128]{1,0:T(8,128)(2,1)S(1)} %collective-permute-done.3.other_ref, ...), custom_call_target="tpu_custom_call" | custom-call | tf_op jit(solution)/shard_map/pallas_call | solution.py:179
  60.0 0.5 collective-permute-start.4
  60.5 0.9 collective-permute-done.4.received_ref
  61.7 14.7 %all_to_all.22.grads_ref.mine_ref = bf16[8,384,128]{2,1,0:T(8,128)(2,1)S(1)} all-to-all(bf16[8,384,128]{2,1,0:T(8,128)(2,1)S(1)} %shard_map.124), channel_id=1, replica_groups={{0,2,4,6,8,10,12,14},{1,3,5,7,9,11,13,15},{16,18,20,22,24,26,28,30},{17..., dimensions={0} | all-to-all | bytes 1572864 | tf_op jit(solution)/shard_map/all_to_all | solution.py:211
  76.3 0.6 shard_map.126
  76.9 1.7 %collective-permute-start.5 = (bf16[384,512]{1,0:T(8,128)(2,1)S(1)}, bf16[384,512]{1,0:T(8,128)(2,1)S(1)}, u32[]{:S(2)}, u32[]{:S(2)}) collective-permute-start(bf16[384,512]{1,0:T(8,128)(2,1)S(1)} %shard_map.126), channel_id=1, source_target_pairs={{0,1},{1,0},{2,3},{3,2},{4,5},{5,4},{6,7},{7,6},{8,9},{9,8},{10,11... | collective-permute-start | bytes 1179656 | tf_op jit(solution)/shard_map/ppermute | solution.py:205
  78.6 0.6 shard_map.125.own_ref
  79.2 0.7 collective-permute-done.5.received_ref
  80.0 0.8 shard_map.127
  81.2 3.6 %all-to-all-start.3 = ((bf16[16,24,512]{2,1,0:T(8,128)(2,1)}), bf16[16,24,512]{2,1,0:T(8,128)(2,1)S(1)}, u32[]{:S(2)}, u32[]{:S(2)}) async-start(bf16[16,24,512]{2,1,0:T(8,128)(2,1)} %bitcast.9), calls=%async_computation.3 | async-start | bytes 786432 | tf_op jit(solution)/shard_map/all_to_all | solution.py:272
  84.8 2.6 %shard_map.128 = (bf16[512,1024]{1,0:T(8,128)(2,1)}, bf16[512,1024]{1,0:T(8,128)(2,1)}) custom-call(s32[1]{0:T(128)} %bitcast.core_ref, bf16[384,512]{1,0:T(8,128)(2,1)S(1)} %bitcast.20, bf16[8,384,128]{2,1,0:T(8,128)(2,1)S(1)} %all_to_all.22.grads_ref.mine_ref, bf16[8,384,128]{2,1,0:T(8,128)(2,1)S(1)} %collective-permute-done.6.other_ref), custom_call_target="tpu_custom_call" | custom-call | flops 805306368 | bytes 4194304 | tf_op jit(solution)/shard_map/pallas_call | solution.py:179
  87.4 12.8 %all-to-all-done.3 = bf16[16,24,512]{2,1,0:T(8,128)(2,1)S(1)} async-done(((bf16[16,24,512]{2,1,0:T(8,128)(2,1)}), bf16[16,24,512]{2,1,0:T(8,128)(2,1)S(1)}, u32[]{:S(2)}, u32[]{:S(2)}) %all-to-all-start.3) | async-done | bytes 393248 | tf_op jit(solution)/shard_map/all_to_all | solution.py:272
  100.2 0.7 convert_reduce_fusion
  (22 shorter events, 0.8 us)
Async XLA Ops:
  0.6 31.0 %collective-permute-start = (bf16[512,1024]{1,0:T(8,128)(2,1)}, bf16[512,1024]{1,0:T(8,128)(2,1)S(1)}, u32[]{:S(2)}, u32[]{:S(2)}) collective-permute-start(bf16[512,1024]{1,0:T(8,128)(2,1)} %bitcast.12), channel_id=1, source_target_pairs={{1,0},{3,2},{5,4},{7,6},{9,8},{11,10},{13,12},{15,14},{17,16},{19,... | collective-permute-start | bytes 3145736 | tf_op jit(solution)/shard_map/ppermute | solution.py:208
  5.8 25.8 %collective-permute-start.1 = (bf16[512,1024]{1,0:T(8,128)(2,1)}, bf16[512,1024]{1,0:T(8,128)(2,1)S(1)}, u32[]{:S(2)}, u32[]{:S(2)}) collective-permute-start(bf16[512,1024]{1,0:T(8,128)(2,1)} %bitcast.15), channel_id=1, source_target_pairs={{0,1},{2,3},{4,5},{6,7},{8,9},{10,11},{12,13},{14,15},{16,17},{18,... | collective-permute-start | bytes 3145736 | tf_op jit(solution)/shard_map/ppermute | solution.py:208
  7.2 0.7 copy-start.7
  7.9 26.0 %copy-start = (bf16[1,512,1024]{2,1,0:T(8,128)(2,1)S(1)}, bf16[1,512,1024]{2,1,0:T(8,128)(2,1)}, u32[]{:S(2)}) copy-start(bf16[1,512,1024]{2,1,0:T(8,128)(2,1)} %param.10) | copy-start | bytes 3145732
  7.9 26.0 %copy-start.1 = (bf16[1,512,1024]{2,1,0:T(8,128)(2,1)S(1)}, bf16[1,512,1024]{2,1,0:T(8,128)(2,1)}, u32[]{:S(2)}) copy-start(bf16[1,512,1024]{2,1,0:T(8,128)(2,1)} %param.11) | copy-start | bytes 3145732
  31.6 3.6 %collective-permute-start.2 = (bf16[384,512]{1,0:T(8,128)(2,1)S(1)}, bf16[384,512]{1,0:T(8,128)(2,1)S(1)}, u32[]{:S(2)}, u32[]{:S(2)}) collective-permute-start(bf16[384,512]{1,0:T(8,128)(2,1)S(1)} %bitcast.18), channel_id=1, source_target_pairs={{0,1},{1,0},{2,3},{3,2},{4,5},{5,4},{6,7},{7,6},{8,9},{9,8},{10,11... | collective-permute-start | bytes 1179656 | tf_op jit(solution)/shard_map/ppermute | solution.py:205
  35.9 16.5 %copy-start.5 = (f32[1,128]{1,0:T(1,128)S(1)}, f32[1,128]{1,0:T(1,128)}, u32[]{:S(2)}) copy-start(f32[1,128]{1,0:T(1,128)} %gain_ref.5) | copy-start | bytes 1540
  35.9 19.6 %copy-start.2 = (bf16[1,512,512]{2,1,0:T(8,128)(2,1)S(1)}, bf16[1,512,512]{2,1,0:T(8,128)(2,1)}, u32[]{:S(2)}) copy-start(bf16[1,512,512]{2,1,0:T(8,128)(2,1)} %param.9) | copy-start | bytes 1572868
  35.9 19.6 %copy-start.3 = (bf16[1,512,512]{2,1,0:T(8,128)(2,1)S(1)}, bf16[1,512,512]{2,1,0:T(8,128)(2,1)}, u32[]{:S(2)}) copy-start(bf16[1,512,512]{2,1,0:T(8,128)(2,1)} %param.15) | copy-start | bytes 1572868
  36.0 19.6 %copy-start.4 = (s32[512]{0:T(512)S(1)}, s32[512]{0:T(512)}, u32[]{:S(2)}) copy-start(s32[512]{0:T(512)} %param.14) | copy-start | bytes 6148
  36.0 19.6 %copy-start.6 = (f32[1,128]{1,0:T(1,128)S(1)}, f32[1,128]{1,0:T(1,128)}, u32[]{:S(2)}) copy-start(f32[1,128]{1,0:T(1,128)} %gain_ref.4) | copy-start | bytes 1540
  52.6 2.9 %collective-permute-start.3 = (bf16[384,128]{1,0:T(8,128)(2,1)S(1)}, bf16[384,128]{1,0:T(8,128)(2,1)S(1)}, u32[]{:S(2)}, u32[]{:S(2)}) collective-permute-start(bf16[384,128]{1,0:T(8,128)(2,1)S(1)} %get-tuple-element.35.mine_ref), channel_id=1, source_target_pairs={{0,1},{1,0},{2,3},{3,2},{4,5},{5,4},{6,7},{7,6},{8,9},{9,8},{10,11... | collective-permute-start | bytes 294920 | tf_op jit(solution)/shard_map/ppermute | solution.py:205
  60.0 1.4 %collective-permute-start.4 = (bf16[384,128]{1,0:T(8,128)(2,1)S(1)}, bf16[384,128]{1,0:T(8,128)(2,1)S(1)}, u32[]{:S(2)}, u32[]{:S(2)}) collective-permute-start(bf16[384,128]{1,0:T(8,128)(2,1)S(1)} %get-tuple-element.41), channel_id=1, source_target_pairs={{0,1},{1,0},{2,3},{3,2},{4,5},{5,4},{6,7},{7,6},{8,9},{9,8},{10,11... | collective-permute-start | bytes 294920 | tf_op jit(solution)/shard_map/ppermute | solution.py:205
  76.9 3.1 %collective-permute-start.5 = (bf16[384,512]{1,0:T(8,128)(2,1)S(1)}, bf16[384,512]{1,0:T(8,128)(2,1)S(1)}, u32[]{:S(2)}, u32[]{:S(2)}) collective-permute-start(bf16[384,512]{1,0:T(8,128)(2,1)S(1)} %shard_map.126), channel_id=1, source_target_pairs={{0,1},{1,0},{2,3},{3,2},{4,5},{5,4},{6,7},{7,6},{8,9},{9,8},{10,11... | collective-permute-start | bytes 1179656 | tf_op jit(solution)/shard_map/ppermute | solution.py:205
  80.8 3.9 %collective-permute-start.6 = (bf16[8,384,128]{2,1,0:T(8,128)(2,1)S(1)}, bf16[8,384,128]{2,1,0:T(8,128)(2,1)S(1)}, u32[]{:S(2)}, u32[]{:S(2)}) collective-permute-start(bf16[8,384,128]{2,1,0:T(8,128)(2,1)S(1)} %all_to_all.22.grads_ref.mine_ref), channel_id=1, source_target_pairs={{0,1},{1,0},{2,3},{3,2},{4,5},{5,4},{6,7},{7,6},{8,9},{9,8},{10,11... | collective-permute-start | bytes 2359304 | tf_op jit(solution)/shard_map/ppermute | solution.py:205
  81.2 19.0 %all-to-all-start.3 = ((bf16[16,24,512]{2,1,0:T(8,128)(2,1)}), bf16[16,24,512]{2,1,0:T(8,128)(2,1)S(1)}, u32[]{:S(2)}, u32[]{:S(2)}) async-start(bf16[16,24,512]{2,1,0:T(8,128)(2,1)} %bitcast.9), calls=%async_computation.3 | async-start | bytes 786432 | tf_op jit(solution)/shard_map/all_to_all | solution.py:272

commit v5 on v4

--- a/solution.py
+++ b/solution.py
@@ -7,6 +7,7 @@
 
 TILE_ROWS = 96
 CORES = 2
+ADD_STEPS = 4
 LOG2_E = 1.4426950408889634
 epsilon = 1e-05
 
@@ -16,9 +17,10 @@
 BOTH_LAST = (((1,), (1,)), ((), ()))
 
 ANY = pl.BlockSpec(memory_space=pl.ANY)
+HBM = pl.BlockSpec(memory_space=pltpu.HBM)
 VMEM = pl.BlockSpec(memory_space=pltpu.VMEM)
 SMEM = pl.BlockSpec(memory_space=pltpu.SMEM)
-PARAMS = pltpu.CompilerParams(vmem_limit_bytes=40 * 1024 * 1024)
+PARAMS = pltpu.CompilerParams(vmem_limit_bytes=16 * 1024 * 1024)
 
 
 def dot(a, b, dims=(((1,), (0,)), ((), ()))):
@@ -72,21 +74,24 @@
     kv_ref[...] = by_core(core_ref[0], keys, total).astype(bf16)
 
 
+def query_kernel(query_ref, gain_ref, normed_ref):
+    head = gain_ref.shape[1]
+    for low in range(0, query_ref.shape[1], head):
+        cols = slice(low, low + head)
+        normed, _ = head_norm(query_ref[:, cols].astype(f32), gain_ref[...])
+        normed_ref[:, cols] = normed.astype(bf16)
+
+
 def attention_kernel(
-    core_ref, mine_ref, other_ref, query_ref, up_ref, gain_ref, seen_ref,
-    context_ref, query_grad_ref, send_ref, keep_ref,
-    context_held, query_grad_held, sems,
+    core_ref, mine_ref, other_ref, normed_ref, up_ref, seen_ref,
+    probs_ref, score_grad_ref, send_ref, keep_ref,
 ):
     core = core_ref[0]
-    head = gain_ref.shape[1]
-    rows = mine_ref.shape[0]
-    text, width = query_ref.shape
+    rows, head = mine_ref.shape
+    text, width = normed_ref.shape
     scale = head ** (-0.5)
     keys = by_core(core, mine_ref[...], other_ref[...])
     values = by_core(core, other_ref[...], mine_ref[...])
-    keys_t = keys.astype(f32).T.astype(bf16)
-    values_t = values.astype(f32).T.astype(bf16)
-    gain = gain_ref[...]
     seen = seen_ref[...]
     empty = jnp.where(seen == 0, 1.0, 0.0)
     visible = jnp.concatenate(
@@ -94,13 +99,10 @@
     )
     key_grad = jnp.zeros((rows, head), f32)
     value_grad = jnp.zeros((rows, head), f32)
-    copies = []
     for h in range(width // head):
         cols = slice(h * head, (h + 1) * head)
-        query = query_ref[:, cols].astype(f32)
         up = up_ref[:, cols]
-        normed_float, inverse = head_norm(query, gain)
-        normed = normed_float.astype(bf16)
+        normed = normed_ref[:, cols]
         scores = dot(keys, normed, BOTH_LAST)
         expo = jnp.where(visible, jnp.exp2(scores * (scale * LOG2_E)), 0.0)
         totals = jnp.sum(expo, 0, keepdims=True) + empty
@@ -111,20 +113,53 @@
         score_grad = (probs * (prob_grad - row_dot)).astype(bf16)
         key_grad = key_grad + dot(score_grad, normed)
         value_grad = value_grad + dot(probs_low, up)
-        context_held[:, cols] = dot(values_t, probs_low).T.astype(bf16)
-        normed_grad = dot(keys_t, score_grad).T * scale
-        query_grad_held[:, cols] = head_norm_back(query, inverse, gain, normed_grad).astype(bf16)
-        for i, (held, out) in enumerate(
-            ((context_held, context_ref), (query_grad_held, query_grad_ref))
-        ):
-            copy = pltpu.make_async_copy(held.at[:, cols], out.at[:, cols], sems.at[2 * h + i])
-            copy.start()
-            copies.append(copy)
+        probs_ref[h] = probs_low
+        score_grad_ref[h] = score_grad
     key_grad = key_grad * scale
     keep_ref[...] = by_core(core, key_grad, value_grad)
     send_ref[...] = by_core(core, value_grad, key_grad).astype(bf16)
+
+
+def send_heads(held, out_ref, sems, width, fill):
+    copies = []
+    for h in range(held.shape[1] // width):
+        cols = slice(h * width, (h + 1) * width)
+        held[:, cols] = fill(h, cols).astype(bf16)
+        copies.append(pltpu.make_async_copy(held.at[:, cols], out_ref.at[:, cols], sems.at[h]))
+        copies[-1].start()
     for copy in copies:
         copy.wait()
+
+
+def context_kernel(core_ref, mine_ref, other_ref, probs_ref, context_ref, held, sems):
+    values = by_core(core_ref[0], other_ref[...], mine_ref[...])
+    values_t = values.astype(f32).T.astype(bf16)
+    send_heads(
+        held, context_ref, sems, values.shape[1], lambda h, _: dot(values_t, probs_ref[h]).T
+    )
+
+
+def normed_grad_kernel(core_ref, mine_ref, other_ref, score_grad_ref, out_ref):
+    keys = by_core(core_ref[0], mine_ref[...], other_ref[...])
+    keys_t = keys.astype(f32).T.astype(bf16)
+    for h in range(score_grad_ref.shape[0]):
+        out_ref[h] = (dot(keys_t, score_grad_ref[h]) * keys.shape[1] ** (-0.5)).astype(bf16)
+
+
+def query_grad_kernel(
+    query_ref, gain_ref, normed_grad_ref, query_grad_ref, held, sems, query_held, query_sem
+):
+    copy = pltpu.make_async_copy(query_ref, query_held, query_sem)
+    copy.start()
+    gain = gain_ref[...]
+    copy.wait()
+
+    def fill(h, cols):
+        query = query_held[:, cols].astype(f32)
+        _, inverse = head_norm(query, gain)
+        return head_norm_back(query, inverse, gain, normed_grad_ref[h].astype(f32).T)
+
+    send_heads(held, query_grad_ref, sems, gain.shape[1], fill)
 
 
 def kv_grad_kernel(core_ref, keep_ref, received_ref, raw_ref, gain_ref, out_ref):
@@ -156,30 +191,58 @@
             out_ref[...] = image_product(grads_ref, weight_ref, slice(None)).astype(out_ref.dtype)
 
 
-def add_kernel(own_ref, received_ref, out_ref):
-    out_ref[...] = (own_ref[...] + received_ref[...].astype(f32)).astype(bf16)
-
-
-def weight_grad_kernel(core_ref, rows_ref, mine_ref, other_ref, key_ref, value_ref):
+def add_kernel(own_ref, received_ref, out_ref, held, sems):
+    copies = []
+    step = held.shape[0] // ADD_STEPS
+    for i in range(ADD_STEPS):
+        now = slice(i * step, (i + 1) * step)
+        held[now] = (own_ref[now] + received_ref[now].astype(f32)).astype(bf16)
+        copies.append(pltpu.make_async_copy(held.at[now], out_ref.at[now], sems.at[i]))
+        copies[-1].start()
+    for copy in copies:
+        copy.wait()
+
+
+def weight_grad_kernel(
+    core_ref, rows_ref, mine_ref, other_ref, key_ref, value_ref, other_held, sems
+):
     kv_heads, _, head = mine_ref.shape
+    copies = [
+        pltpu.make_async_copy(other_ref.at[h], other_held.at[h], sems.at[h])
+        for h in range(kv_heads)
+    ]
+    for copy in copies:
+        copy.start()
     core = core_ref[0]
     rows_t = rows_ref[...].astype(f32).T.astype(bf16)
     for low in range(0, kv_heads, 2):
         cols = slice(low * head, (low + 2) * head)
         mine = jnp.concatenate([mine_ref[low], mine_ref[low + 1]], 1)
-        other = jnp.concatenate([other_ref[low], other_ref[low + 1]], 1)
+        copies[low].wait()
+        copies[low + 1].wait()
+        other = jnp.concatenate([other_held[low], other_held[low + 1]], 1)
         key_ref[:, cols] = dot(rows_t, by_core(core, mine, other)).astype(bf16)
         value_ref[:, cols] = dot(rows_t, by_core(core, other, mine)).astype(bf16)
 
 
-def call(kernel, outs, *args, scalar=False, cost=None, scratch=(), to_hbm=()):
+def sum_kernel(parts_ref, out_ref):
+    total = parts_ref[0].astype(f32)
+    for i in range(1, parts_ref.shape[0]):
+        total = total + parts_ref[i].astype(f32)
+    out_ref[...] = total
+
+
+def call(kernel, outs, *args, scalar=False, cost=None, scratch=(), to_hbm=(), from_hbm=()):
     many = len(outs) > 1
     shapes = tuple(jax.ShapeDtypeStruct(shape, kind) for shape, kind in outs)
     places = tuple(ANY if i in to_hbm else VMEM for i in range(len(outs)))
+    takes = [HBM if i in from_hbm else VMEM for i in range(len(args))]
+    if scalar:
+        takes[0] = SMEM
     return pl.pallas_call(
         kernel,
         out_shape=shapes if many else shapes[0],
-        in_specs=[SMEM if scalar and i == 0 else VMEM for i in range(len(args))],
+        in_specs=takes,
         out_specs=places if many else places[0],
         scratch_shapes=list(scratch),
         compiler_params=PARAMS,
@@ -204,9 +267,6 @@
     def other_core(x):
         return lax.ppermute(x, "tp", swap)
 
-    def to_core(x, c):
-        return lax.ppermute(x, "tp", [(i ^ 1, i) for i in range(tp) if i % CORES == c])
-
     def over_chips(x):
         return lax.all_to_all(x, "tp", 0, 0, axis_index_groups=same_core)
 
@@ -219,8 +279,8 @@
     pieces = (kv_heads, rows_total, head)
     square = (rows_total, head)
 
-    key_other = to_core(key_weight[0], 0)
-    value_other = to_core(value_weight[0], 1)
+    key_other = other_core(key_weight[0])
+    value_other = other_core(value_weight[0])
     image_rows, core = fence(image_rows, core)
     copies = call(
         copies_kernel, [((sections, own_rows, features), bf16)], image_rows,
@@ -243,16 +303,28 @@
     kv_mine, raw = call(
         norm_kernel, [(square, bf16), (square, f32)], core, parts, key_gain, scalar=True
     )
+    kv_mine, raw, queries, context_grad = fence(kv_mine, raw, queries, context_grad)
     kv_other = other_core(kv_mine)
-    context, query_grad, send, keep = call(
-        attention_kernel,
-        [((text, width), bf16), ((text, width), bf16), (square, bf16), (square, f32)],
-        core, kv_mine, kv_other, queries, context_grad, query_gain, tiles_seen[None],
-        scalar=True, to_hbm=(0, 1),
-        scratch=[pltpu.VMEM((text, width), bf16)] * 2
-        + [pltpu.SemaphoreType.DMA((2 * width // head,))],
-    )
+    normed = call(
+        query_kernel, [((text, width), bf16)], queries, query_gain,
+        cost=pl.CostEstimate(flops=2**30, bytes_accessed=2**20, transcendentals=0),
+    )
+    per_head = (width // head, rows_total, text)
+    probs, score_grad, send, keep = call(
+        attention_kernel, [(per_head, bf16), (per_head, bf16), (square, bf16), (square, f32)],
+        core, kv_mine, kv_other, normed, context_grad, tiles_seen[None], scalar=True,
+    )
+    send, keep, raw, probs, score_grad = fence(send, keep, raw, probs, score_grad)
     received = other_core(send)
+    out_scratch = [
+        pltpu.VMEM((text, width), bf16), pltpu.SemaphoreType.DMA((width // head,))
+    ]
+    context = call(
+        context_kernel, [((text, width), bf16)], core, kv_mine, kv_other, probs,
+        scalar=True, to_hbm=(0,), scratch=out_scratch,
+        cost=pl.CostEstimate(flops=2**30, bytes_accessed=2**20, transcendentals=0),
+    )
+    received, context = fence(received, context)
     copies = call(
         kv_grad_kernel, [(pieces, bf16)], core, keep, received, raw, key_gain, scalar=True
     )
@@ -261,30 +333,47 @@
         image_kernel, [((rows_total, features), bf16)],
         core, grads, key_other, value_other, scalar=True,
     )
+    image_send, grads, score_grad = fence(image_send, grads, score_grad)
     received = other_core(image_send)
     image_own = call(
         image_kernel, [((rows_total, features), f32)],
         core, grads, key_weight, value_weight, scalar=True,
     )
-    image_part = call(add_kernel, [((rows_total, features), bf16)], image_own, received)
-    image_part, rows, grads = fence(image_part, rows, grads)
+    normed_grad = call(
+        normed_grad_kernel, [((width // head, head, text), bf16)],
+        core, kv_mine, kv_other, score_grad, scalar=True,
+        cost=pl.CostEstimate(flops=2**30, bytes_accessed=2**20, transcendentals=0),
+    )
+    image_own, received, normed_grad = fence(image_own, received, normed_grad)
+    image_part = call(
+        add_kernel, [((rows_total, features), bf16)], image_own, received, to_hbm=(0,),
+        scratch=[pltpu.VMEM((rows_total, features), bf16), pltpu.SemaphoreType.DMA((ADD_STEPS,))],
+    )
+    image_part, rows, grads, normed_grad = fence(image_part, rows, grads, normed_grad)
     grads_other = other_core(grads)
     image_parts = lax.all_to_all(
         image_part.reshape(sections, own_rows, features), "section", 0, 0
     )
     key_weight_grad, value_weight_grad = call(
         weight_grad_kernel, [((features, kv_width), bf16)] * 2,
-        core, rows, grads, grads_other, scalar=True,
+        core, rows, grads, grads_other, scalar=True, from_hbm=(3,),
+        scratch=[pltpu.VMEM(pieces, bf16), pltpu.SemaphoreType.DMA((kv_heads,))],
         cost=pl.CostEstimate(
             flops=2 * features * 2 * kv_width * rows_total,
             bytes_accessed=4 * features * 2 * kv_width,
             transcendentals=0,
         ),
     )
-    image_parts, key_weight_grad, value_weight_grad = fence(
-        image_parts, key_weight_grad, value_weight_grad
-    )
-    image_grad = jnp.sum(image_parts.astype(f32), 0)
+    query_grad = call(
+        query_grad_kernel, [((text, width), bf16)],
+        queries, query_gain, normed_grad, to_hbm=(0,), from_hbm=(0,),
+        scratch=out_scratch + [pltpu.VMEM((text, width), bf16), pltpu.SemaphoreType.DMA],
+        cost=pl.CostEstimate(flops=2**30, bytes_accessed=2**20, transcendentals=0),
+    )
+    image_parts, key_weight_grad, value_weight_grad, query_grad = fence(
+        image_parts, key_weight_grad, value_weight_grad, query_grad
+    )
+    image_grad = call(sum_kernel, [((own_rows, features), f32)], image_parts)
     return (
         context[None], query_grad[None], key_weight_grad[None], value_weight_grad[None], image_grad
     )

time: 101 us -> 96.7 us (0.957)
  waiting for transfers between devices: 16.1 us -> 9.41 us
  Pallas kernels: 10.8 us -> 15.1 us
  starting transfers between devices: 16.8 us -> 13.2 us
  local copies, waits for them, and re-layouts: 0.77 us -> 2.6 us
    ppermute x2 -> x0, starting transfers between devices: 6.5 us -> none  [to_core(): lax.ppermute(x, 'tp', [(i ^ 1, i) for i in range(tp) if i % CORES == c])]
    all_to_all x1, waiting for transfers between devices: 12.8 us -> 8.08 us  [shards(): lax.all_to_all(image_part.reshape(sections, own_rows, features), 'section...]
    pallas_call x10 -> x15, Pallas kernels: 10.8 us -> 15.1 us  [call(): pl.pallas_call(kernel, out_shape=shapes if many else shapes[0], in_specs=...]
    ppermute x5 -> x7, starting transfers between devices: 6.76 us -> 9.64 us  [other_core(): return lax.ppermute(x, 'tp', swap)]
    ppermute x5 -> x7, waiting for transfers between devices: 3.37 us -> 1.33 us  [other_core(): return lax.ppermute(x, 'tp', swap)]
    unnamed x16 -> x22, local copies, waits for them, and re-layouts: 0.77 us -> 2.6 us
  transfers between devices with their start and end apart: 8 -> 8, of which waited for: 5 -> 3; matrix products, arithmetic and copies ran while one was open for 0% -> 0% of each run, Pallas kernels for 4% -> 10%
where the time goes in v5:
time: 96.7 us; the launch traced here: 96.3 us
  blocking collectives  55.2 us (57%)
  Pallas kernels  15.1 us (16%)
  starting transfers between devices  13.2 us (14%)
  waiting for transfers between devices  9.41 us (10%)
  local copies, waits for them, and re-layouts  2.6 us (3%)
    all_to_all x2, blocking collectives, over_chips(): return lax.all_to_all(x, 'tp', 0, 0, axis_index_groups=same_core)  31.4 us
    all_to_all x1, blocking collectives, shards(): blocks = lax.all_to_all(copies, 'section', 0, 0)  23.8 us
    pallas_call x15, Pallas kernels, call(): pl.pallas_call(kernel, out_shape=shapes if many else shapes[0], in_specs=...  15.1 us
    ppermute x7, starting transfers between devices, other_core(): return lax.ppermute(x, 'tp', swap)  9.64 us
    all_to_all x1, waiting for transfers between devices, shards(): lax.all_to_all(image_part.reshape(sections, own_rows, features), 'section...  8.08 us
    all_to_all x1, starting transfers between devices, shards(): lax.all_to_all(image_part.reshape(sections, own_rows, features), 'section...  3.55 us
    unnamed x22, local copies, waits for them, and re-layouts  2.6 us
  transfers between devices with their start and end apart: 8, of which 3 were waited for; matrix products, arithmetic and copies ran while one was open for 0% of the time, Pallas kernels for 10%

profile of v5, /device:TPU:1, one launch (start us, length us, event | category | flops | bytes accessed | tf_op | source)
XLA Modules:
  0.0 96.3 jit_solution(4882778942965298387)
XLA Ops:
  0.6 3.3 %collective-permute-start = (bf16[512,1024]{1,0:T(8,128)(2,1)}, bf16[512,1024]{1,0:T(8,128)(2,1)S(1)}, u32[]{:S(2)}, u32[]{:S(2)}) collective-permute-start(bf16[512,1024]{1,0:T(8,128)(2,1)} %bitcast.12), channel_id=1, source_target_pairs={{0,1},{1,0},{2,3},{3,2},{4,5},{5,4},{6,7},{7,6},{8,9},{9,8},{10,11... | collective-permute-start | bytes 3145736 | tf_op jit(solution)/shard_map/ppermute | solution.py:268
  4.1 0.7 copy-done.7
  4.8 23.8 %all_to_all.20 = bf16[16,24,512]{2,1,0:T(8,128)(2,1)S(1)} all-to-all(bf16[16,24,512]{2,1,0:T(8,128)(2,1)S(1)} %shard_map.119), channel_id=1, replica_groups=mesh['section'=16,'tp'=16] {'section'}, dimensions={0} | all-to-all | bytes 786432 | tf_op jit(solution)/shard_map/all_to_all | solution.py:289
  28.7 2.6 %collective-permute-start.2 = (bf16[384,512]{1,0:T(8,128)(2,1)S(1)}, bf16[384,512]{1,0:T(8,128)(2,1)S(1)}, u32[]{:S(2)}, u32[]{:S(2)}) collective-permute-start(bf16[384,512]{1,0:T(8,128)(2,1)S(1)} %bitcast.18), channel_id=1, source_target_pairs={{0,1},{1,0},{2,3},{3,2},{4,5},{5,4},{6,7},{7,6},{8,9},{9,8},{10,11... | collective-permute-start | bytes 1179656 | tf_op jit(solution)/shard_map/ppermute | solution.py:268
  31.2 0.6 shard_map.120.refs_0_
  31.8 0.7 collective-permute-done.2.rows_ref
  32.6 0.6 shard_map.121
  33.2 16.2 %all_to_all.21.parts_ref = bf16[8,384,128]{2,1,0:T(8,128)(2,1)S(1)} all-to-all(bf16[8,384,128]{2,1,0:T(8,128)(2,1)S(1)} %shard_map.121), channel_id=1, replica_groups={{0,2,4,6,8,10,12,14},{1,3,5,7,9,11,13,15},{16,18,20,22,24,26,28,30},{17..., dimensions={0} | all-to-all | bytes 1572864 | tf_op jit(solution)/shard_map/all_to_all | solution.py:271
  49.7 1.9 %collective-permute-start.3 = (bf16[384,128]{1,0:T(8,128)(2,1)S(1)}, bf16[384,128]{1,0:T(8,128)(2,1)S(1)}, u32[]{:S(2)}, u32[]{:S(2)}) collective-permute-start(bf16[384,128]{1,0:T(8,128)(2,1)S(1)} %get-tuple-element.58.mine_ref), channel_id=1, source_target_pairs={{0,1},{1,0},{2,3},{3,2},{4,5},{5,4},{6,7},{7,6},{8,9},{9,8},{10,11... | collective-permute-start | bytes 294920 | tf_op jit(solution)/shard_map/ppermute | solution.py:268
  51.9 0.6 collective-permute-done.3.other_ref
  52.5 2.7 %shard_map.124 = (bf16[4,384,512]{2,1,0:T(8,128)(2,1)S(1)}, bf16[4,384,512]{2,1,0:T(8,128)(2,1)S(1)}, bf16[384,128]{1,0:T(8,128)(2,1)S(1)}, f32[384,128]{1,0:T(8,128)S(1)}) custom-call(s32[1]{0:T(128)} %bitcast.core_ref, bf16[384,128]{1,0:T(8,128)(2,1)S(1)} %get-tuple-element.58.mine_ref, bf16[384,128]{1,0:T(8,128)(2,1)S(1)} %collective-permute-done.3.other_ref, ...), custom_call_target="tpu_custom_call" | custom-call | tf_op jit(solution)/shard_map/pallas_call | solution.py:242
  55.7 1.3 %shard_map.125 = bf16[512,512]{1,0:T(8,128)(2,1)} custom-call(s32[1]{0:T(128)} %bitcast.core_ref, bf16[384,128]{1,0:T(8,128)(2,1)S(1)} %get-tuple-element.58.mine_ref, bf16[384,128]{1,0:T(8,128)(2,1)S(1)} %collective-permute-done.3.other_ref, bf16[4,384,512]{2,1,0:T(8,128)(2,1)S(1)} %get-tuple-element.67.probs_ref), custom_call_target="tpu_custom_call" | custom-call | flops 1073741824 | bytes 1048576 | tf_op jit(solution)/shard_map/pallas_call | solution.py:242
  57.2 15.2 %all_to_all.22.grads_ref.mine_ref = bf16[8,384,128]{2,1,0:T(8,128)(2,1)S(1)} all-to-all(bf16[8,384,128]{2,1,0:T(8,128)(2,1)S(1)} %shard_map.126), channel_id=1, replica_groups={{0,2,4,6,8,10,12,14},{1,3,5,7,9,11,13,15},{16,18,20,22,24,26,28,30},{17..., dimensions={0} | all-to-all | bytes 1572864 | tf_op jit(solution)/shard_map/all_to_all | solution.py:271
  72.3 0.6 shard_map.127
  73.0 1.2 %collective-permute-start.5 = (bf16[384,512]{1,0:T(8,128)(2,1)S(1)}, bf16[384,512]{1,0:T(8,128)(2,1)S(1)}, u32[]{:S(2)}, u32[]{:S(2)}) collective-permute-start(bf16[384,512]{1,0:T(8,128)(2,1)S(1)} %shard_map.127), channel_id=1, source_target_pairs={{0,1},{1,0},{2,3},{3,2},{4,5},{5,4},{6,7},{7,6},{8,9},{9,8},{10,11... | collective-permute-start | bytes 1179656 | tf_op jit(solution)/shard_map/ppermute | solution.py:268
  74.1 0.6 shard_map.128.own_ref
  75.3 0.8 copy-done.9
  76.1 0.8 shard_map.130
  77.0 3.6 %all-to-all-start.3 = ((bf16[16,24,512]{2,1,0:T(8,128)(2,1)}), bf16[16,24,512]{2,1,0:T(8,128)(2,1)S(1)}, u32[]{:S(2)}, u32[]{:S(2)}) async-start(bf16[16,24,512]{2,1,0:T(8,128)(2,1)} %bitcast.8), calls=%async_computation.3 | async-start | bytes 786432 | tf_op jit(solution)/shard_map/all_to_all | solution.py:354
  80.6 1.0 %copy-done.10 = bf16[4,128,512]{2,1,0:T(8,128)(2,1)S(1)} copy-done((bf16[4,128,512]{2,1,0:T(8,128)(2,1)S(1)}, bf16[4,128,512]{2,1,0:T(8,128)(2,1)}, u32[]{:S(2)}) %copy-start.10) | copy-done | bytes 524312
  81.6 1.6 %shard_map.132 = bf16[512,512]{1,0:T(8,128)(2,1)} custom-call(bf16[512,512]{1,0:T(8,128)(2,1)S(1)} %bitcast.24, f32[1,128]{1,0:T(1,128)S(1)} %copy-done.8, bf16[4,128,512]{2,1,0:T(8,128)(2,1)S(1)} %copy-done.10), custom_call_target="tpu_custom_call" | custom-call | flops 1073741824 | bytes 1048576 | tf_op jit(solution)/shard_map/pallas_call | solution.py:242
  83.2 4.4 %shard_map.131 = (bf16[512,1024]{1,0:T(8,128)(2,1)}, bf16[512,1024]{1,0:T(8,128)(2,1)}) custom-call(s32[1]{0:T(128)} %bitcast.core_ref, bf16[384,512]{1,0:T(8,128)(2,1)S(1)} %bitcast.20, bf16[8,384,128]{2,1,0:T(8,128)(2,1)S(1)} %all_to_all.22.grads_ref.mine_ref, bf16[8,384,128]{2,1,0:T(8,128)(2,1)S(1)} %collective-permute-done.6.other_ref), custom_call_target="tpu_custom_call" | custom-call | flops 805306368 | bytes 4194304 | tf_op jit(solution)/shard_map/pallas_call | solution.py:242
  87.6 8.1 %all-to-all-done.3.parts_ref = bf16[16,24,512]{2,1,0:T(8,128)(2,1)S(1)} async-done(((bf16[16,24,512]{2,1,0:T(8,128)(2,1)}), bf16[16,24,512]{2,1,0:T(8,128)(2,1)S(1)}, u32[]{:S(2)}, u32[]{:S(2)}) %all-to-all-start.3) | async-done | bytes 393248 | tf_op jit(solution)/shard_map/all_to_all | solution.py:354
  95.6 0.7 shard_map.133
  (32 shorter events, 2.0 us)
Async XLA Ops:
  0.6 28.0 %collective-permute-start = (bf16[512,1024]{1,0:T(8,128)(2,1)}, bf16[512,1024]{1,0:T(8,128)(2,1)S(1)}, u32[]{:S(2)}, u32[]{:S(2)}) collective-permute-start(bf16[512,1024]{1,0:T(8,128)(2,1)} %bitcast.12), channel_id=1, source_target_pairs={{0,1},{1,0},{2,3},{3,2},{4,5},{5,4},{6,7},{7,6},{8,9},{9,8},{10,11... | collective-permute-start | bytes 3145736 | tf_op jit(solution)/shard_map/ppermute | solution.py:268
  4.0 24.7 %collective-permute-start.1 = (bf16[512,1024]{1,0:T(8,128)(2,1)}, bf16[512,1024]{1,0:T(8,128)(2,1)S(1)}, u32[]{:S(2)}, u32[]{:S(2)}) collective-permute-start(bf16[512,1024]{1,0:T(8,128)(2,1)} %bitcast.15), channel_id=1, source_target_pairs={{0,1},{1,0},{2,3},{3,2},{4,5},{5,4},{6,7},{7,6},{8,9},{9,8},{10,11... | collective-permute-start | bytes 3145736 | tf_op jit(solution)/shard_map/ppermute | solution.py:268
  4.1 0.7 copy-start.7
  4.8 26.4 %copy-start = (bf16[1,512,1024]{2,1,0:T(8,128)(2,1)S(1)}, bf16[1,512,1024]{2,1,0:T(8,128)(2,1)}, u32[]{:S(2)}) copy-start(bf16[1,512,1024]{2,1,0:T(8,128)(2,1)} %param.10) | copy-start | bytes 3145732
  4.8 26.4 %copy-start.1 = (bf16[1,512,1024]{2,1,0:T(8,128)(2,1)S(1)}, bf16[1,512,1024]{2,1,0:T(8,128)(2,1)}, u32[]{:S(2)}) copy-start(bf16[1,512,1024]{2,1,0:T(8,128)(2,1)} %param.11) | copy-start | bytes 3145732
  28.7 3.9 %collective-permute-start.2 = (bf16[384,512]{1,0:T(8,128)(2,1)S(1)}, bf16[384,512]{1,0:T(8,128)(2,1)S(1)}, u32[]{:S(2)}, u32[]{:S(2)}) collective-permute-start(bf16[384,512]{1,0:T(8,128)(2,1)S(1)} %bitcast.18), channel_id=1, source_target_pairs={{0,1},{1,0},{2,3},{3,2},{4,5},{5,4},{6,7},{7,6},{8,9},{9,8},{10,11... | collective-permute-start | bytes 1179656 | tf_op jit(solution)/shard_map/ppermute | solution.py:268
  33.2 16.2 %copy-start.4 = (f32[1,128]{1,0:T(1,128)S(1)}, f32[1,128]{1,0:T(1,128)}, u32[]{:S(2)}) copy-start(f32[1,128]{1,0:T(1,128)} %gain_ref.6) | copy-start | bytes 1540
  33.2 18.4 %copy-start.5 = (bf16[1,512,512]{2,1,0:T(8,128)(2,1)S(1)}, bf16[1,512,512]{2,1,0:T(8,128)(2,1)}, u32[]{:S(2)}) copy-start(bf16[1,512,512]{2,1,0:T(8,128)(2,1)} %param.9) | copy-start | bytes 1572868
  33.2 18.4 %copy-start.8 = (f32[1,128]{1,0:T(1,128)S(1)}, f32[1,128]{1,0:T(1,128)}, u32[]{:S(2)}) copy-start(f32[1,128]{1,0:T(1,128)} %gain_ref.7) | copy-start | bytes 1540
  49.6 2.9 %copy-start.2 = (bf16[1,512,512]{2,1,0:T(8,128)(2,1)S(1)}, bf16[1,512,512]{2,1,0:T(8,128)(2,1)}, u32[]{:S(2)}) copy-start(bf16[1,512,512]{2,1,0:T(8,128)(2,1)} %param.15) | copy-start | bytes 1572868
  49.6 2.9 %copy-start.3 = (s32[512]{0:T(512)S(1)}, s32[512]{0:T(512)}, u32[]{:S(2)}) copy-start(s32[512]{0:T(512)} %param.14) | copy-start | bytes 6148
  49.7 2.9 %collective-permute-start.3 = (bf16[384,128]{1,0:T(8,128)(2,1)S(1)}, bf16[384,128]{1,0:T(8,128)(2,1)S(1)}, u32[]{:S(2)}, u32[]{:S(2)}) collective-permute-start(bf16[384,128]{1,0:T(8,128)(2,1)S(1)} %get-tuple-element.58.mine_ref), channel_id=1, source_target_pairs={{0,1},{1,0},{2,3},{3,2},{4,5},{5,4},{6,7},{7,6},{8,9},{9,8},{10,11... | collective-permute-start | bytes 294920 | tf_op jit(solution)/shard_map/ppermute | solution.py:268
  55.3 1.7 %collective-permute-start.4 = (bf16[384,128]{1,0:T(8,128)(2,1)S(1)}, bf16[384,128]{1,0:T(8,128)(2,1)S(1)}, u32[]{:S(2)}, u32[]{:S(2)}) collective-permute-start(bf16[384,128]{1,0:T(8,128)(2,1)S(1)} %get-tuple-element.66), channel_id=1, source_target_pairs={{0,1},{1,0},{2,3},{3,2},{4,5},{5,4},{6,7},{7,6},{8,9},{9,8},{10,11... | collective-permute-start | bytes 294920 | tf_op jit(solution)/shard_map/ppermute | solution.py:268
  73.0 3.1 %collective-permute-start.5 = (bf16[384,512]{1,0:T(8,128)(2,1)S(1)}, bf16[384,512]{1,0:T(8,128)(2,1)S(1)}, u32[]{:S(2)}, u32[]{:S(2)}) collective-permute-start(bf16[384,512]{1,0:T(8,128)(2,1)S(1)} %shard_map.127), channel_id=1, source_target_pairs={{0,1},{1,0},{2,3},{3,2},{4,5},{5,4},{6,7},{7,6},{8,9},{9,8},{10,11... | collective-permute-start | bytes 1179656 | tf_op jit(solution)/shard_map/ppermute | solution.py:268
  75.3 0.8 copy-start.9
  76.1 4.5 %copy-start.6 = (bf16[1,512,512]{2,1,0:T(8,128)(2,1)S(1)}, bf16[1,512,512]{2,1,0:T(8,128)(2,1)}, u32[]{:S(2)}) copy-start(bf16[1,512,512]{2,1,0:T(8,128)(2,1)} %param.9) | copy-start | bytes 1572868
  76.9 6.3 %collective-permute-start.6 = (bf16[8,384,128]{2,1,0:T(8,128)(2,1)S(1)}, bf16[8,384,128]{2,1,0:T(8,128)(2,1)S(1)}, u32[]{:S(2)}, u32[]{:S(2)}) collective-permute-start(bf16[8,384,128]{2,1,0:T(8,128)(2,1)S(1)} %all_to_all.22.grads_ref.mine_ref), channel_id=1, source_target_pairs={{0,1},{1,0},{2,3},{3,2},{4,5},{5,4},{6,7},{7,6},{8,9},{9,8},{10,11... | collective-permute-start | bytes 2359304 | tf_op jit(solution)/shard_map/ppermute | solution.py:268
  77.0 18.6 %all-to-all-start.3 = ((bf16[16,24,512]{2,1,0:T(8,128)(2,1)}), bf16[16,24,512]{2,1,0:T(8,128)(2,1)S(1)}, u32[]{:S(2)}, u32[]{:S(2)}) async-start(bf16[16,24,512]{2,1,0:T(8,128)(2,1)} %bitcast.8), calls=%async_computation.3 | async-start | bytes 786432 | tf_op jit(solution)/shard_map/all_to_all | solution.py:354
  80.6 1.0 %copy-start.10 = (bf16[4,128,512]{2,1,0:T(8,128)(2,1)S(1)}, bf16[4,128,512]{2,1,0:T(8,128)(2,1)}, u32[]{:S(2)}) copy-start(bf16[4,128,512]{2,1,0:T(8,128)(2,1)} %copy-done.9) | copy-start | bytes 1572868

commit v6 on v5

--- a/solution.py
+++ b/solution.py
@@ -7,7 +7,7 @@
 
 TILE_ROWS = 96
 CORES = 2
-ADD_STEPS = 4
+SIDE = 4
 LOG2_E = 1.4426950408889634
 epsilon = 1e-05
 
@@ -17,7 +17,6 @@
 BOTH_LAST = (((1,), (1,)), ((), ()))
 
 ANY = pl.BlockSpec(memory_space=pl.ANY)
-HBM = pl.BlockSpec(memory_space=pltpu.HBM)
 VMEM = pl.BlockSpec(memory_space=pltpu.VMEM)
 SMEM = pl.BlockSpec(memory_space=pltpu.SMEM)
 PARAMS = pltpu.CompilerParams(vmem_limit_bytes=16 * 1024 * 1024)
@@ -39,13 +38,30 @@
     )
 
 
+def wrap(i):
+    return lax.rem(i + SIDE, SIDE)
+
+
 def by_core(core, zero, one):
     return jnp.where(core == 0, zero, one)
 
 
-def copies_kernel(rows_ref, out_ref):
-    for i in range(out_ref.shape[0]):
-        out_ref[i] = rows_ref[...]
+def copy_kernel(rows_ref, out_ref):
+    out_ref[...] = rows_ref[...]
+
+
+def gather_z_kernel(z_ref, *refs):
+    *blocks, out_ref = refs
+    for k, block in enumerate(blocks):
+        out_ref[wrap(z_ref[0] - k)] = block[...]
+
+
+def gather_y_kernel(y_ref, *refs):
+    *blocks, out_ref = refs
+    for k, block in enumerate(blocks):
+        y = wrap(y_ref[0] - k)
+        for z in range(SIDE):
+            out_ref[y * SIDE + z] = block[z]
 
 
 def project_kernel(core_ref, rows_ref, key_ref, value_ref, *refs):
@@ -139,27 +155,21 @@
     )
 
 
-def normed_grad_kernel(core_ref, mine_ref, other_ref, score_grad_ref, out_ref):
+def query_grad_kernel(
+    core_ref, mine_ref, other_ref, query_ref, gain_ref, score_grad_ref, query_grad_ref, held, sems
+):
     keys = by_core(core_ref[0], mine_ref[...], other_ref[...])
     keys_t = keys.astype(f32).T.astype(bf16)
-    for h in range(score_grad_ref.shape[0]):
-        out_ref[h] = (dot(keys_t, score_grad_ref[h]) * keys.shape[1] ** (-0.5)).astype(bf16)
-
-
-def query_grad_kernel(
-    query_ref, gain_ref, normed_grad_ref, query_grad_ref, held, sems, query_held, query_sem
-):
-    copy = pltpu.make_async_copy(query_ref, query_held, query_sem)
-    copy.start()
+    head = keys.shape[1]
     gain = gain_ref[...]
-    copy.wait()
 
     def fill(h, cols):
-        query = query_held[:, cols].astype(f32)
+        query = query_ref[:, cols].astype(f32)
         _, inverse = head_norm(query, gain)
-        return head_norm_back(query, inverse, gain, normed_grad_ref[h].astype(f32).T)
-
-    send_heads(held, query_grad_ref, sems, gain.shape[1], fill)
+        normed_grad = dot(keys_t, score_grad_ref[h]).T * head ** (-0.5)
+        return head_norm_back(query, inverse, gain, normed_grad)
+
+    send_heads(held, query_grad_ref, sems, head, fill)
 
 
 def kv_grad_kernel(core_ref, keep_ref, received_ref, raw_ref, gain_ref, out_ref):
@@ -191,52 +201,50 @@
             out_ref[...] = image_product(grads_ref, weight_ref, slice(None)).astype(out_ref.dtype)
 
 
-def add_kernel(own_ref, received_ref, out_ref, held, sems):
-    copies = []
-    step = held.shape[0] // ADD_STEPS
-    for i in range(ADD_STEPS):
-        now = slice(i * step, (i + 1) * step)
-        held[now] = (own_ref[now] + received_ref[now].astype(f32)).astype(bf16)
-        copies.append(pltpu.make_async_copy(held.at[now], out_ref.at[now], sems.at[i]))
-        copies[-1].start()
-    for copy in copies:
-        copy.wait()
-
-
-def weight_grad_kernel(
-    core_ref, rows_ref, mine_ref, other_ref, key_ref, value_ref, other_held, sems
-):
+def scatter_y_kernel(y_ref, own_ref, received_ref, keep_ref, *send_refs):
+    for k, out_ref in enumerate((keep_ref, *send_refs)):
+        y = wrap(y_ref[0] + k)
+        for z in range(SIDE):
+            i = y * SIDE + z
+            out_ref[z] = (own_ref[i] + received_ref[i].astype(f32)).astype(out_ref.dtype)
+
+
+def scatter_z_kernel(z_ref, keep_ref, *refs):
+    received, outs, total_ref = refs[: SIDE - 1], refs[SIDE - 1 : -1], refs[-1]
+    for z in range(SIDE):
+        total = keep_ref[z]
+        for block in received:
+            total = total + block[z].astype(f32)
+        total_ref[z] = total
+    for k, out_ref in enumerate(outs):
+        out_ref[...] = total_ref[wrap(z_ref[0] + k)].astype(out_ref.dtype)
+
+
+def sum_kernel(keep_ref, *refs):
+    *received, out_ref = refs
+    total = keep_ref[...]
+    for block in received:
+        total = total + block[...].astype(f32)
+    out_ref[...] = total
+
+
+def weight_grad_kernel(core_ref, rows_ref, mine_ref, other_ref, key_ref, value_ref):
     kv_heads, _, head = mine_ref.shape
-    copies = [
-        pltpu.make_async_copy(other_ref.at[h], other_held.at[h], sems.at[h])
-        for h in range(kv_heads)
-    ]
-    for copy in copies:
-        copy.start()
     core = core_ref[0]
     rows_t = rows_ref[...].astype(f32).T.astype(bf16)
     for low in range(0, kv_heads, 2):
         cols = slice(low * head, (low + 2) * head)
         mine = jnp.concatenate([mine_ref[low], mine_ref[low + 1]], 1)
-        copies[low].wait()
-        copies[low + 1].wait()
-        other = jnp.concatenate([other_held[low], other_held[low + 1]], 1)
+        other = jnp.concatenate([other_ref[low], other_ref[low + 1]], 1)
         key_ref[:, cols] = dot(rows_t, by_core(core, mine, other)).astype(bf16)
         value_ref[:, cols] = dot(rows_t, by_core(core, other, mine)).astype(bf16)
 
 
-def sum_kernel(parts_ref, out_ref):
-    total = parts_ref[0].astype(f32)
-    for i in range(1, parts_ref.shape[0]):
-        total = total + parts_ref[i].astype(f32)
-    out_ref[...] = total
-
-
-def call(kernel, outs, *args, scalar=False, cost=None, scratch=(), to_hbm=(), from_hbm=()):
+def call(kernel, outs, *args, scalar=False, cost=None, scratch=(), to_hbm=()):
     many = len(outs) > 1
     shapes = tuple(jax.ShapeDtypeStruct(shape, kind) for shape, kind in outs)
     places = tuple(ANY if i in to_hbm else VMEM for i in range(len(outs)))
-    takes = [HBM if i in from_hbm else VMEM for i in range(len(args))]
+    takes = [VMEM] * len(args)
     if scalar:
         takes[0] = SMEM
     return pl.pallas_call(
@@ -281,12 +289,32 @@
 
     key_other = other_core(key_weight[0])
     value_other = other_core(value_weight[0])
-    image_rows, core = fence(image_rows, core)
-    copies = call(
-        copies_kernel, [((sections, own_rows, features), bf16)], image_rows,
+    block = (own_rows, features)
+    column = (SIDE, *block)
+    section = lax.axis_index("section").astype(jnp.int32)
+    my_y, my_z = (section // SIDE).reshape(1), (section % SIDE).reshape(1)
+
+    def along_z(x, k):
+        to = [(i, i // SIDE * SIDE + (i + k) % SIDE) for i in range(sections)]
+        return lax.ppermute(x, "section", to)
+
+    def along_y(x, k):
+        return lax.ppermute(x, "section", [(i, (i + k * SIDE) % sections) for i in range(sections)])
+
+    image_rows, core, my_y, my_z = fence(image_rows, core, my_y, my_z)
+    others = [along_z(image_rows, k) for k in range(1, SIDE)]
+    own = call(
+        copy_kernel, [(block, bf16)], image_rows,
+        cost=pl.CostEstimate(flops=2**30, bytes_accessed=2**20, transcendentals=0),
+    )
+    rows_z = call(
+        gather_z_kernel, [(column, bf16)], my_z, own, *others, scalar=True,
         cost=pl.CostEstimate(flops=2**34, bytes_accessed=2**25, transcendentals=0),
     )
-    blocks = lax.all_to_all(copies, "section", 0, 0)
+    others = [along_y(rows_z, k) for k in range(1, SIDE)]
+    blocks = call(
+        gather_y_kernel, [((sections, *block), bf16)], my_y, rows_z, *others, scalar=True
+    )
     blocks, key_weight, value_weight, key_other, value_other, queries, context_grad = fence(
         blocks, key_weight[0], value_weight[0], key_other, value_other, queries[0], context_grad[0]
     )
@@ -339,41 +367,41 @@
         image_kernel, [((rows_total, features), f32)],
         core, grads, key_weight, value_weight, scalar=True,
     )
-    normed_grad = call(
-        normed_grad_kernel, [((width // head, head, text), bf16)],
-        core, kv_mine, kv_other, score_grad, scalar=True,
-        cost=pl.CostEstimate(flops=2**30, bytes_accessed=2**20, transcendentals=0),
-    )
-    image_own, received, normed_grad = fence(image_own, received, normed_grad)
-    image_part = call(
-        add_kernel, [((rows_total, features), bf16)], image_own, received, to_hbm=(0,),
-        scratch=[pltpu.VMEM((rows_total, features), bf16), pltpu.SemaphoreType.DMA((ADD_STEPS,))],
-    )
-    image_part, rows, grads, normed_grad = fence(image_part, rows, grads, normed_grad)
+    image_own, received = fence(image_own, received)
+    keep, *sends = call(
+        scatter_y_kernel, [(column, f32)] + [(column, bf16)] * (SIDE - 1),
+        my_y, image_own.reshape(sections, *block), received.reshape(sections, *block),
+        scalar=True,
+    )
+    keep, sends, rows, grads, score_grad = fence(keep, sends, rows, grads, score_grad)
+    received = [along_y(x, k + 1) for k, x in enumerate(sends)]
     grads_other = other_core(grads)
-    image_parts = lax.all_to_all(
-        image_part.reshape(sections, own_rows, features), "section", 0, 0
-    )
     key_weight_grad, value_weight_grad = call(
         weight_grad_kernel, [((features, kv_width), bf16)] * 2,
-        core, rows, grads, grads_other, scalar=True, from_hbm=(3,),
-        scratch=[pltpu.VMEM(pieces, bf16), pltpu.SemaphoreType.DMA((kv_heads,))],
+        core, rows, grads, grads_other, scalar=True,
         cost=pl.CostEstimate(
             flops=2 * features * 2 * kv_width * rows_total,
             bytes_accessed=4 * features * 2 * kv_width,
             transcendentals=0,
         ),
     )
+    received, key_weight_grad, value_weight_grad, score_grad = fence(
+        received, key_weight_grad, value_weight_grad, score_grad
+    )
+    keep, *sends = call(
+        scatter_z_kernel, [(block, f32)] + [(block, bf16)] * (SIDE - 1),
+        my_z, keep, *received, scalar=True, scratch=[pltpu.VMEM(column, f32)],
+    )
+    keep, sends, score_grad = fence(keep, sends, score_grad)
+    received = [along_z(x, k + 1) for k, x in enumerate(sends)]
     query_grad = call(
         query_grad_kernel, [((text, width), bf16)],
-        queries, query_gain, normed_grad, to_hbm=(0,), from_hbm=(0,),
-        scratch=out_scratch + [pltpu.VMEM((text, width), bf16), pltpu.SemaphoreType.DMA],
+        core, kv_mine, kv_other, queries, query_gain, score_grad,
+        scalar=True, to_hbm=(0,), scratch=out_scratch,
         cost=pl.CostEstimate(flops=2**30, bytes_accessed=2**20, transcendentals=0),
     )
-    image_parts, key_weight_grad, value_weight_grad, query_grad = fence(
-        image_parts, key_weight_grad, value_weight_grad, query_grad
-    )
-    image_grad = call(sum_kernel, [((own_rows, features), f32)], image_parts)
+    received, query_grad = fence(received, query_grad)
+    image_grad = call(sum_kernel, [(block, f32)], keep, *received)
     return (
         context[None], query_grad[None], key_weight_grad[None], value_weight_grad[None], image_grad
     )

time: 96.7 us -> 90.4 us (0.935)
  blocking collectives: 55.2 us -> 31.6 us
  starting transfers between devices: 13.2 us -> 33.6 us
  Pallas kernels: 15.1 us -> 12.5 us
  local copies, waits for them, and re-layouts: 2.6 us -> 0.78 us
  waiting for transfers between devices: 9.41 us -> 10.8 us
    ppermute x0 -> x12, starting transfers between devices: none -> 24.3 us  [the longest x6 17.7 us: along_z(): return lax.ppermute(x, 'section', to)]
    all_to_all x1 -> x0, blocking collectives: 23.8 us -> none  [shards(): blocks = lax.all_to_all(copies, 'section', 0, 0)]
    ppermute x0 -> x12, waiting for transfers between devices: none -> 8.75 us  [the longest x6 7.46 us: along_y(): lax.ppermute(x, 'section', [(i, (i + k * SIDE) % sections) for i in range...]
    all_to_all x1 -> x0, waiting for transfers between devices: 8.08 us -> none  [shards(): lax.all_to_all(image_part.reshape(sections, own_rows, features), 'section...]
    all_to_all x1 -> x0, starting transfers between devices: 3.55 us -> none  [shards(): lax.all_to_all(image_part.reshape(sections, own_rows, features), 'section...]
    pallas_call x15 -> x17, Pallas kernels: 15.1 us -> 12.5 us  [call(): pl.pallas_call(kernel, out_shape=shapes if many else shapes[0], in_specs=...]
    unnamed x22 -> x16, local copies, waits for them, and re-layouts: 2.6 us -> 0.78 us
  transfers between devices with their start and end apart: 8 -> 19, of which waited for: 3 -> 9; matrix products, arithmetic and copies ran while one was open for 0% -> 0% of each run, Pallas kernels for 10% -> 8%
where the time goes in v6:
time: 90.4 us; the launch traced here: 90.2 us
  starting transfers between devices  33.6 us (37%)
  blocking collectives  31.6 us (35%)
  Pallas kernels  12.5 us (14%)
  waiting for transfers between devices  10.8 us (12%)
    all_to_all x2, blocking collectives, over_chips(): return lax.all_to_all(x, 'tp', 0, 0, axis_index_groups=same_core)  31.6 us
    ppermute x6, starting transfers between devices, along_z(): return lax.ppermute(x, 'section', to)  17.7 us
    pallas_call x17, Pallas kernels, call(): pl.pallas_call(kernel, out_shape=shapes if many else shapes[0], in_specs=...  12.5 us
    ppermute x7, starting transfers between devices, other_core(): return lax.ppermute(x, 'tp', swap)  9.3 us
    ppermute x6, waiting for transfers between devices, along_y(): lax.ppermute(x, 'section', [(i, (i + k * SIDE) % sections) for i in range...  7.46 us
    ppermute x6, starting transfers between devices, along_y(): lax.ppermute(x, 'section', [(i, (i + k * SIDE) % sections) for i in range...  6.62 us
    ppermute x7, waiting for transfers between devices, other_core(): return lax.ppermute(x, 'tp', swap)  2.07 us
  transfers between devices with their start and end apart: 19, of which 9 were waited for; matrix products, arithmetic and copies ran while one was open for 0% of the time, Pallas kernels for 8%

profile of v6, /device:TPU:1, one launch (start us, length us, event | category | flops | bytes accessed | tf_op | source)
XLA Modules:
  0.0 90.2 jit_solution(5369067463566807114)
XLA Ops:
  0.7 6.9 %collective-permute-start.2 = (bf16[24,512]{1,0:T(8,128)(2,1)}, bf16[24,512]{1,0:T(8,128)(2,1)S(1)}, u32[]{:S(2)}, u32[]{:S(2)}) collective-permute-start(bf16[24,512]{1,0:T(8,128)(2,1)} %rows_ref), channel_id=1, source_target_pairs={{0,48},{16,0},{32,16},{48,32},{64,112},{80,64},{96,80},{112,96},{1... | collective-permute-start | bytes 73736 | tf_op jit(solution)/shard_map/ppermute | solution.py:299
  7.6 1.0 %collective-permute-start.1 = (bf16[24,512]{1,0:T(8,128)(2,1)}, bf16[24,512]{1,0:T(8,128)(2,1)S(1)}, u32[]{:S(2)}, u32[]{:S(2)}) collective-permute-start(bf16[24,512]{1,0:T(8,128)(2,1)} %rows_ref), channel_id=1, source_target_pairs={{0,32},{16,48},{32,0},{48,16},{64,96},{80,112},{96,64},{112,80},{1... | collective-permute-start | bytes 73736 | tf_op jit(solution)/shard_map/ppermute | solution.py:299
  8.6 2.3 %collective-permute-start = (bf16[24,512]{1,0:T(8,128)(2,1)}, bf16[24,512]{1,0:T(8,128)(2,1)S(1)}, u32[]{:S(2)}, u32[]{:S(2)}) collective-permute-start(bf16[24,512]{1,0:T(8,128)(2,1)} %rows_ref), channel_id=1, source_target_pairs={{0,16},{16,32},{32,48},{48,0},{64,80},{80,96},{96,112},{112,64},{1... | collective-permute-start | bytes 73736 | tf_op jit(solution)/shard_map/ppermute | solution.py:299
  10.8 1.5 %collective-permute-start.6 = (bf16[512,1024]{1,0:T(8,128)(2,1)}, bf16[512,1024]{1,0:T(8,128)(2,1)S(1)}, u32[]{:S(2)}, u32[]{:S(2)}) collective-permute-start(bf16[512,1024]{1,0:T(8,128)(2,1)} %bitcast.15), channel_id=1, source_target_pairs={{0,1},{1,0},{2,3},{3,2},{4,5},{5,4},{6,7},{7,6},{8,9},{9,8},{10,11... | collective-permute-start | bytes 3145736 | tf_op jit(solution)/shard_map/ppermute | solution.py:276
  13.1 1.3 %collective-permute-done.1.refs_2_ = bf16[24,512]{1,0:T(8,128)(2,1)S(1)} collective-permute-done((bf16[24,512]{1,0:T(8,128)(2,1)}, bf16[24,512]{1,0:T(8,128)(2,1)S(1)}, u32[]{:S(2)}, u32[]{:S(2)}) %collective-permute-start.1) | collective-permute-done | bytes 24608 | tf_op jit(solution)/shard_map/ppermute | solution.py:299
  14.4 2.8 %collective-permute-start.5 = (bf16[4,24,512]{2,1,0:T(8,128)(2,1)S(1)}, bf16[4,24,512]{2,1,0:T(8,128)(2,1)S(1)}, u32[]{:S(2)}, u32[]{:S(2)}) collective-permute-start(bf16[4,24,512]{2,1,0:T(8,128)(2,1)S(1)} %shard_map.120.refs_0_), channel_id=1, source_target_pairs={{0,192},{16,208},{32,224},{48,240},{64,0},{80,16},{96,32},{112,48}... | collective-permute-start | bytes 294920 | tf_op jit(solution)/shard_map/ppermute | solution.py:302
  18.9 3.4 %collective-permute-done.4.refs_2_ = bf16[4,24,512]{2,1,0:T(8,128)(2,1)S(1)} collective-permute-done((bf16[4,24,512]{2,1,0:T(8,128)(2,1)S(1)}, bf16[4,24,512]{2,1,0:T(8,128)(2,1)S(1)}, u32[]{:S(2)}, u32[]{:S(2)}) %collective-permute-start.4) | collective-permute-done | bytes 98336 | tf_op jit(solution)/shard_map/ppermute | solution.py:302
  22.3 0.9 %collective-permute-done.3.refs_1_ = bf16[4,24,512]{2,1,0:T(8,128)(2,1)S(1)} collective-permute-done((bf16[4,24,512]{2,1,0:T(8,128)(2,1)S(1)}, bf16[4,24,512]{2,1,0:T(8,128)(2,1)S(1)}, u32[]{:S(2)}, u32[]{:S(2)}) %collective-permute-start.3) | collective-permute-done | bytes 98336 | tf_op jit(solution)/shard_map/ppermute | solution.py:302
  23.3 3.6 %collective-permute-start.8 = (bf16[384,512]{1,0:T(8,128)(2,1)S(1)}, bf16[384,512]{1,0:T(8,128)(2,1)S(1)}, u32[]{:S(2)}, u32[]{:S(2)}) collective-permute-start(bf16[384,512]{1,0:T(8,128)(2,1)S(1)} %bitcast.22), channel_id=1, source_target_pairs={{0,1},{1,0},{2,3},{3,2},{4,5},{5,4},{6,7},{7,6},{8,9},{9,8},{10,11... | collective-permute-start | bytes 1179656 | tf_op jit(solution)/shard_map/ppermute | solution.py:276
  27.5 0.7 collective-permute-done.8.rows_ref
  28.9 16.4 %all_to_all.10.parts_ref = bf16[8,384,128]{2,1,0:T(8,128)(2,1)S(1)} all-to-all(bf16[8,384,128]{2,1,0:T(8,128)(2,1)S(1)} %shard_map.123), channel_id=1, replica_groups={{0,2,4,6,8,10,12,14},{1,3,5,7,9,11,13,15},{16,18,20,22,24,26,28,30},{17..., dimensions={0} | all-to-all | bytes 1572864 | tf_op jit(solution)/shard_map/all_to_all | solution.py:279
  45.6 1.9 %collective-permute-start.9 = (bf16[384,128]{1,0:T(8,128)(2,1)S(1)}, bf16[384,128]{1,0:T(8,128)(2,1)S(1)}, u32[]{:S(2)}, u32[]{:S(2)}) collective-permute-start(bf16[384,128]{1,0:T(8,128)(2,1)S(1)} %get-tuple-element.83.mine_ref), channel_id=1, source_target_pairs={{0,1},{1,0},{2,3},{3,2},{4,5},{5,4},{6,7},{7,6},{8,9},{9,8},{10,11... | collective-permute-start | bytes 294920 | tf_op jit(solution)/shard_map/ppermute | solution.py:276
  48.4 2.7 %shard_map.126 = (bf16[4,384,512]{2,1,0:T(8,128)(2,1)S(1)}, bf16[4,384,512]{2,1,0:T(8,128)(2,1)S(1)}, bf16[384,128]{1,0:T(8,128)(2,1)S(1)}, f32[384,128]{1,0:T(8,128)S(1)}) custom-call(s32[1]{0:T(128)} %bitcast.core_ref, bf16[384,128]{1,0:T(8,128)(2,1)S(1)} %get-tuple-element.83.mine_ref, bf16[384,128]{1,0:T(8,128)(2,1)S(1)} %collective-permute-done.9.other_ref, ...), custom_call_target="tpu_custom_call" | custom-call | tf_op jit(solution)/shard_map/pallas_call | solution.py:250
  51.8 1.3 %shard_map.127 = bf16[512,512]{1,0:T(8,128)(2,1)} custom-call(s32[1]{0:T(128)} %bitcast.core_ref, bf16[384,128]{1,0:T(8,128)(2,1)S(1)} %get-tuple-element.83.mine_ref, bf16[384,128]{1,0:T(8,128)(2,1)S(1)} %collective-permute-done.9.other_ref, bf16[4,384,512]{2,1,0:T(8,128)(2,1)S(1)} %get-tuple-element.92.probs_ref), custom_call_target="tpu_custom_call" | custom-call | flops 1073741824 | bytes 1048576 | tf_op jit(solution)/shard_map/pallas_call | solution.py:250
  53.3 15.2 %all_to_all.11.grads_ref.mine_ref = bf16[8,384,128]{2,1,0:T(8,128)(2,1)S(1)} all-to-all(bf16[8,384,128]{2,1,0:T(8,128)(2,1)S(1)} %shard_map.128), channel_id=1, replica_groups={{0,2,4,6,8,10,12,14},{1,3,5,7,9,11,13,15},{16,18,20,22,24,26,28,30},{17..., dimensions={0} | all-to-all | bytes 1572864 | tf_op jit(solution)/shard_map/all_to_all | solution.py:279
  69.1 1.2 %collective-permute-start.11 = (bf16[384,512]{1,0:T(8,128)(2,1)S(1)}, bf16[384,512]{1,0:T(8,128)(2,1)S(1)}, u32[]{:S(2)}, u32[]{:S(2)}) collective-permute-start(bf16[384,512]{1,0:T(8,128)(2,1)S(1)} %shard_map.129), channel_id=1, source_target_pairs={{0,1},{1,0},{2,3},{3,2},{4,5},{5,4},{6,7},{7,6},{8,9},{9,8},{10,11... | collective-permute-start | bytes 1179656 | tf_op jit(solution)/shard_map/ppermute | solution.py:276
  70.9 0.7 collective-permute-done.11
  72.2 1.4 %collective-permute-start.13 = (bf16[4,24,512]{2,1,0:T(8,128)(2,1)S(1)}, bf16[4,24,512]{2,1,0:T(8,128)(2,1)S(1)}, u32[]{:S(2)}, u32[]{:S(2)}) collective-permute-start(bf16[4,24,512]{2,1,0:T(8,128)(2,1)S(1)} %get-tuple-element.109), channel_id=1, source_target_pairs={{0,128},{16,144},{32,160},{48,176},{64,192},{80,208},{96,224},{112... | collective-permute-start | bytes 294920 | tf_op jit(solution)/shard_map/ppermute | solution.py:302
  73.6 1.3 %collective-permute-start.14 = (bf16[4,24,512]{2,1,0:T(8,128)(2,1)S(1)}, bf16[4,24,512]{2,1,0:T(8,128)(2,1)S(1)}, u32[]{:S(2)}, u32[]{:S(2)}) collective-permute-start(bf16[4,24,512]{2,1,0:T(8,128)(2,1)S(1)} %get-tuple-element.110), channel_id=1, source_target_pairs={{0,192},{16,208},{32,224},{48,240},{64,0},{80,16},{96,32},{112,48}... | collective-permute-start | bytes 294920 | tf_op jit(solution)/shard_map/ppermute | solution.py:302
  74.9 2.6 %shard_map.132 = (bf16[512,1024]{1,0:T(8,128)(2,1)}, bf16[512,1024]{1,0:T(8,128)(2,1)}) custom-call(s32[1]{0:T(128)} %bitcast.core_ref, bf16[384,512]{1,0:T(8,128)(2,1)S(1)} %bitcast.24, bf16[8,384,128]{2,1,0:T(8,128)(2,1)S(1)} %all_to_all.11.grads_ref.mine_ref, bf16[8,384,128]{2,1,0:T(8,128)(2,1)S(1)} %collective-permute-done.15.other_ref), custom_call_target="tpu_custom_call" | custom-call | flops 805306368 | bytes 4194304 | tf_op jit(solution)/shard_map/pallas_call | solution.py:250
  77.5 2.3 %collective-permute-done.12.refs_0_ = bf16[4,24,512]{2,1,0:T(8,128)(2,1)S(1)} collective-permute-done((bf16[4,24,512]{2,1,0:T(8,128)(2,1)S(1)}, bf16[4,24,512]{2,1,0:T(8,128)(2,1)S(1)}, u32[]{:S(2)}, u32[]{:S(2)}) %collective-permute-start.12) | collective-permute-done | bytes 98336 | tf_op jit(solution)/shard_map/ppermute | solution.py:302
  80.7 3.4 %collective-permute-start.17 = (bf16[24,512]{1,0:T(8,128)(2,1)S(1)}, bf16[24,512]{1,0:T(8,128)(2,1)S(1)}, u32[]{:S(2)}, u32[]{:S(2)}) collective-permute-start(bf16[24,512]{1,0:T(8,128)(2,1)S(1)} %get-tuple-element.125), channel_id=1, source_target_pairs={{0,32},{16,48},{32,0},{48,16},{64,96},{80,112},{96,64},{112,80},{1... | collective-permute-start | bytes 73736 | tf_op jit(solution)/shard_map/ppermute | solution.py:299
  84.1 3.5 %collective-permute-start.18 = (bf16[24,512]{1,0:T(8,128)(2,1)S(1)}, bf16[24,512]{1,0:T(8,128)(2,1)S(1)}, u32[]{:S(2)}, u32[]{:S(2)}) collective-permute-start(bf16[24,512]{1,0:T(8,128)(2,1)S(1)} %get-tuple-element.126), channel_id=1, source_target_pairs={{0,48},{16,0},{32,16},{48,32},{64,112},{80,64},{96,80},{112,96},{1... | collective-permute-start | bytes 73736 | tf_op jit(solution)/shard_map/ppermute | solution.py:299
  87.6 1.9 %shard_map.134 = bf16[512,512]{1,0:T(8,128)(2,1)} custom-call(s32[1]{0:T(128)} %bitcast.core_ref, bf16[384,128]{1,0:T(8,128)(2,1)S(1)} %get-tuple-element.83.mine_ref, bf16[384,128]{1,0:T(8,128)(2,1)S(1)} %collective-permute-done.9.other_ref, bf16[512,512]{1,0:T(8,128)(2,1)S(1)} %bitcast.29, f32[1,128]{1,0:T(1,128)S(1)} %copy-done.7, ...), custom_call_target="tpu_custom_call" | custom-call | flops 1073741824 | bytes 1048576 | tf_op jit(solution)/shard_map/pallas_call | solution.py:250
  (49 shorter events, 8.8 us)
Async XLA Ops:
  0.7 12.4 %collective-permute-start.2 = (bf16[24,512]{1,0:T(8,128)(2,1)}, bf16[24,512]{1,0:T(8,128)(2,1)S(1)}, u32[]{:S(2)}, u32[]{:S(2)}) collective-permute-start(bf16[24,512]{1,0:T(8,128)(2,1)} %rows_ref), channel_id=1, source_target_pairs={{0,48},{16,0},{32,16},{48,32},{64,112},{80,64},{96,80},{112,96},{1... | collective-permute-start | bytes 73736 | tf_op jit(solution)/shard_map/ppermute | solution.py:299
  7.6 6.8 %collective-permute-start.1 = (bf16[24,512]{1,0:T(8,128)(2,1)}, bf16[24,512]{1,0:T(8,128)(2,1)S(1)}, u32[]{:S(2)}, u32[]{:S(2)}) collective-permute-start(bf16[24,512]{1,0:T(8,128)(2,1)} %rows_ref), channel_id=1, source_target_pairs={{0,32},{16,48},{32,0},{48,16},{64,96},{80,112},{96,64},{112,80},{1... | collective-permute-start | bytes 73736 | tf_op jit(solution)/shard_map/ppermute | solution.py:299
  8.6 5.8 %collective-permute-start = (bf16[24,512]{1,0:T(8,128)(2,1)}, bf16[24,512]{1,0:T(8,128)(2,1)S(1)}, u32[]{:S(2)}, u32[]{:S(2)}) collective-permute-start(bf16[24,512]{1,0:T(8,128)(2,1)} %rows_ref), channel_id=1, source_target_pairs={{0,16},{16,32},{32,48},{48,0},{64,80},{80,96},{96,112},{112,64},{1... | collective-permute-start | bytes 73736 | tf_op jit(solution)/shard_map/ppermute | solution.py:299
  10.8 12.4 %collective-permute-start.6 = (bf16[512,1024]{1,0:T(8,128)(2,1)}, bf16[512,1024]{1,0:T(8,128)(2,1)S(1)}, u32[]{:S(2)}, u32[]{:S(2)}) collective-permute-start(bf16[512,1024]{1,0:T(8,128)(2,1)} %bitcast.15), channel_id=1, source_target_pairs={{0,1},{1,0},{2,3},{3,2},{4,5},{5,4},{6,7},{7,6},{8,9},{9,8},{10,11... | collective-permute-start | bytes 3145736 | tf_op jit(solution)/shard_map/ppermute | solution.py:276
  12.4 10.9 %collective-permute-start.7 = (bf16[512,1024]{1,0:T(8,128)(2,1)}, bf16[512,1024]{1,0:T(8,128)(2,1)S(1)}, u32[]{:S(2)}, u32[]{:S(2)}) collective-permute-start(bf16[512,1024]{1,0:T(8,128)(2,1)} %bitcast.18), channel_id=1, source_target_pairs={{0,1},{1,0},{2,3},{3,2},{4,5},{5,4},{6,7},{7,6},{8,9},{9,8},{10,11... | collective-permute-start | bytes 3145736 | tf_op jit(solution)/shard_map/ppermute | solution.py:276
  13.1 13.8 %copy-start = (bf16[1,512,1024]{2,1,0:T(8,128)(2,1)S(1)}, bf16[1,512,1024]{2,1,0:T(8,128)(2,1)}, u32[]{:S(2)}) copy-start(bf16[1,512,1024]{2,1,0:T(8,128)(2,1)} %param.10) | copy-start | bytes 3145732
  13.1 13.8 %copy-start.1 = (bf16[1,512,1024]{2,1,0:T(8,128)(2,1)S(1)}, bf16[1,512,1024]{2,1,0:T(8,128)(2,1)}, u32[]{:S(2)}) copy-start(bf16[1,512,1024]{2,1,0:T(8,128)(2,1)} %param.11) | copy-start | bytes 3145732
  14.4 4.5 %collective-permute-start.5 = (bf16[4,24,512]{2,1,0:T(8,128)(2,1)S(1)}, bf16[4,24,512]{2,1,0:T(8,128)(2,1)S(1)}, u32[]{:S(2)}, u32[]{:S(2)}) collective-permute-start(bf16[4,24,512]{2,1,0:T(8,128)(2,1)S(1)} %shard_map.120.refs_0_), channel_id=1, source_target_pairs={{0,192},{16,208},{32,224},{48,240},{64,0},{80,16},{96,32},{112,48}... | collective-permute-start | bytes 294920 | tf_op jit(solution)/shard_map/ppermute | solution.py:302
  17.2 5.1 %collective-permute-start.4 = (bf16[4,24,512]{2,1,0:T(8,128)(2,1)S(1)}, bf16[4,24,512]{2,1,0:T(8,128)(2,1)S(1)}, u32[]{:S(2)}, u32[]{:S(2)}) collective-permute-start(bf16[4,24,512]{2,1,0:T(8,128)(2,1)S(1)} %shard_map.120.refs_0_), channel_id=1, source_target_pairs={{0,128},{16,144},{32,160},{48,176},{64,192},{80,208},{96,224},{112... | collective-permute-start | bytes 294920 | tf_op jit(solution)/shard_map/ppermute | solution.py:302
  17.6 5.7 %collective-permute-start.3 = (bf16[4,24,512]{2,1,0:T(8,128)(2,1)S(1)}, bf16[4,24,512]{2,1,0:T(8,128)(2,1)S(1)}, u32[]{:S(2)}, u32[]{:S(2)}) collective-permute-start(bf16[4,24,512]{2,1,0:T(8,128)(2,1)S(1)} %shard_map.120.refs_0_), channel_id=1, source_target_pairs={{0,64},{16,80},{32,96},{48,112},{64,128},{80,144},{96,160},{112,17... | collective-permute-start | bytes 294920 | tf_op jit(solution)/shard_map/ppermute | solution.py:302
  23.3 5.0 %collective-permute-start.8 = (bf16[384,512]{1,0:T(8,128)(2,1)S(1)}, bf16[384,512]{1,0:T(8,128)(2,1)S(1)}, u32[]{:S(2)}, u32[]{:S(2)}) collective-permute-start(bf16[384,512]{1,0:T(8,128)(2,1)S(1)} %bitcast.22), channel_id=1, source_target_pairs={{0,1},{1,0},{2,3},{3,2},{4,5},{5,4},{6,7},{7,6},{8,9},{9,8},{10,11... | collective-permute-start | bytes 1179656 | tf_op jit(solution)/shard_map/ppermute | solution.py:276
  28.9 16.5 %copy-start.4 = (f32[1,128]{1,0:T(1,128)S(1)}, f32[1,128]{1,0:T(1,128)}, u32[]{:S(2)}) copy-start(f32[1,128]{1,0:T(1,128)} %gain_ref.6) | copy-start | bytes 1540
  28.9 18.6 %copy-start.5 = (bf16[1,512,512]{2,1,0:T(8,128)(2,1)S(1)}, bf16[1,512,512]{2,1,0:T(8,128)(2,1)}, u32[]{:S(2)}) copy-start(bf16[1,512,512]{2,1,0:T(8,128)(2,1)} %param.9) | copy-start | bytes 1572868
  28.9 18.6 %copy-start.7 = (f32[1,128]{1,0:T(1,128)S(1)}, f32[1,128]{1,0:T(1,128)}, u32[]{:S(2)}) copy-start(f32[1,128]{1,0:T(1,128)} %gain_ref.7) | copy-start | bytes 1540
  45.6 2.8 %collective-permute-start.9 = (bf16[384,128]{1,0:T(8,128)(2,1)S(1)}, bf16[384,128]{1,0:T(8,128)(2,1)S(1)}, u32[]{:S(2)}, u32[]{:S(2)}) collective-permute-start(bf16[384,128]{1,0:T(8,128)(2,1)S(1)} %get-tuple-element.83.mine_ref), channel_id=1, source_target_pairs={{0,1},{1,0},{2,3},{3,2},{4,5},{5,4},{6,7},{7,6},{8,9},{9,8},{10,11... | collective-permute-start | bytes 294920 | tf_op jit(solution)/shard_map/ppermute | solution.py:276
  51.2 1.9 %collective-permute-start.10 = (bf16[384,128]{1,0:T(8,128)(2,1)S(1)}, bf16[384,128]{1,0:T(8,128)(2,1)S(1)}, u32[]{:S(2)}, u32[]{:S(2)}) collective-permute-start(bf16[384,128]{1,0:T(8,128)(2,1)S(1)} %get-tuple-element.91), channel_id=1, source_target_pairs={{0,1},{1,0},{2,3},{3,2},{4,5},{5,4},{6,7},{7,6},{8,9},{9,8},{10,11... | collective-permute-start | bytes 294920 | tf_op jit(solution)/shard_map/ppermute | solution.py:276
  69.1 2.5 %collective-permute-start.11 = (bf16[384,512]{1,0:T(8,128)(2,1)S(1)}, bf16[384,512]{1,0:T(8,128)(2,1)S(1)}, u32[]{:S(2)}, u32[]{:S(2)}) collective-permute-start(bf16[384,512]{1,0:T(8,128)(2,1)S(1)} %shard_map.129), channel_id=1, source_target_pairs={{0,1},{1,0},{2,3},{3,2},{4,5},{5,4},{6,7},{7,6},{8,9},{9,8},{10,11... | collective-permute-start | bytes 1179656 | tf_op jit(solution)/shard_map/ppermute | solution.py:276
  71.7 3.2 %collective-permute-start.15 = (bf16[8,384,128]{2,1,0:T(8,128)(2,1)S(1)}, bf16[8,384,128]{2,1,0:T(8,128)(2,1)S(1)}, u32[]{:S(2)}, u32[]{:S(2)}) collective-permute-start(bf16[8,384,128]{2,1,0:T(8,128)(2,1)S(1)} %all_to_all.11.grads_ref.mine_ref), channel_id=1, source_target_pairs={{0,1},{1,0},{2,3},{3,2},{4,5},{5,4},{6,7},{7,6},{8,9},{9,8},{10,11... | collective-permute-start | bytes 2359304 | tf_op jit(solution)/shard_map/ppermute | solution.py:276
  72.2 7.7 %collective-permute-start.12 = (bf16[4,24,512]{2,1,0:T(8,128)(2,1)S(1)}, bf16[4,24,512]{2,1,0:T(8,128)(2,1)S(1)}, u32[]{:S(2)}, u32[]{:S(2)}) collective-permute-start(bf16[4,24,512]{2,1,0:T(8,128)(2,1)S(1)} %get-tuple-element.108), channel_id=1, source_target_pairs={{0,64},{16,80},{32,96},{48,112},{64,128},{80,144},{96,160},{112,17... | collective-permute-start | bytes 294920 | tf_op jit(solution)/shard_map/ppermute | solution.py:302
  72.2 7.7 %collective-permute-start.13 = (bf16[4,24,512]{2,1,0:T(8,128)(2,1)S(1)}, bf16[4,24,512]{2,1,0:T(8,128)(2,1)S(1)}, u32[]{:S(2)}, u32[]{:S(2)}) collective-permute-start(bf16[4,24,512]{2,1,0:T(8,128)(2,1)S(1)} %get-tuple-element.109), channel_id=1, source_target_pairs={{0,128},{16,144},{32,160},{48,176},{64,192},{80,208},{96,224},{112... | collective-permute-start | bytes 294920 | tf_op jit(solution)/shard_map/ppermute | solution.py:302
  73.6 6.4 %collective-permute-start.14 = (bf16[4,24,512]{2,1,0:T(8,128)(2,1)S(1)}, bf16[4,24,512]{2,1,0:T(8,128)(2,1)S(1)}, u32[]{:S(2)}, u32[]{:S(2)}) collective-permute-start(bf16[4,24,512]{2,1,0:T(8,128)(2,1)S(1)} %get-tuple-element.110), channel_id=1, source_target_pairs={{0,192},{16,208},{32,224},{48,240},{64,0},{80,16},{96,32},{112,48}... | collective-permute-start | bytes 294920 | tf_op jit(solution)/shard_map/ppermute | solution.py:302
  80.1 9.4 %collective-permute-start.16 = (bf16[24,512]{1,0:T(8,128)(2,1)S(1)}, bf16[24,512]{1,0:T(8,128)(2,1)S(1)}, u32[]{:S(2)}, u32[]{:S(2)}) collective-permute-start(bf16[24,512]{1,0:T(8,128)(2,1)S(1)} %get-tuple-element.124), channel_id=1, source_target_pairs={{0,16},{16,32},{32,48},{48,0},{64,80},{80,96},{96,112},{112,64},{1... | collective-permute-start | bytes 73736 | tf_op jit(solution)/shard_map/ppermute | solution.py:299
  80.7 8.9 %collective-permute-start.17 = (bf16[24,512]{1,0:T(8,128)(2,1)S(1)}, bf16[24,512]{1,0:T(8,128)(2,1)S(1)}, u32[]{:S(2)}, u32[]{:S(2)}) collective-permute-start(bf16[24,512]{1,0:T(8,128)(2,1)S(1)} %get-tuple-element.125), channel_id=1, source_target_pairs={{0,32},{16,48},{32,0},{48,16},{64,96},{80,112},{96,64},{112,80},{1... | collective-permute-start | bytes 73736 | tf_op jit(solution)/shard_map/ppermute | solution.py:299
  84.1 5.4 %collective-permute-start.18 = (bf16[24,512]{1,0:T(8,128)(2,1)S(1)}, bf16[24,512]{1,0:T(8,128)(2,1)S(1)}, u32[]{:S(2)}, u32[]{:S(2)}) collective-permute-start(bf16[24,512]{1,0:T(8,128)(2,1)S(1)} %get-tuple-element.126), channel_id=1, source_target_pairs={{0,48},{16,0},{32,16},{48,32},{64,112},{80,64},{96,80},{112,96},{1... | collective-permute-start | bytes 73736 | tf_op jit(solution)/shard_map/ppermute | solution.py:299
  (3 other events, 6.5 us)

commit v7 on v6

--- a/solution.py
+++ b/solution.py
@@ -8,6 +8,8 @@
 TILE_ROWS = 96
 CORES = 2
 SIDE = 4
+STEPS = (0, 1, 3, 2)
+LATE_STEPS = (0, 2, 1, 3)
 LOG2_E = 1.4426950408889634
 epsilon = 1e-05
 
@@ -52,13 +54,13 @@
 
 def gather_z_kernel(z_ref, *refs):
     *blocks, out_ref = refs
-    for k, block in enumerate(blocks):
+    for k, block in zip(STEPS, blocks):
         out_ref[wrap(z_ref[0] - k)] = block[...]
 
 
 def gather_y_kernel(y_ref, *refs):
     *blocks, out_ref = refs
-    for k, block in enumerate(blocks):
+    for k, block in zip(STEPS, blocks):
         y = wrap(y_ref[0] - k)
         for z in range(SIDE):
             out_ref[y * SIDE + z] = block[z]
@@ -202,7 +204,7 @@
 
 
 def scatter_y_kernel(y_ref, own_ref, received_ref, keep_ref, *send_refs):
-    for k, out_ref in enumerate((keep_ref, *send_refs)):
+    for k, out_ref in zip(LATE_STEPS, (keep_ref, *send_refs)):
         y = wrap(y_ref[0] + k)
         for z in range(SIDE):
             i = y * SIDE + z
@@ -216,7 +218,7 @@
         for block in received:
             total = total + block[z].astype(f32)
         total_ref[z] = total
-    for k, out_ref in enumerate(outs):
+    for k, out_ref in zip(LATE_STEPS, outs):
         out_ref[...] = total_ref[wrap(z_ref[0] + k)].astype(out_ref.dtype)
 
 
@@ -302,7 +304,7 @@
         return lax.ppermute(x, "section", [(i, (i + k * SIDE) % sections) for i in range(sections)])
 
     image_rows, core, my_y, my_z = fence(image_rows, core, my_y, my_z)
-    others = [along_z(image_rows, k) for k in range(1, SIDE)]
+    others = [along_z(image_rows, k) for k in STEPS[1:]]
     own = call(
         copy_kernel, [(block, bf16)], image_rows,
         cost=pl.CostEstimate(flops=2**30, bytes_accessed=2**20, transcendentals=0),
@@ -311,7 +313,7 @@
         gather_z_kernel, [(column, bf16)], my_z, own, *others, scalar=True,
         cost=pl.CostEstimate(flops=2**34, bytes_accessed=2**25, transcendentals=0),
     )
-    others = [along_y(rows_z, k) for k in range(1, SIDE)]
+    others = [along_y(rows_z, k) for k in STEPS[1:]]
     blocks = call(
         gather_y_kernel, [((sections, *block), bf16)], my_y, rows_z, *others, scalar=True
     )
@@ -374,7 +376,7 @@
         scalar=True,
     )
     keep, sends, rows, grads, score_grad = fence(keep, sends, rows, grads, score_grad)
-    received = [along_y(x, k + 1) for k, x in enumerate(sends)]
+    received = [along_y(x, k) for k, x in zip(LATE_STEPS[1:], sends)]
     grads_other = other_core(grads)
     key_weight_grad, value_weight_grad = call(
         weight_grad_kernel, [((features, kv_width), bf16)] * 2,
@@ -385,22 +387,20 @@
             transcendentals=0,
         ),
     )
-    received, key_weight_grad, value_weight_grad, score_grad = fence(
-        received, key_weight_grad, value_weight_grad, score_grad
-    )
-    keep, *sends = call(
-        scatter_z_kernel, [(block, f32)] + [(block, bf16)] * (SIDE - 1),
-        my_z, keep, *received, scalar=True, scratch=[pltpu.VMEM(column, f32)],
-    )
-    keep, sends, score_grad = fence(keep, sends, score_grad)
-    received = [along_z(x, k + 1) for k, x in enumerate(sends)]
     query_grad = call(
         query_grad_kernel, [((text, width), bf16)],
         core, kv_mine, kv_other, queries, query_gain, score_grad,
         scalar=True, to_hbm=(0,), scratch=out_scratch,
         cost=pl.CostEstimate(flops=2**30, bytes_accessed=2**20, transcendentals=0),
     )
-    received, query_grad = fence(received, query_grad)
+    received, key_weight_grad, value_weight_grad, query_grad = fence(
+        received, key_weight_grad, value_weight_grad, query_grad
+    )
+    keep, *sends = call(
+        scatter_z_kernel, [(block, f32)] + [(block, bf16)] * (SIDE - 1),
+        my_z, keep, *received, scalar=True, scratch=[pltpu.VMEM(column, f32)],
+    )
+    received = [along_z(x, k) for k, x in zip(LATE_STEPS[1:], sends)]
     image_grad = call(sum_kernel, [(block, f32)], keep, *received)
     return (
         context[None], query_grad[None], key_weight_grad[None], value_weight_grad[None], image_grad

time: 90.4 us -> 89.9 us (level)
  waiting for transfers between devices: 10.8 us -> 8.94 us
    ppermute x6, waiting for transfers between devices: 7.46 us -> 5.21 us  [along_y(): lax.ppermute(x, 'section', [(i, (i + k * SIDE) % sections) for i in range...]
where the time goes in v7:
time: 89.9 us; the launch traced here: 89.6 us
  starting transfers between devices  34.2 us (38%)
  blocking collectives  32.3 us (36%)
  Pallas kernels  12.5 us (14%)
  waiting for transfers between devices  8.94 us (10%)
    all_to_all x2, blocking collectives, over_chips(): return lax.all_to_all(x, 'tp', 0, 0, axis_index_groups=same_core)  32.3 us
    ppermute x6, starting transfers between devices, along_z(): return lax.ppermute(x, 'section', to)  17.9 us
    pallas_call x17, Pallas kernels, call(): pl.pallas_call(kernel, out_shape=shapes if many else shapes[0], in_specs=...  12.5 us
    ppermute x7, starting transfers between devices, other_core(): return lax.ppermute(x, 'tp', swap)  8.97 us
    ppermute x6, starting transfers between devices, along_y(): lax.ppermute(x, 'section', [(i, (i + k * SIDE) % sections) for i in range...  7.35 us
    ppermute x6, waiting for transfers between devices, along_y(): lax.ppermute(x, 'section', [(i, (i + k * SIDE) % sections) for i in range...  5.21 us
    ppermute x7, waiting for transfers between devices, other_core(): return lax.ppermute(x, 'tp', swap)  2.07 us
  transfers between devices with their start and end apart: 19, of which 9 were waited for; matrix products, arithmetic and copies ran while one was open for 0% of the time, Pallas kernels for 8%

profile of v7, /device:TPU:1, one launch (start us, length us, event | category | flops | bytes accessed | tf_op | source)
XLA Modules:
  0.0 89.6 jit_solution(6809074574317874965)
XLA Ops:
  0.7 7.8 %collective-permute-start.2 = (bf16[24,512]{1,0:T(8,128)(2,1)}, bf16[24,512]{1,0:T(8,128)(2,1)S(1)}, u32[]{:S(2)}, u32[]{:S(2)}) collective-permute-start(bf16[24,512]{1,0:T(8,128)(2,1)} %rows_ref), channel_id=1, source_target_pairs={{0,32},{16,48},{32,0},{48,16},{64,96},{80,112},{96,64},{112,80},{1... | collective-permute-start | bytes 73736 | tf_op jit(solution)/shard_map/ppermute | solution.py:301
  8.5 2.4 %collective-permute-start = (bf16[24,512]{1,0:T(8,128)(2,1)}, bf16[24,512]{1,0:T(8,128)(2,1)S(1)}, u32[]{:S(2)}, u32[]{:S(2)}) collective-permute-start(bf16[24,512]{1,0:T(8,128)(2,1)} %rows_ref), channel_id=1, source_target_pairs={{0,16},{16,32},{32,48},{48,0},{64,80},{80,96},{96,112},{112,64},{1... | collective-permute-start | bytes 73736 | tf_op jit(solution)/shard_map/ppermute | solution.py:301
  10.8 1.5 %collective-permute-start.6 = (bf16[512,1024]{1,0:T(8,128)(2,1)}, bf16[512,1024]{1,0:T(8,128)(2,1)S(1)}, u32[]{:S(2)}, u32[]{:S(2)}) collective-permute-start(bf16[512,1024]{1,0:T(8,128)(2,1)} %bitcast.15), channel_id=1, source_target_pairs={{0,1},{1,0},{2,3},{3,2},{4,5},{5,4},{6,7},{7,6},{8,9},{9,8},{10,11... | collective-permute-start | bytes 3145736 | tf_op jit(solution)/shard_map/ppermute | solution.py:278
  12.4 0.7 copy-done.6
  13.6 3.0 %collective-permute-start.5 = (bf16[4,24,512]{2,1,0:T(8,128)(2,1)S(1)}, bf16[4,24,512]{2,1,0:T(8,128)(2,1)S(1)}, u32[]{:S(2)}, u32[]{:S(2)}) collective-permute-start(bf16[4,24,512]{2,1,0:T(8,128)(2,1)S(1)} %shard_map.120.refs_0_), channel_id=1, source_target_pairs={{0,128},{16,144},{32,160},{48,176},{64,192},{80,208},{96,224},{112... | collective-permute-start | bytes 294920 | tf_op jit(solution)/shard_map/ppermute | solution.py:304
  16.6 0.8 collective-permute-start.4
  17.4 0.7 collective-permute-start.3
  18.6 1.4 %collective-permute-done.4.refs_2_ = bf16[4,24,512]{2,1,0:T(8,128)(2,1)S(1)} collective-permute-done((bf16[4,24,512]{2,1,0:T(8,128)(2,1)S(1)}, bf16[4,24,512]{2,1,0:T(8,128)(2,1)S(1)}, u32[]{:S(2)}, u32[]{:S(2)}) %collective-permute-start.4) | collective-permute-done | bytes 98336 | tf_op jit(solution)/shard_map/ppermute | solution.py:304
  20.1 2.5 %collective-permute-done.3.refs_1_ = bf16[4,24,512]{2,1,0:T(8,128)(2,1)S(1)} collective-permute-done((bf16[4,24,512]{2,1,0:T(8,128)(2,1)S(1)}, bf16[4,24,512]{2,1,0:T(8,128)(2,1)S(1)}, u32[]{:S(2)}, u32[]{:S(2)}) %collective-permute-start.3) | collective-permute-done | bytes 98336 | tf_op jit(solution)/shard_map/ppermute | solution.py:304
  22.7 3.3 %collective-permute-start.8 = (bf16[384,512]{1,0:T(8,128)(2,1)S(1)}, bf16[384,512]{1,0:T(8,128)(2,1)S(1)}, u32[]{:S(2)}, u32[]{:S(2)}) collective-permute-start(bf16[384,512]{1,0:T(8,128)(2,1)S(1)} %bitcast.22), channel_id=1, source_target_pairs={{0,1},{1,0},{2,3},{3,2},{4,5},{5,4},{6,7},{7,6},{8,9},{9,8},{10,11... | collective-permute-start | bytes 1179656 | tf_op jit(solution)/shard_map/ppermute | solution.py:278
  26.5 0.7 collective-permute-done.8.rows_ref
  27.9 17.1 %all_to_all.10.parts_ref = bf16[8,384,128]{2,1,0:T(8,128)(2,1)S(1)} all-to-all(bf16[8,384,128]{2,1,0:T(8,128)(2,1)S(1)} %shard_map.123), channel_id=1, replica_groups={{0,2,4,6,8,10,12,14},{1,3,5,7,9,11,13,15},{16,18,20,22,24,26,28,30},{17..., dimensions={0} | all-to-all | bytes 1572864 | tf_op jit(solution)/shard_map/all_to_all | solution.py:281
  45.3 1.9 %collective-permute-start.9 = (bf16[384,128]{1,0:T(8,128)(2,1)S(1)}, bf16[384,128]{1,0:T(8,128)(2,1)S(1)}, u32[]{:S(2)}, u32[]{:S(2)}) collective-permute-start(bf16[384,128]{1,0:T(8,128)(2,1)S(1)} %get-tuple-element.74.mine_ref), channel_id=1, source_target_pairs={{0,1},{1,0},{2,3},{3,2},{4,5},{5,4},{6,7},{7,6},{8,9},{9,8},{10,11... | collective-permute-start | bytes 294920 | tf_op jit(solution)/shard_map/ppermute | solution.py:278
  48.1 2.7 %shard_map.126 = (bf16[4,384,512]{2,1,0:T(8,128)(2,1)S(1)}, bf16[4,384,512]{2,1,0:T(8,128)(2,1)S(1)}, bf16[384,128]{1,0:T(8,128)(2,1)S(1)}, f32[384,128]{1,0:T(8,128)S(1)}) custom-call(s32[1]{0:T(128)} %bitcast.core_ref, bf16[384,128]{1,0:T(8,128)(2,1)S(1)} %get-tuple-element.74.mine_ref, bf16[384,128]{1,0:T(8,128)(2,1)S(1)} %collective-permute-done.9.other_ref, ...), custom_call_target="tpu_custom_call" | custom-call | tf_op jit(solution)/shard_map/pallas_call | solution.py:252
  51.5 1.3 %shard_map.127 = bf16[512,512]{1,0:T(8,128)(2,1)} custom-call(s32[1]{0:T(128)} %bitcast.core_ref, bf16[384,128]{1,0:T(8,128)(2,1)S(1)} %get-tuple-element.74.mine_ref, bf16[384,128]{1,0:T(8,128)(2,1)S(1)} %collective-permute-done.9.other_ref, bf16[4,384,512]{2,1,0:T(8,128)(2,1)S(1)} %get-tuple-element.83.probs_ref), custom_call_target="tpu_custom_call" | custom-call | flops 1073741824 | bytes 1048576 | tf_op jit(solution)/shard_map/pallas_call | solution.py:252
  53.0 15.2 %all_to_all.11.grads_ref.mine_ref = bf16[8,384,128]{2,1,0:T(8,128)(2,1)S(1)} all-to-all(bf16[8,384,128]{2,1,0:T(8,128)(2,1)S(1)} %shard_map.128), channel_id=1, replica_groups={{0,2,4,6,8,10,12,14},{1,3,5,7,9,11,13,15},{16,18,20,22,24,26,28,30},{17..., dimensions={0} | all-to-all | bytes 1572864 | tf_op jit(solution)/shard_map/all_to_all | solution.py:281
  68.8 1.2 %collective-permute-start.11 = (bf16[384,512]{1,0:T(8,128)(2,1)S(1)}, bf16[384,512]{1,0:T(8,128)(2,1)S(1)}, u32[]{:S(2)}, u32[]{:S(2)}) collective-permute-start(bf16[384,512]{1,0:T(8,128)(2,1)S(1)} %shard_map.129), channel_id=1, source_target_pairs={{0,1},{1,0},{2,3},{3,2},{4,5},{5,4},{6,7},{7,6},{8,9},{9,8},{10,11... | collective-permute-start | bytes 1179656 | tf_op jit(solution)/shard_map/ppermute | solution.py:278
  70.6 0.7 collective-permute-done.11
  72.2 2.5 %collective-permute-start.14 = (bf16[4,24,512]{2,1,0:T(8,128)(2,1)S(1)}, bf16[4,24,512]{2,1,0:T(8,128)(2,1)S(1)}, u32[]{:S(2)}, u32[]{:S(2)}) collective-permute-start(bf16[4,24,512]{2,1,0:T(8,128)(2,1)S(1)} %get-tuple-element.100), channel_id=1, source_target_pairs={{0,192},{16,208},{32,224},{48,240},{64,0},{80,16},{96,32},{112,48}... | collective-permute-start | bytes 294920 | tf_op jit(solution)/shard_map/ppermute | solution.py:304
  74.7 1.9 %shard_map.133 = bf16[512,512]{1,0:T(8,128)(2,1)} custom-call(s32[1]{0:T(128)} %bitcast.core_ref, bf16[384,128]{1,0:T(8,128)(2,1)S(1)} %get-tuple-element.74.mine_ref, bf16[384,128]{1,0:T(8,128)(2,1)S(1)} %collective-permute-done.9.other_ref, bf16[512,512]{1,0:T(8,128)(2,1)S(1)} %bitcast.29, f32[1,128]{1,0:T(1,128)S(1)} %copy-done.7, ...), custom_call_target="tpu_custom_call" | custom-call | flops 1073741824 | bytes 1048576 | tf_op jit(solution)/shard_map/pallas_call | solution.py:252
  76.7 2.6 %shard_map.132 = (bf16[512,1024]{1,0:T(8,128)(2,1)}, bf16[512,1024]{1,0:T(8,128)(2,1)}) custom-call(s32[1]{0:T(128)} %bitcast.core_ref, bf16[384,512]{1,0:T(8,128)(2,1)S(1)} %bitcast.24, bf16[8,384,128]{2,1,0:T(8,128)(2,1)S(1)} %all_to_all.11.grads_ref.mine_ref, bf16[8,384,128]{2,1,0:T(8,128)(2,1)S(1)} %collective-permute-done.15.other_ref), custom_call_target="tpu_custom_call" | custom-call | flops 805306368 | bytes 4194304 | tf_op jit(solution)/shard_map/pallas_call | solution.py:252
  80.0 4.2 %collective-permute-start.16 = (bf16[24,512]{1,0:T(8,128)(2,1)S(1)}, bf16[24,512]{1,0:T(8,128)(2,1)S(1)}, u32[]{:S(2)}, u32[]{:S(2)}) collective-permute-start(bf16[24,512]{1,0:T(8,128)(2,1)S(1)} %get-tuple-element.114), channel_id=1, source_target_pairs={{0,32},{16,48},{32,0},{48,16},{64,96},{80,112},{96,64},{112,80},{1... | collective-permute-start | bytes 73736 | tf_op jit(solution)/shard_map/ppermute | solution.py:301
  84.2 3.6 %collective-permute-start.18 = (bf16[24,512]{1,0:T(8,128)(2,1)S(1)}, bf16[24,512]{1,0:T(8,128)(2,1)S(1)}, u32[]{:S(2)}, u32[]{:S(2)}) collective-permute-start(bf16[24,512]{1,0:T(8,128)(2,1)S(1)} %get-tuple-element.116), channel_id=1, source_target_pairs={{0,48},{16,0},{32,16},{48,32},{64,112},{80,64},{96,80},{112,96},{1... | collective-permute-start | bytes 73736 | tf_op jit(solution)/shard_map/ppermute | solution.py:301
  87.8 1.2 %collective-permute-done.17.refs_1_ = bf16[24,512]{1,0:T(8,128)(2,1)S(1)} collective-permute-done((bf16[24,512]{1,0:T(8,128)(2,1)S(1)}, bf16[24,512]{1,0:T(8,128)(2,1)S(1)}, u32[]{:S(2)}, u32[]{:S(2)}) %collective-permute-start.17) | collective-permute-done | bytes 24608 | tf_op jit(solution)/shard_map/ppermute | solution.py:301
  (49 shorter events, 7.8 us)
Async XLA Ops:
  0.7 12.5 %collective-permute-start.2 = (bf16[24,512]{1,0:T(8,128)(2,1)}, bf16[24,512]{1,0:T(8,128)(2,1)S(1)}, u32[]{:S(2)}, u32[]{:S(2)}) collective-permute-start(bf16[24,512]{1,0:T(8,128)(2,1)} %rows_ref), channel_id=1, source_target_pairs={{0,32},{16,48},{32,0},{48,16},{64,96},{80,112},{96,64},{112,80},{1... | collective-permute-start | bytes 73736 | tf_op jit(solution)/shard_map/ppermute | solution.py:301
  8.5 4.6 %collective-permute-start.1 = (bf16[24,512]{1,0:T(8,128)(2,1)}, bf16[24,512]{1,0:T(8,128)(2,1)S(1)}, u32[]{:S(2)}, u32[]{:S(2)}) collective-permute-start(bf16[24,512]{1,0:T(8,128)(2,1)} %rows_ref), channel_id=1, source_target_pairs={{0,48},{16,0},{32,16},{48,32},{64,112},{80,64},{96,80},{112,96},{1... | collective-permute-start | bytes 73736 | tf_op jit(solution)/shard_map/ppermute | solution.py:301
  8.5 5.1 %collective-permute-start = (bf16[24,512]{1,0:T(8,128)(2,1)}, bf16[24,512]{1,0:T(8,128)(2,1)S(1)}, u32[]{:S(2)}, u32[]{:S(2)}) collective-permute-start(bf16[24,512]{1,0:T(8,128)(2,1)} %rows_ref), channel_id=1, source_target_pairs={{0,16},{16,32},{32,48},{48,0},{64,80},{80,96},{96,112},{112,64},{1... | collective-permute-start | bytes 73736 | tf_op jit(solution)/shard_map/ppermute | solution.py:301
  10.8 11.8 %collective-permute-start.6 = (bf16[512,1024]{1,0:T(8,128)(2,1)}, bf16[512,1024]{1,0:T(8,128)(2,1)S(1)}, u32[]{:S(2)}, u32[]{:S(2)}) collective-permute-start(bf16[512,1024]{1,0:T(8,128)(2,1)} %bitcast.15), channel_id=1, source_target_pairs={{0,1},{1,0},{2,3},{3,2},{4,5},{5,4},{6,7},{7,6},{8,9},{9,8},{10,11... | collective-permute-start | bytes 3145736 | tf_op jit(solution)/shard_map/ppermute | solution.py:278
  12.4 10.3 %collective-permute-start.7 = (bf16[512,1024]{1,0:T(8,128)(2,1)}, bf16[512,1024]{1,0:T(8,128)(2,1)S(1)}, u32[]{:S(2)}, u32[]{:S(2)}) collective-permute-start(bf16[512,1024]{1,0:T(8,128)(2,1)} %bitcast.18), channel_id=1, source_target_pairs={{0,1},{1,0},{2,3},{3,2},{4,5},{5,4},{6,7},{7,6},{8,9},{9,8},{10,11... | collective-permute-start | bytes 3145736 | tf_op jit(solution)/shard_map/ppermute | solution.py:278
  13.1 12.8 %copy-start = (bf16[1,512,1024]{2,1,0:T(8,128)(2,1)S(1)}, bf16[1,512,1024]{2,1,0:T(8,128)(2,1)}, u32[]{:S(2)}) copy-start(bf16[1,512,1024]{2,1,0:T(8,128)(2,1)} %param.10) | copy-start | bytes 3145732
  13.1 12.8 %copy-start.1 = (bf16[1,512,1024]{2,1,0:T(8,128)(2,1)S(1)}, bf16[1,512,1024]{2,1,0:T(8,128)(2,1)}, u32[]{:S(2)}) copy-start(bf16[1,512,1024]{2,1,0:T(8,128)(2,1)} %param.11) | copy-start | bytes 3145732
  13.6 5.1 %collective-permute-start.5 = (bf16[4,24,512]{2,1,0:T(8,128)(2,1)S(1)}, bf16[4,24,512]{2,1,0:T(8,128)(2,1)S(1)}, u32[]{:S(2)}, u32[]{:S(2)}) collective-permute-start(bf16[4,24,512]{2,1,0:T(8,128)(2,1)S(1)} %shard_map.120.refs_0_), channel_id=1, source_target_pairs={{0,128},{16,144},{32,160},{48,176},{64,192},{80,208},{96,224},{112... | collective-permute-start | bytes 294920 | tf_op jit(solution)/shard_map/ppermute | solution.py:304
  16.6 3.5 %collective-permute-start.4 = (bf16[4,24,512]{2,1,0:T(8,128)(2,1)S(1)}, bf16[4,24,512]{2,1,0:T(8,128)(2,1)S(1)}, u32[]{:S(2)}, u32[]{:S(2)}) collective-permute-start(bf16[4,24,512]{2,1,0:T(8,128)(2,1)S(1)} %shard_map.120.refs_0_), channel_id=1, source_target_pairs={{0,192},{16,208},{32,224},{48,240},{64,0},{80,16},{96,32},{112,48}... | collective-permute-start | bytes 294920 | tf_op jit(solution)/shard_map/ppermute | solution.py:304
  17.4 5.2 %collective-permute-start.3 = (bf16[4,24,512]{2,1,0:T(8,128)(2,1)S(1)}, bf16[4,24,512]{2,1,0:T(8,128)(2,1)S(1)}, u32[]{:S(2)}, u32[]{:S(2)}) collective-permute-start(bf16[4,24,512]{2,1,0:T(8,128)(2,1)S(1)} %shard_map.120.refs_0_), channel_id=1, source_target_pairs={{0,64},{16,80},{32,96},{48,112},{64,128},{80,144},{96,160},{112,17... | collective-permute-start | bytes 294920 | tf_op jit(solution)/shard_map/ppermute | solution.py:304
  22.7 4.6 %collective-permute-start.8 = (bf16[384,512]{1,0:T(8,128)(2,1)S(1)}, bf16[384,512]{1,0:T(8,128)(2,1)S(1)}, u32[]{:S(2)}, u32[]{:S(2)}) collective-permute-start(bf16[384,512]{1,0:T(8,128)(2,1)S(1)} %bitcast.22), channel_id=1, source_target_pairs={{0,1},{1,0},{2,3},{3,2},{4,5},{5,4},{6,7},{7,6},{8,9},{9,8},{10,11... | collective-permute-start | bytes 1179656 | tf_op jit(solution)/shard_map/ppermute | solution.py:278
  27.9 17.2 %copy-start.4 = (f32[1,128]{1,0:T(1,128)S(1)}, f32[1,128]{1,0:T(1,128)}, u32[]{:S(2)}) copy-start(f32[1,128]{1,0:T(1,128)} %gain_ref.6) | copy-start | bytes 1540
  27.9 19.3 %copy-start.5 = (bf16[1,512,512]{2,1,0:T(8,128)(2,1)S(1)}, bf16[1,512,512]{2,1,0:T(8,128)(2,1)}, u32[]{:S(2)}) copy-start(bf16[1,512,512]{2,1,0:T(8,128)(2,1)} %param.9) | copy-start | bytes 1572868
  27.9 19.3 %copy-start.7 = (f32[1,128]{1,0:T(1,128)S(1)}, f32[1,128]{1,0:T(1,128)}, u32[]{:S(2)}) copy-start(f32[1,128]{1,0:T(1,128)} %gain_ref.7) | copy-start | bytes 1540
  45.3 2.8 %collective-permute-start.9 = (bf16[384,128]{1,0:T(8,128)(2,1)S(1)}, bf16[384,128]{1,0:T(8,128)(2,1)S(1)}, u32[]{:S(2)}, u32[]{:S(2)}) collective-permute-start(bf16[384,128]{1,0:T(8,128)(2,1)S(1)} %get-tuple-element.74.mine_ref), channel_id=1, source_target_pairs={{0,1},{1,0},{2,3},{3,2},{4,5},{5,4},{6,7},{7,6},{8,9},{9,8},{10,11... | collective-permute-start | bytes 294920 | tf_op jit(solution)/shard_map/ppermute | solution.py:278
  50.9 1.9 %collective-permute-start.10 = (bf16[384,128]{1,0:T(8,128)(2,1)S(1)}, bf16[384,128]{1,0:T(8,128)(2,1)S(1)}, u32[]{:S(2)}, u32[]{:S(2)}) collective-permute-start(bf16[384,128]{1,0:T(8,128)(2,1)S(1)} %get-tuple-element.82), channel_id=1, source_target_pairs={{0,1},{1,0},{2,3},{3,2},{4,5},{5,4},{6,7},{7,6},{8,9},{9,8},{10,11... | collective-permute-start | bytes 294920 | tf_op jit(solution)/shard_map/ppermute | solution.py:278
  68.8 2.5 %collective-permute-start.11 = (bf16[384,512]{1,0:T(8,128)(2,1)S(1)}, bf16[384,512]{1,0:T(8,128)(2,1)S(1)}, u32[]{:S(2)}, u32[]{:S(2)}) collective-permute-start(bf16[384,512]{1,0:T(8,128)(2,1)S(1)} %shard_map.129), channel_id=1, source_target_pairs={{0,1},{1,0},{2,3},{3,2},{4,5},{5,4},{6,7},{7,6},{8,9},{9,8},{10,11... | collective-permute-start | bytes 1179656 | tf_op jit(solution)/shard_map/ppermute | solution.py:278
  71.4 5.3 %collective-permute-start.15 = (bf16[8,384,128]{2,1,0:T(8,128)(2,1)S(1)}, bf16[8,384,128]{2,1,0:T(8,128)(2,1)S(1)}, u32[]{:S(2)}, u32[]{:S(2)}) collective-permute-start(bf16[8,384,128]{2,1,0:T(8,128)(2,1)S(1)} %all_to_all.11.grads_ref.mine_ref), channel_id=1, source_target_pairs={{0,1},{1,0},{2,3},{3,2},{4,5},{5,4},{6,7},{7,6},{8,9},{9,8},{10,11... | collective-permute-start | bytes 2359304 | tf_op jit(solution)/shard_map/ppermute | solution.py:278
  71.8 7.5 %collective-permute-start.12 = (bf16[4,24,512]{2,1,0:T(8,128)(2,1)S(1)}, bf16[4,24,512]{2,1,0:T(8,128)(2,1)S(1)}, u32[]{:S(2)}, u32[]{:S(2)}) collective-permute-start(bf16[4,24,512]{2,1,0:T(8,128)(2,1)S(1)} %get-tuple-element.98), channel_id=1, source_target_pairs={{0,128},{16,144},{32,160},{48,176},{64,192},{80,208},{96,224},{112... | collective-permute-start | bytes 294920 | tf_op jit(solution)/shard_map/ppermute | solution.py:304
  72.0 7.9 %collective-permute-start.13 = (bf16[4,24,512]{2,1,0:T(8,128)(2,1)S(1)}, bf16[4,24,512]{2,1,0:T(8,128)(2,1)S(1)}, u32[]{:S(2)}, u32[]{:S(2)}) collective-permute-start(bf16[4,24,512]{2,1,0:T(8,128)(2,1)S(1)} %get-tuple-element.99), channel_id=1, source_target_pairs={{0,64},{16,80},{32,96},{48,112},{64,128},{80,144},{96,160},{112,17... | collective-permute-start | bytes 294920 | tf_op jit(solution)/shard_map/ppermute | solution.py:304
  72.2 7.7 %collective-permute-start.14 = (bf16[4,24,512]{2,1,0:T(8,128)(2,1)S(1)}, bf16[4,24,512]{2,1,0:T(8,128)(2,1)S(1)}, u32[]{:S(2)}, u32[]{:S(2)}) collective-permute-start(bf16[4,24,512]{2,1,0:T(8,128)(2,1)S(1)} %get-tuple-element.100), channel_id=1, source_target_pairs={{0,192},{16,208},{32,224},{48,240},{64,0},{80,16},{96,32},{112,48}... | collective-permute-start | bytes 294920 | tf_op jit(solution)/shard_map/ppermute | solution.py:304
  80.0 7.7 %collective-permute-start.16 = (bf16[24,512]{1,0:T(8,128)(2,1)S(1)}, bf16[24,512]{1,0:T(8,128)(2,1)S(1)}, u32[]{:S(2)}, u32[]{:S(2)}) collective-permute-start(bf16[24,512]{1,0:T(8,128)(2,1)S(1)} %get-tuple-element.114), channel_id=1, source_target_pairs={{0,32},{16,48},{32,0},{48,16},{64,96},{80,112},{96,64},{112,80},{1... | collective-permute-start | bytes 73736 | tf_op jit(solution)/shard_map/ppermute | solution.py:301
  84.2 4.8 %collective-permute-start.17 = (bf16[24,512]{1,0:T(8,128)(2,1)S(1)}, bf16[24,512]{1,0:T(8,128)(2,1)S(1)}, u32[]{:S(2)}, u32[]{:S(2)}) collective-permute-start(bf16[24,512]{1,0:T(8,128)(2,1)S(1)} %get-tuple-element.115), channel_id=1, source_target_pairs={{0,16},{16,32},{32,48},{48,0},{64,80},{80,96},{96,112},{112,64},{1... | collective-permute-start | bytes 73736 | tf_op jit(solution)/shard_map/ppermute | solution.py:301
  84.2 4.8 %collective-permute-start.18 = (bf16[24,512]{1,0:T(8,128)(2,1)S(1)}, bf16[24,512]{1,0:T(8,128)(2,1)S(1)}, u32[]{:S(2)}, u32[]{:S(2)}) collective-permute-start(bf16[24,512]{1,0:T(8,128)(2,1)S(1)} %get-tuple-element.116), channel_id=1, source_target_pairs={{0,48},{16,0},{32,16},{48,32},{64,112},{80,64},{96,80},{112,96},{1... | collective-permute-start | bytes 73736 | tf_op jit(solution)/shard_map/ppermute | solution.py:301
  (3 other events, 6.5 us)

commit v8 on v7

--- a/solution.py
+++ b/solution.py
@@ -112,9 +112,7 @@
     values = by_core(core, other_ref[...], mine_ref[...])
     seen = seen_ref[...]
     empty = jnp.where(seen == 0, 1.0, 0.0)
-    visible = jnp.concatenate(
-        [jnp.broadcast_to(i < seen, (TILE_ROWS, text)) for i in range(rows // TILE_ROWS)], 0
-    )
+    shown = [jnp.where(i < seen, 1.0, 0.0) for i in range(rows // TILE_ROWS)]
     key_grad = jnp.zeros((rows, head), f32)
     value_grad = jnp.zeros((rows, head), f32)
     for h in range(width // head):
@@ -122,7 +120,10 @@
         up = up_ref[:, cols]
         normed = normed_ref[:, cols]
         scores = dot(keys, normed, BOTH_LAST)
-        expo = jnp.where(visible, jnp.exp2(scores * (scale * LOG2_E)), 0.0)
+        expo = jnp.exp2(scores * (scale * LOG2_E))
+        expo = jnp.concatenate(
+            [expo[i * TILE_ROWS : (i + 1) * TILE_ROWS] * row for i, row in enumerate(shown)], 0
+        )
         totals = jnp.sum(expo, 0, keepdims=True) + empty
         probs = expo * (1.0 / totals)
         probs_low = probs.astype(bf16)
@@ -349,12 +350,6 @@
     out_scratch = [
         pltpu.VMEM((text, width), bf16), pltpu.SemaphoreType.DMA((width // head,))
     ]
-    context = call(
-        context_kernel, [((text, width), bf16)], core, kv_mine, kv_other, probs,
-        scalar=True, to_hbm=(0,), scratch=out_scratch,
-        cost=pl.CostEstimate(flops=2**30, bytes_accessed=2**20, transcendentals=0),
-    )
-    received, context = fence(received, context)
     copies = call(
         kv_grad_kernel, [(pieces, bf16)], core, keep, received, raw, key_gain, scalar=True
     )
@@ -375,7 +370,9 @@
         my_y, image_own.reshape(sections, *block), received.reshape(sections, *block),
         scalar=True,
     )
-    keep, sends, rows, grads, score_grad = fence(keep, sends, rows, grads, score_grad)
+    keep, sends, rows, grads, probs, score_grad = fence(
+        keep, sends, rows, grads, probs, score_grad
+    )
     received = [along_y(x, k) for k, x in zip(LATE_STEPS[1:], sends)]
     grads_other = other_core(grads)
     key_weight_grad, value_weight_grad = call(
@@ -387,20 +384,27 @@
             transcendentals=0,
         ),
     )
+    context = call(
+        context_kernel, [((text, width), bf16)], core, kv_mine, kv_other, probs,
+        scalar=True, to_hbm=(0,), scratch=out_scratch,
+        cost=pl.CostEstimate(flops=2**30, bytes_accessed=2**20, transcendentals=0),
+    )
+    received, key_weight_grad, value_weight_grad, context, score_grad = fence(
+        received, key_weight_grad, value_weight_grad, context, score_grad
+    )
+    keep, *sends = call(
+        scatter_z_kernel, [(block, f32)] + [(block, bf16)] * (SIDE - 1),
+        my_z, keep, *received, scalar=True, scratch=[pltpu.VMEM(column, f32)],
+    )
+    keep, sends, score_grad = fence(keep, sends, score_grad)
+    received = [along_z(x, k) for k, x in zip(LATE_STEPS[1:], sends)]
     query_grad = call(
         query_grad_kernel, [((text, width), bf16)],
         core, kv_mine, kv_other, queries, query_gain, score_grad,
         scalar=True, to_hbm=(0,), scratch=out_scratch,
         cost=pl.CostEstimate(flops=2**30, bytes_accessed=2**20, transcendentals=0),
     )
-    received, key_weight_grad, value_weight_grad, query_grad = fence(
-        received, key_weight_grad, value_weight_grad, query_grad
-    )
-    keep, *sends = call(
-        scatter_z_kernel, [(block, f32)] + [(block, bf16)] * (SIDE - 1),
-        my_z, keep, *received, scalar=True, scratch=[pltpu.VMEM(column, f32)],
-    )
-    received = [along_z(x, k) for k, x in zip(LATE_STEPS[1:], sends)]
+    received, query_grad = fence(received, query_grad)
     image_grad = call(sum_kernel, [(block, f32)], keep, *received)
     return (
         context[None], query_grad[None], key_weight_grad[None], value_weight_grad[None], image_grad

time: 89.9 us -> 90.2 us (level)
    ppermute x6, waiting for transfers between devices: 1.66 us -> 0.46 us  [along_z(): return lax.ppermute(x, 'section', to)]
    ppermute x7, waiting for transfers between devices: 2.07 us -> 3.01 us  [other_core(): return lax.ppermute(x, 'tp', swap)]
where the time goes in v8:
time: 90.2 us; the launch traced here: 90 us
  starting transfers between devices  34.1 us (38%)
  blocking collectives  32.4 us (36%)
  Pallas kernels  12.4 us (14%)
  waiting for transfers between devices  9.37 us (10%)
    all_to_all x2, blocking collectives, over_chips(): return lax.all_to_all(x, 'tp', 0, 0, axis_index_groups=same_core)  32.4 us
    ppermute x6, starting transfers between devices, along_z(): return lax.ppermute(x, 'section', to)  17.9 us
    pallas_call x17, Pallas kernels, call(): pl.pallas_call(kernel, out_shape=shapes if many else shapes[0], in_specs=...  12.4 us
    ppermute x7, starting transfers between devices, other_core(): return lax.ppermute(x, 'tp', swap)  8.87 us
    ppermute x6, starting transfers between devices, along_y(): lax.ppermute(x, 'section', [(i, (i + k * SIDE) % sections) for i in range...  7.34 us
    ppermute x6, waiting for transfers between devices, along_y(): lax.ppermute(x, 'section', [(i, (i + k * SIDE) % sections) for i in range...  5.91 us
    ppermute x7, waiting for transfers between devices, other_core(): return lax.ppermute(x, 'tp', swap)  3.01 us
  transfers between devices with their start and end apart: 19, of which 9 were waited for; matrix products, arithmetic and copies ran while one was open for 0% of the time, Pallas kernels for 8%

profile of v8, /device:TPU:1, one launch (start us, length us, event | category | flops | bytes accessed | tf_op | source)
XLA Modules:
  0.0 90.0 jit_solution(8861053767281222107)
XLA Ops:
  0.7 7.8 %collective-permute-start.2 = (bf16[24,512]{1,0:T(8,128)(2,1)}, bf16[24,512]{1,0:T(8,128)(2,1)S(1)}, u32[]{:S(2)}, u32[]{:S(2)}) collective-permute-start(bf16[24,512]{1,0:T(8,128)(2,1)} %rows_ref), channel_id=1, source_target_pairs={{0,32},{16,48},{32,0},{48,16},{64,96},{80,112},{96,64},{112,80},{1... | collective-permute-start | bytes 73736 | tf_op jit(solution)/shard_map/ppermute | solution.py:302
  8.5 2.4 %collective-permute-start = (bf16[24,512]{1,0:T(8,128)(2,1)}, bf16[24,512]{1,0:T(8,128)(2,1)S(1)}, u32[]{:S(2)}, u32[]{:S(2)}) collective-permute-start(bf16[24,512]{1,0:T(8,128)(2,1)} %rows_ref), channel_id=1, source_target_pairs={{0,16},{16,32},{32,48},{48,0},{64,80},{80,96},{96,112},{112,64},{1... | collective-permute-start | bytes 73736 | tf_op jit(solution)/shard_map/ppermute | solution.py:302
  10.8 1.5 %collective-permute-start.6 = (bf16[512,1024]{1,0:T(8,128)(2,1)}, bf16[512,1024]{1,0:T(8,128)(2,1)S(1)}, u32[]{:S(2)}, u32[]{:S(2)}) collective-permute-start(bf16[512,1024]{1,0:T(8,128)(2,1)} %bitcast.15), channel_id=1, source_target_pairs={{0,1},{1,0},{2,3},{3,2},{4,5},{5,4},{6,7},{7,6},{8,9},{9,8},{10,11... | collective-permute-start | bytes 3145736 | tf_op jit(solution)/shard_map/ppermute | solution.py:279
  12.4 0.7 copy-done.6
  13.6 3.0 %collective-permute-start.5 = (bf16[4,24,512]{2,1,0:T(8,128)(2,1)S(1)}, bf16[4,24,512]{2,1,0:T(8,128)(2,1)S(1)}, u32[]{:S(2)}, u32[]{:S(2)}) collective-permute-start(bf16[4,24,512]{2,1,0:T(8,128)(2,1)S(1)} %shard_map.120.refs_0_), channel_id=1, source_target_pairs={{0,128},{16,144},{32,160},{48,176},{64,192},{80,208},{96,224},{112... | collective-permute-start | bytes 294920 | tf_op jit(solution)/shard_map/ppermute | solution.py:305
  16.6 0.8 collective-permute-start.4
  18.6 1.4 %collective-permute-done.4.refs_2_ = bf16[4,24,512]{2,1,0:T(8,128)(2,1)S(1)} collective-permute-done((bf16[4,24,512]{2,1,0:T(8,128)(2,1)S(1)}, bf16[4,24,512]{2,1,0:T(8,128)(2,1)S(1)}, u32[]{:S(2)}, u32[]{:S(2)}) %collective-permute-start.4) | collective-permute-done | bytes 98336 | tf_op jit(solution)/shard_map/ppermute | solution.py:305
  20.1 2.5 %collective-permute-done.3.refs_1_ = bf16[4,24,512]{2,1,0:T(8,128)(2,1)S(1)} collective-permute-done((bf16[4,24,512]{2,1,0:T(8,128)(2,1)S(1)}, bf16[4,24,512]{2,1,0:T(8,128)(2,1)S(1)}, u32[]{:S(2)}, u32[]{:S(2)}) %collective-permute-start.3) | collective-permute-done | bytes 98336 | tf_op jit(solution)/shard_map/ppermute | solution.py:305
  22.7 3.3 %collective-permute-start.8 = (bf16[384,512]{1,0:T(8,128)(2,1)S(1)}, bf16[384,512]{1,0:T(8,128)(2,1)S(1)}, u32[]{:S(2)}, u32[]{:S(2)}) collective-permute-start(bf16[384,512]{1,0:T(8,128)(2,1)S(1)} %bitcast.22), channel_id=1, source_target_pairs={{0,1},{1,0},{2,3},{3,2},{4,5},{5,4},{6,7},{7,6},{8,9},{9,8},{10,11... | collective-permute-start | bytes 1179656 | tf_op jit(solution)/shard_map/ppermute | solution.py:279
  26.5 0.7 collective-permute-done.8.rows_ref
  27.9 17.1 %all_to_all.10.parts_ref = bf16[8,384,128]{2,1,0:T(8,128)(2,1)S(1)} all-to-all(bf16[8,384,128]{2,1,0:T(8,128)(2,1)S(1)} %shard_map.123), channel_id=1, replica_groups={{0,2,4,6,8,10,12,14},{1,3,5,7,9,11,13,15},{16,18,20,22,24,26,28,30},{17..., dimensions={0} | all-to-all | bytes 1572864 | tf_op jit(solution)/shard_map/all_to_all | solution.py:282
  45.3 1.9 %collective-permute-start.9 = (bf16[384,128]{1,0:T(8,128)(2,1)S(1)}, bf16[384,128]{1,0:T(8,128)(2,1)S(1)}, u32[]{:S(2)}, u32[]{:S(2)}) collective-permute-start(bf16[384,128]{1,0:T(8,128)(2,1)S(1)} %get-tuple-element.83.mine_ref), channel_id=1, source_target_pairs={{0,1},{1,0},{2,3},{3,2},{4,5},{5,4},{6,7},{7,6},{8,9},{9,8},{10,11... | collective-permute-start | bytes 294920 | tf_op jit(solution)/shard_map/ppermute | solution.py:279
  48.1 2.7 %shard_map.126 = (bf16[4,384,512]{2,1,0:T(8,128)(2,1)S(1)}, bf16[4,384,512]{2,1,0:T(8,128)(2,1)S(1)}, bf16[384,128]{1,0:T(8,128)(2,1)S(1)}, f32[384,128]{1,0:T(8,128)S(1)}) custom-call(s32[1]{0:T(128)} %bitcast.core_ref, bf16[384,128]{1,0:T(8,128)(2,1)S(1)} %get-tuple-element.83.mine_ref, bf16[384,128]{1,0:T(8,128)(2,1)S(1)} %collective-permute-done.9.other_ref, ...), custom_call_target="tpu_custom_call" | custom-call | tf_op jit(solution)/shard_map/pallas_call | solution.py:253
  51.2 0.9 %collective-permute-done.10.received_ref = bf16[384,128]{1,0:T(8,128)(2,1)S(1)} collective-permute-done((bf16[384,128]{1,0:T(8,128)(2,1)S(1)}, bf16[384,128]{1,0:T(8,128)(2,1)S(1)}, u32[]{:S(2)}, u32[]{:S(2)}) %collective-permute-start.10) | collective-permute-done | bytes 98336 | tf_op jit(solution)/shard_map/ppermute | solution.py:279
  52.4 15.3 %all_to_all.11.grads_ref.mine_ref = bf16[8,384,128]{2,1,0:T(8,128)(2,1)S(1)} all-to-all(bf16[8,384,128]{2,1,0:T(8,128)(2,1)S(1)} %shard_map.127), channel_id=1, replica_groups={{0,2,4,6,8,10,12,14},{1,3,5,7,9,11,13,15},{16,18,20,22,24,26,28,30},{17..., dimensions={0} | all-to-all | bytes 1572864 | tf_op jit(solution)/shard_map/all_to_all | solution.py:282
  68.3 1.3 %collective-permute-start.11 = (bf16[384,512]{1,0:T(8,128)(2,1)S(1)}, bf16[384,512]{1,0:T(8,128)(2,1)S(1)}, u32[]{:S(2)}, u32[]{:S(2)}) collective-permute-start(bf16[384,512]{1,0:T(8,128)(2,1)S(1)} %shard_map.128), channel_id=1, source_target_pairs={{0,1},{1,0},{2,3},{3,2},{4,5},{5,4},{6,7},{7,6},{8,9},{9,8},{10,11... | collective-permute-start | bytes 1179656 | tf_op jit(solution)/shard_map/ppermute | solution.py:279
  70.1 0.7 collective-permute-done.11
  71.8 2.5 %collective-permute-start.14 = (bf16[4,24,512]{2,1,0:T(8,128)(2,1)S(1)}, bf16[4,24,512]{2,1,0:T(8,128)(2,1)S(1)}, u32[]{:S(2)}, u32[]{:S(2)}) collective-permute-start(bf16[4,24,512]{2,1,0:T(8,128)(2,1)S(1)} %get-tuple-element.107), channel_id=1, source_target_pairs={{0,192},{16,208},{32,224},{48,240},{64,0},{80,16},{96,32},{112,48}... | collective-permute-start | bytes 294920 | tf_op jit(solution)/shard_map/ppermute | solution.py:305
  74.3 1.2 %shard_map.132 = bf16[512,512]{1,0:T(8,128)(2,1)} custom-call(s32[1]{0:T(128)} %bitcast.core_ref, bf16[384,128]{1,0:T(8,128)(2,1)S(1)} %get-tuple-element.83.mine_ref, bf16[384,128]{1,0:T(8,128)(2,1)S(1)} %collective-permute-done.9.other_ref, bf16[4,384,512]{2,1,0:T(8,128)(2,1)S(1)} %get-tuple-element.112.probs_ref), custom_call_target="tpu_custom_call" | custom-call | flops 1073741824 | bytes 1048576 | tf_op jit(solution)/shard_map/pallas_call | solution.py:253
  75.6 2.6 %shard_map.131 = (bf16[512,1024]{1,0:T(8,128)(2,1)}, bf16[512,1024]{1,0:T(8,128)(2,1)}) custom-call(s32[1]{0:T(128)} %bitcast.core_ref, bf16[384,512]{1,0:T(8,128)(2,1)S(1)} %bitcast.24, bf16[8,384,128]{2,1,0:T(8,128)(2,1)S(1)} %all_to_all.11.grads_ref.mine_ref, bf16[8,384,128]{2,1,0:T(8,128)(2,1)S(1)} %collective-permute-done.15.other_ref), custom_call_target="tpu_custom_call" | custom-call | flops 805306368 | bytes 4194304 | tf_op jit(solution)/shard_map/pallas_call | solution.py:253
  78.2 1.4 %collective-permute-done.13.refs_1_ = bf16[4,24,512]{2,1,0:T(8,128)(2,1)S(1)} collective-permute-done((bf16[4,24,512]{2,1,0:T(8,128)(2,1)S(1)}, bf16[4,24,512]{2,1,0:T(8,128)(2,1)S(1)}, u32[]{:S(2)}, u32[]{:S(2)}) %collective-permute-start.13) | collective-permute-done | bytes 98336 | tf_op jit(solution)/shard_map/ppermute | solution.py:305
  79.6 4.1 %collective-permute-start.16 = (bf16[24,512]{1,0:T(8,128)(2,1)S(1)}, bf16[24,512]{1,0:T(8,128)(2,1)S(1)}, u32[]{:S(2)}, u32[]{:S(2)}) collective-permute-start(bf16[24,512]{1,0:T(8,128)(2,1)S(1)} %get-tuple-element.124), channel_id=1, source_target_pairs={{0,32},{16,48},{32,0},{48,16},{64,96},{80,112},{96,64},{112,80},{1... | collective-permute-start | bytes 73736 | tf_op jit(solution)/shard_map/ppermute | solution.py:302
  83.8 3.6 %collective-permute-start.18 = (bf16[24,512]{1,0:T(8,128)(2,1)S(1)}, bf16[24,512]{1,0:T(8,128)(2,1)S(1)}, u32[]{:S(2)}, u32[]{:S(2)}) collective-permute-start(bf16[24,512]{1,0:T(8,128)(2,1)S(1)} %get-tuple-element.126), channel_id=1, source_target_pairs={{0,48},{16,0},{32,16},{48,32},{64,112},{80,64},{96,80},{112,96},{1... | collective-permute-start | bytes 73736 | tf_op jit(solution)/shard_map/ppermute | solution.py:302
  87.3 1.9 %shard_map.134 = bf16[512,512]{1,0:T(8,128)(2,1)} custom-call(s32[1]{0:T(128)} %bitcast.core_ref, bf16[384,128]{1,0:T(8,128)(2,1)S(1)} %get-tuple-element.83.mine_ref, bf16[384,128]{1,0:T(8,128)(2,1)S(1)} %collective-permute-done.9.other_ref, bf16[512,512]{1,0:T(8,128)(2,1)S(1)} %bitcast.29, f32[1,128]{1,0:T(1,128)S(1)} %copy-done.7, ...), custom_call_target="tpu_custom_call" | custom-call | flops 1073741824 | bytes 1048576 | tf_op jit(solution)/shard_map/pallas_call | solution.py:253
  (49 shorter events, 7.6 us)
Async XLA Ops:
  0.7 12.5 %collective-permute-start.2 = (bf16[24,512]{1,0:T(8,128)(2,1)}, bf16[24,512]{1,0:T(8,128)(2,1)S(1)}, u32[]{:S(2)}, u32[]{:S(2)}) collective-permute-start(bf16[24,512]{1,0:T(8,128)(2,1)} %rows_ref), channel_id=1, source_target_pairs={{0,32},{16,48},{32,0},{48,16},{64,96},{80,112},{96,64},{112,80},{1... | collective-permute-start | bytes 73736 | tf_op jit(solution)/shard_map/ppermute | solution.py:302
  8.5 4.6 %collective-permute-start.1 = (bf16[24,512]{1,0:T(8,128)(2,1)}, bf16[24,512]{1,0:T(8,128)(2,1)S(1)}, u32[]{:S(2)}, u32[]{:S(2)}) collective-permute-start(bf16[24,512]{1,0:T(8,128)(2,1)} %rows_ref), channel_id=1, source_target_pairs={{0,48},{16,0},{32,16},{48,32},{64,112},{80,64},{96,80},{112,96},{1... | collective-permute-start | bytes 73736 | tf_op jit(solution)/shard_map/ppermute | solution.py:302
  8.5 5.1 %collective-permute-start = (bf16[24,512]{1,0:T(8,128)(2,1)}, bf16[24,512]{1,0:T(8,128)(2,1)S(1)}, u32[]{:S(2)}, u32[]{:S(2)}) collective-permute-start(bf16[24,512]{1,0:T(8,128)(2,1)} %rows_ref), channel_id=1, source_target_pairs={{0,16},{16,32},{32,48},{48,0},{64,80},{80,96},{96,112},{112,64},{1... | collective-permute-start | bytes 73736 | tf_op jit(solution)/shard_map/ppermute | solution.py:302
  10.8 11.8 %collective-permute-start.6 = (bf16[512,1024]{1,0:T(8,128)(2,1)}, bf16[512,1024]{1,0:T(8,128)(2,1)S(1)}, u32[]{:S(2)}, u32[]{:S(2)}) collective-permute-start(bf16[512,1024]{1,0:T(8,128)(2,1)} %bitcast.15), channel_id=1, source_target_pairs={{0,1},{1,0},{2,3},{3,2},{4,5},{5,4},{6,7},{7,6},{8,9},{9,8},{10,11... | collective-permute-start | bytes 3145736 | tf_op jit(solution)/shard_map/ppermute | solution.py:279
  12.4 10.3 %collective-permute-start.7 = (bf16[512,1024]{1,0:T(8,128)(2,1)}, bf16[512,1024]{1,0:T(8,128)(2,1)S(1)}, u32[]{:S(2)}, u32[]{:S(2)}) collective-permute-start(bf16[512,1024]{1,0:T(8,128)(2,1)} %bitcast.18), channel_id=1, source_target_pairs={{0,1},{1,0},{2,3},{3,2},{4,5},{5,4},{6,7},{7,6},{8,9},{9,8},{10,11... | collective-permute-start | bytes 3145736 | tf_op jit(solution)/shard_map/ppermute | solution.py:279
  13.1 12.8 %copy-start = (bf16[1,512,1024]{2,1,0:T(8,128)(2,1)S(1)}, bf16[1,512,1024]{2,1,0:T(8,128)(2,1)}, u32[]{:S(2)}) copy-start(bf16[1,512,1024]{2,1,0:T(8,128)(2,1)} %param.10) | copy-start | bytes 3145732
  13.1 12.8 %copy-start.1 = (bf16[1,512,1024]{2,1,0:T(8,128)(2,1)S(1)}, bf16[1,512,1024]{2,1,0:T(8,128)(2,1)}, u32[]{:S(2)}) copy-start(bf16[1,512,1024]{2,1,0:T(8,128)(2,1)} %param.11) | copy-start | bytes 3145732
  13.6 5.1 %collective-permute-start.5 = (bf16[4,24,512]{2,1,0:T(8,128)(2,1)S(1)}, bf16[4,24,512]{2,1,0:T(8,128)(2,1)S(1)}, u32[]{:S(2)}, u32[]{:S(2)}) collective-permute-start(bf16[4,24,512]{2,1,0:T(8,128)(2,1)S(1)} %shard_map.120.refs_0_), channel_id=1, source_target_pairs={{0,128},{16,144},{32,160},{48,176},{64,192},{80,208},{96,224},{112... | collective-permute-start | bytes 294920 | tf_op jit(solution)/shard_map/ppermute | solution.py:305
  16.6 3.5 %collective-permute-start.4 = (bf16[4,24,512]{2,1,0:T(8,128)(2,1)S(1)}, bf16[4,24,512]{2,1,0:T(8,128)(2,1)S(1)}, u32[]{:S(2)}, u32[]{:S(2)}) collective-permute-start(bf16[4,24,512]{2,1,0:T(8,128)(2,1)S(1)} %shard_map.120.refs_0_), channel_id=1, source_target_pairs={{0,192},{16,208},{32,224},{48,240},{64,0},{80,16},{96,32},{112,48}... | collective-permute-start | bytes 294920 | tf_op jit(solution)/shard_map/ppermute | solution.py:305
  17.4 5.2 %collective-permute-start.3 = (bf16[4,24,512]{2,1,0:T(8,128)(2,1)S(1)}, bf16[4,24,512]{2,1,0:T(8,128)(2,1)S(1)}, u32[]{:S(2)}, u32[]{:S(2)}) collective-permute-start(bf16[4,24,512]{2,1,0:T(8,128)(2,1)S(1)} %shard_map.120.refs_0_), channel_id=1, source_target_pairs={{0,64},{16,80},{32,96},{48,112},{64,128},{80,144},{96,160},{112,17... | collective-permute-start | bytes 294920 | tf_op jit(solution)/shard_map/ppermute | solution.py:305
  22.7 4.6 %collective-permute-start.8 = (bf16[384,512]{1,0:T(8,128)(2,1)S(1)}, bf16[384,512]{1,0:T(8,128)(2,1)S(1)}, u32[]{:S(2)}, u32[]{:S(2)}) collective-permute-start(bf16[384,512]{1,0:T(8,128)(2,1)S(1)} %bitcast.22), channel_id=1, source_target_pairs={{0,1},{1,0},{2,3},{3,2},{4,5},{5,4},{6,7},{7,6},{8,9},{9,8},{10,11... | collective-permute-start | bytes 1179656 | tf_op jit(solution)/shard_map/ppermute | solution.py:279
  27.9 17.2 %copy-start.4 = (f32[1,128]{1,0:T(1,128)S(1)}, f32[1,128]{1,0:T(1,128)}, u32[]{:S(2)}) copy-start(f32[1,128]{1,0:T(1,128)} %gain_ref.6) | copy-start | bytes 1540
  27.9 19.3 %copy-start.5 = (bf16[1,512,512]{2,1,0:T(8,128)(2,1)S(1)}, bf16[1,512,512]{2,1,0:T(8,128)(2,1)}, u32[]{:S(2)}) copy-start(bf16[1,512,512]{2,1,0:T(8,128)(2,1)} %param.9) | copy-start | bytes 1572868
  27.9 19.3 %copy-start.7 = (f32[1,128]{1,0:T(1,128)S(1)}, f32[1,128]{1,0:T(1,128)}, u32[]{:S(2)}) copy-start(f32[1,128]{1,0:T(1,128)} %gain_ref.7) | copy-start | bytes 1540
  45.3 2.8 %collective-permute-start.9 = (bf16[384,128]{1,0:T(8,128)(2,1)S(1)}, bf16[384,128]{1,0:T(8,128)(2,1)S(1)}, u32[]{:S(2)}, u32[]{:S(2)}) collective-permute-start(bf16[384,128]{1,0:T(8,128)(2,1)S(1)} %get-tuple-element.83.mine_ref), channel_id=1, source_target_pairs={{0,1},{1,0},{2,3},{3,2},{4,5},{5,4},{6,7},{7,6},{8,9},{9,8},{10,11... | collective-permute-start | bytes 294920 | tf_op jit(solution)/shard_map/ppermute | solution.py:279
  50.8 1.4 %collective-permute-start.10 = (bf16[384,128]{1,0:T(8,128)(2,1)S(1)}, bf16[384,128]{1,0:T(8,128)(2,1)S(1)}, u32[]{:S(2)}, u32[]{:S(2)}) collective-permute-start(bf16[384,128]{1,0:T(8,128)(2,1)S(1)} %get-tuple-element.92), channel_id=1, source_target_pairs={{0,1},{1,0},{2,3},{3,2},{4,5},{5,4},{6,7},{7,6},{8,9},{9,8},{10,11... | collective-permute-start | bytes 294920 | tf_op jit(solution)/shard_map/ppermute | solution.py:279
  68.3 2.6 %collective-permute-start.11 = (bf16[384,512]{1,0:T(8,128)(2,1)S(1)}, bf16[384,512]{1,0:T(8,128)(2,1)S(1)}, u32[]{:S(2)}, u32[]{:S(2)}) collective-permute-start(bf16[384,512]{1,0:T(8,128)(2,1)S(1)} %shard_map.128), channel_id=1, source_target_pairs={{0,1},{1,0},{2,3},{3,2},{4,5},{5,4},{6,7},{7,6},{8,9},{9,8},{10,11... | collective-permute-start | bytes 1179656 | tf_op jit(solution)/shard_map/ppermute | solution.py:279
  71.0 4.6 %collective-permute-start.15 = (bf16[8,384,128]{2,1,0:T(8,128)(2,1)S(1)}, bf16[8,384,128]{2,1,0:T(8,128)(2,1)S(1)}, u32[]{:S(2)}, u32[]{:S(2)}) collective-permute-start(bf16[8,384,128]{2,1,0:T(8,128)(2,1)S(1)} %all_to_all.11.grads_ref.mine_ref), channel_id=1, source_target_pairs={{0,1},{1,0},{2,3},{3,2},{4,5},{5,4},{6,7},{7,6},{8,9},{9,8},{10,11... | collective-permute-start | bytes 2359304 | tf_op jit(solution)/shard_map/ppermute | solution.py:279
  71.4 6.8 %collective-permute-start.12 = (bf16[4,24,512]{2,1,0:T(8,128)(2,1)S(1)}, bf16[4,24,512]{2,1,0:T(8,128)(2,1)S(1)}, u32[]{:S(2)}, u32[]{:S(2)}) collective-permute-start(bf16[4,24,512]{2,1,0:T(8,128)(2,1)S(1)} %get-tuple-element.105), channel_id=1, source_target_pairs={{0,128},{16,144},{32,160},{48,176},{64,192},{80,208},{96,224},{112... | collective-permute-start | bytes 294920 | tf_op jit(solution)/shard_map/ppermute | solution.py:305
  71.6 7.9 %collective-permute-start.13 = (bf16[4,24,512]{2,1,0:T(8,128)(2,1)S(1)}, bf16[4,24,512]{2,1,0:T(8,128)(2,1)S(1)}, u32[]{:S(2)}, u32[]{:S(2)}) collective-permute-start(bf16[4,24,512]{2,1,0:T(8,128)(2,1)S(1)} %get-tuple-element.106), channel_id=1, source_target_pairs={{0,64},{16,80},{32,96},{48,112},{64,128},{80,144},{96,160},{112,17... | collective-permute-start | bytes 294920 | tf_op jit(solution)/shard_map/ppermute | solution.py:305
  71.8 7.7 %collective-permute-start.14 = (bf16[4,24,512]{2,1,0:T(8,128)(2,1)S(1)}, bf16[4,24,512]{2,1,0:T(8,128)(2,1)S(1)}, u32[]{:S(2)}, u32[]{:S(2)}) collective-permute-start(bf16[4,24,512]{2,1,0:T(8,128)(2,1)S(1)} %get-tuple-element.107), channel_id=1, source_target_pairs={{0,192},{16,208},{32,224},{48,240},{64,0},{80,16},{96,32},{112,48}... | collective-permute-start | bytes 294920 | tf_op jit(solution)/shard_map/ppermute | solution.py:305
  79.6 9.7 %collective-permute-start.16 = (bf16[24,512]{1,0:T(8,128)(2,1)S(1)}, bf16[24,512]{1,0:T(8,128)(2,1)S(1)}, u32[]{:S(2)}, u32[]{:S(2)}) collective-permute-start(bf16[24,512]{1,0:T(8,128)(2,1)S(1)} %get-tuple-element.124), channel_id=1, source_target_pairs={{0,32},{16,48},{32,0},{48,16},{64,96},{80,112},{96,64},{112,80},{1... | collective-permute-start | bytes 73736 | tf_op jit(solution)/shard_map/ppermute | solution.py:302
  83.8 5.5 %collective-permute-start.17 = (bf16[24,512]{1,0:T(8,128)(2,1)S(1)}, bf16[24,512]{1,0:T(8,128)(2,1)S(1)}, u32[]{:S(2)}, u32[]{:S(2)}) collective-permute-start(bf16[24,512]{1,0:T(8,128)(2,1)S(1)} %get-tuple-element.125), channel_id=1, source_target_pairs={{0,16},{16,32},{32,48},{48,0},{64,80},{80,96},{96,112},{112,64},{1... | collective-permute-start | bytes 73736 | tf_op jit(solution)/shard_map/ppermute | solution.py:302
  83.8 5.5 %collective-permute-start.18 = (bf16[24,512]{1,0:T(8,128)(2,1)S(1)}, bf16[24,512]{1,0:T(8,128)(2,1)S(1)}, u32[]{:S(2)}, u32[]{:S(2)}) collective-permute-start(bf16[24,512]{1,0:T(8,128)(2,1)S(1)} %get-tuple-element.126), channel_id=1, source_target_pairs={{0,48},{16,0},{32,16},{48,32},{64,112},{80,64},{96,80},{112,96},{1... | collective-permute-start | bytes 73736 | tf_op jit(solution)/shard_map/ppermute | solution.py:302
  (3 other events, 6.5 us)

commit v9 on v7

--- a/solution.py
+++ b/solution.py
@@ -112,9 +112,7 @@
     values = by_core(core, other_ref[...], mine_ref[...])
     seen = seen_ref[...]
     empty = jnp.where(seen == 0, 1.0, 0.0)
-    visible = jnp.concatenate(
-        [jnp.broadcast_to(i < seen, (TILE_ROWS, text)) for i in range(rows // TILE_ROWS)], 0
-    )
+    shown = [jnp.where(i < seen, 1.0, 0.0) for i in range(rows // TILE_ROWS)]
     key_grad = jnp.zeros((rows, head), f32)
     value_grad = jnp.zeros((rows, head), f32)
     for h in range(width // head):
@@ -122,7 +120,10 @@
         up = up_ref[:, cols]
         normed = normed_ref[:, cols]
         scores = dot(keys, normed, BOTH_LAST)
-        expo = jnp.where(visible, jnp.exp2(scores * (scale * LOG2_E)), 0.0)
+        expo = jnp.exp2(scores * (scale * LOG2_E))
+        expo = jnp.concatenate(
+            [expo[i * TILE_ROWS : (i + 1) * TILE_ROWS] * row for i, row in enumerate(shown)], 0
+        )
         totals = jnp.sum(expo, 0, keepdims=True) + empty
         probs = expo * (1.0 / totals)
         probs_low = probs.astype(bf16)
@@ -349,12 +350,6 @@
     out_scratch = [
         pltpu.VMEM((text, width), bf16), pltpu.SemaphoreType.DMA((width // head,))
     ]
-    context = call(
-        context_kernel, [((text, width), bf16)], core, kv_mine, kv_other, probs,
-        scalar=True, to_hbm=(0,), scratch=out_scratch,
-        cost=pl.CostEstimate(flops=2**30, bytes_accessed=2**20, transcendentals=0),
-    )
-    received, context = fence(received, context)
     copies = call(
         kv_grad_kernel, [(pieces, bf16)], core, keep, received, raw, key_gain, scalar=True
     )
@@ -375,7 +370,9 @@
         my_y, image_own.reshape(sections, *block), received.reshape(sections, *block),
         scalar=True,
     )
-    keep, sends, rows, grads, score_grad = fence(keep, sends, rows, grads, score_grad)
+    keep, sends, rows, grads, probs, score_grad = fence(
+        keep, sends, rows, grads, probs, score_grad
+    )
     received = [along_y(x, k) for k, x in zip(LATE_STEPS[1:], sends)]
     grads_other = other_core(grads)
     key_weight_grad, value_weight_grad = call(
@@ -400,7 +397,14 @@
         scatter_z_kernel, [(block, f32)] + [(block, bf16)] * (SIDE - 1),
         my_z, keep, *received, scalar=True, scratch=[pltpu.VMEM(column, f32)],
     )
+    keep, sends, probs = fence(keep, sends, probs)
     received = [along_z(x, k) for k, x in zip(LATE_STEPS[1:], sends)]
+    context = call(
+        context_kernel, [((text, width), bf16)], core, kv_mine, kv_other, probs,
+        scalar=True, to_hbm=(0,), scratch=out_scratch,
+        cost=pl.CostEstimate(flops=2**30, bytes_accessed=2**20, transcendentals=0),
+    )
+    received, context = fence(received, context)
     image_grad = call(sum_kernel, [(block, f32)], keep, *received)
     return (
         context[None], query_grad[None], key_weight_grad[None], value_weight_grad[None], image_grad

time: 89.9 us -> 89.5 us (level)
    ppermute x6, waiting for transfers between devices: 1.66 us -> 0.46 us  [along_z(): return lax.ppermute(x, 'section', to)]
    ppermute x7, waiting for transfers between devices: 2.07 us -> 3.01 us  [other_core(): return lax.ppermute(x, 'tp', swap)]
where the time goes in v9:
time: 89.5 us; the launch traced here: 89.3 us
  starting transfers between devices  34.1 us (38%)
  blocking collectives  32.4 us (36%)
  Pallas kernels  12.4 us (14%)
  waiting for transfers between devices  8.68 us (10%)
    all_to_all x2, blocking collectives, over_chips(): return lax.all_to_all(x, 'tp', 0, 0, axis_index_groups=same_core)  32.4 us
    ppermute x6, starting transfers between devices, along_z(): return lax.ppermute(x, 'section', to)  17.9 us
    pallas_call x17, Pallas kernels, call(): pl.pallas_call(kernel, out_shape=shapes if many else shapes[0], in_specs=...  12.4 us
    ppermute x7, starting transfers between devices, other_core(): return lax.ppermute(x, 'tp', swap)  8.87 us
    ppermute x6, starting transfers between devices, along_y(): lax.ppermute(x, 'section', [(i, (i + k * SIDE) % sections) for i in range...  7.34 us
    ppermute x6, waiting for transfers between devices, along_y(): lax.ppermute(x, 'section', [(i, (i + k * SIDE) % sections) for i in range...  5.21 us
    ppermute x7, waiting for transfers between devices, other_core(): return lax.ppermute(x, 'tp', swap)  3.01 us
  transfers between devices with their start and end apart: 19, of which 9 were waited for; matrix products, arithmetic and copies ran while one was open for 0% of the time, Pallas kernels for 8%

profile of v9, /device:TPU:1, one launch (start us, length us, event | category | flops | bytes accessed | tf_op | source)
XLA Modules:
  0.0 89.3 jit_solution(1869878303921330686)
XLA Ops:
  0.7 7.8 %collective-permute-start.2 = (bf16[24,512]{1,0:T(8,128)(2,1)}, bf16[24,512]{1,0:T(8,128)(2,1)S(1)}, u32[]{:S(2)}, u32[]{:S(2)}) collective-permute-start(bf16[24,512]{1,0:T(8,128)(2,1)} %rows_ref), channel_id=1, source_target_pairs={{0,32},{16,48},{32,0},{48,16},{64,96},{80,112},{96,64},{112,80},{1... | collective-permute-start | bytes 73736 | tf_op jit(solution)/shard_map/ppermute | solution.py:302
  8.5 2.4 %collective-permute-start = (bf16[24,512]{1,0:T(8,128)(2,1)}, bf16[24,512]{1,0:T(8,128)(2,1)S(1)}, u32[]{:S(2)}, u32[]{:S(2)}) collective-permute-start(bf16[24,512]{1,0:T(8,128)(2,1)} %rows_ref), channel_id=1, source_target_pairs={{0,16},{16,32},{32,48},{48,0},{64,80},{80,96},{96,112},{112,64},{1... | collective-permute-start | bytes 73736 | tf_op jit(solution)/shard_map/ppermute | solution.py:302
  10.8 1.5 %collective-permute-start.6 = (bf16[512,1024]{1,0:T(8,128)(2,1)}, bf16[512,1024]{1,0:T(8,128)(2,1)S(1)}, u32[]{:S(2)}, u32[]{:S(2)}) collective-permute-start(bf16[512,1024]{1,0:T(8,128)(2,1)} %bitcast.15), channel_id=1, source_target_pairs={{0,1},{1,0},{2,3},{3,2},{4,5},{5,4},{6,7},{7,6},{8,9},{9,8},{10,11... | collective-permute-start | bytes 3145736 | tf_op jit(solution)/shard_map/ppermute | solution.py:279
  12.4 0.7 copy-done.6
  13.6 3.0 %collective-permute-start.5 = (bf16[4,24,512]{2,1,0:T(8,128)(2,1)S(1)}, bf16[4,24,512]{2,1,0:T(8,128)(2,1)S(1)}, u32[]{:S(2)}, u32[]{:S(2)}) collective-permute-start(bf16[4,24,512]{2,1,0:T(8,128)(2,1)S(1)} %shard_map.120.refs_0_), channel_id=1, source_target_pairs={{0,128},{16,144},{32,160},{48,176},{64,192},{80,208},{96,224},{112... | collective-permute-start | bytes 294920 | tf_op jit(solution)/shard_map/ppermute | solution.py:305
  16.6 0.8 collective-permute-start.4
  17.4 0.7 collective-permute-start.3
  18.6 1.4 %collective-permute-done.4.refs_2_ = bf16[4,24,512]{2,1,0:T(8,128)(2,1)S(1)} collective-permute-done((bf16[4,24,512]{2,1,0:T(8,128)(2,1)S(1)}, bf16[4,24,512]{2,1,0:T(8,128)(2,1)S(1)}, u32[]{:S(2)}, u32[]{:S(2)}) %collective-permute-start.4) | collective-permute-done | bytes 98336 | tf_op jit(solution)/shard_map/ppermute | solution.py:305
  20.1 2.5 %collective-permute-done.3.refs_1_ = bf16[4,24,512]{2,1,0:T(8,128)(2,1)S(1)} collective-permute-done((bf16[4,24,512]{2,1,0:T(8,128)(2,1)S(1)}, bf16[4,24,512]{2,1,0:T(8,128)(2,1)S(1)}, u32[]{:S(2)}, u32[]{:S(2)}) %collective-permute-start.3) | collective-permute-done | bytes 98336 | tf_op jit(solution)/shard_map/ppermute | solution.py:305
  22.7 3.3 %collective-permute-start.8 = (bf16[384,512]{1,0:T(8,128)(2,1)S(1)}, bf16[384,512]{1,0:T(8,128)(2,1)S(1)}, u32[]{:S(2)}, u32[]{:S(2)}) collective-permute-start(bf16[384,512]{1,0:T(8,128)(2,1)S(1)} %bitcast.22), channel_id=1, source_target_pairs={{0,1},{1,0},{2,3},{3,2},{4,5},{5,4},{6,7},{7,6},{8,9},{9,8},{10,11... | collective-permute-start | bytes 1179656 | tf_op jit(solution)/shard_map/ppermute | solution.py:279
  26.5 0.7 collective-permute-done.8.rows_ref
  27.9 17.1 %all_to_all.10.parts_ref = bf16[8,384,128]{2,1,0:T(8,128)(2,1)S(1)} all-to-all(bf16[8,384,128]{2,1,0:T(8,128)(2,1)S(1)} %shard_map.123), channel_id=1, replica_groups={{0,2,4,6,8,10,12,14},{1,3,5,7,9,11,13,15},{16,18,20,22,24,26,28,30},{17..., dimensions={0} | all-to-all | bytes 1572864 | tf_op jit(solution)/shard_map/all_to_all | solution.py:282
  45.3 1.9 %collective-permute-start.9 = (bf16[384,128]{1,0:T(8,128)(2,1)S(1)}, bf16[384,128]{1,0:T(8,128)(2,1)S(1)}, u32[]{:S(2)}, u32[]{:S(2)}) collective-permute-start(bf16[384,128]{1,0:T(8,128)(2,1)S(1)} %get-tuple-element.82.mine_ref), channel_id=1, source_target_pairs={{0,1},{1,0},{2,3},{3,2},{4,5},{5,4},{6,7},{7,6},{8,9},{9,8},{10,11... | collective-permute-start | bytes 294920 | tf_op jit(solution)/shard_map/ppermute | solution.py:279
  48.1 2.7 %shard_map.126 = (bf16[4,384,512]{2,1,0:T(8,128)(2,1)S(1)}, bf16[4,384,512]{2,1,0:T(8,128)(2,1)S(1)}, bf16[384,128]{1,0:T(8,128)(2,1)S(1)}, f32[384,128]{1,0:T(8,128)S(1)}) custom-call(s32[1]{0:T(128)} %bitcast.core_ref, bf16[384,128]{1,0:T(8,128)(2,1)S(1)} %get-tuple-element.82.mine_ref, bf16[384,128]{1,0:T(8,128)(2,1)S(1)} %collective-permute-done.9.other_ref, ...), custom_call_target="tpu_custom_call" | custom-call | tf_op jit(solution)/shard_map/pallas_call | solution.py:253
  51.2 0.9 %collective-permute-done.10.received_ref = bf16[384,128]{1,0:T(8,128)(2,1)S(1)} collective-permute-done((bf16[384,128]{1,0:T(8,128)(2,1)S(1)}, bf16[384,128]{1,0:T(8,128)(2,1)S(1)}, u32[]{:S(2)}, u32[]{:S(2)}) %collective-permute-start.10) | collective-permute-done | bytes 98336 | tf_op jit(solution)/shard_map/ppermute | solution.py:279
  52.4 15.3 %all_to_all.11.grads_ref.mine_ref = bf16[8,384,128]{2,1,0:T(8,128)(2,1)S(1)} all-to-all(bf16[8,384,128]{2,1,0:T(8,128)(2,1)S(1)} %shard_map.127), channel_id=1, replica_groups={{0,2,4,6,8,10,12,14},{1,3,5,7,9,11,13,15},{16,18,20,22,24,26,28,30},{17..., dimensions={0} | all-to-all | bytes 1572864 | tf_op jit(solution)/shard_map/all_to_all | solution.py:282
  68.3 1.3 %collective-permute-start.11 = (bf16[384,512]{1,0:T(8,128)(2,1)S(1)}, bf16[384,512]{1,0:T(8,128)(2,1)S(1)}, u32[]{:S(2)}, u32[]{:S(2)}) collective-permute-start(bf16[384,512]{1,0:T(8,128)(2,1)S(1)} %shard_map.128), channel_id=1, source_target_pairs={{0,1},{1,0},{2,3},{3,2},{4,5},{5,4},{6,7},{7,6},{8,9},{9,8},{10,11... | collective-permute-start | bytes 1179656 | tf_op jit(solution)/shard_map/ppermute | solution.py:279
  70.1 0.7 collective-permute-done.11
  71.8 2.5 %collective-permute-start.14 = (bf16[4,24,512]{2,1,0:T(8,128)(2,1)S(1)}, bf16[4,24,512]{2,1,0:T(8,128)(2,1)S(1)}, u32[]{:S(2)}, u32[]{:S(2)}) collective-permute-start(bf16[4,24,512]{2,1,0:T(8,128)(2,1)S(1)} %get-tuple-element.107), channel_id=1, source_target_pairs={{0,192},{16,208},{32,224},{48,240},{64,0},{80,16},{96,32},{112,48}... | collective-permute-start | bytes 294920 | tf_op jit(solution)/shard_map/ppermute | solution.py:305
  74.3 1.9 %shard_map.132 = bf16[512,512]{1,0:T(8,128)(2,1)} custom-call(s32[1]{0:T(128)} %bitcast.core_ref, bf16[384,128]{1,0:T(8,128)(2,1)S(1)} %get-tuple-element.82.mine_ref, bf16[384,128]{1,0:T(8,128)(2,1)S(1)} %collective-permute-done.9.other_ref, bf16[512,512]{1,0:T(8,128)(2,1)S(1)} %bitcast.29, f32[1,128]{1,0:T(1,128)S(1)} %copy-done.7, ...), custom_call_target="tpu_custom_call" | custom-call | flops 1073741824 | bytes 1048576 | tf_op jit(solution)/shard_map/pallas_call | solution.py:253
  76.3 2.6 %shard_map.131 = (bf16[512,1024]{1,0:T(8,128)(2,1)}, bf16[512,1024]{1,0:T(8,128)(2,1)}) custom-call(s32[1]{0:T(128)} %bitcast.core_ref, bf16[384,512]{1,0:T(8,128)(2,1)S(1)} %bitcast.24, bf16[8,384,128]{2,1,0:T(8,128)(2,1)S(1)} %all_to_all.11.grads_ref.mine_ref, bf16[8,384,128]{2,1,0:T(8,128)(2,1)S(1)} %collective-permute-done.15.other_ref), custom_call_target="tpu_custom_call" | custom-call | flops 805306368 | bytes 4194304 | tf_op jit(solution)/shard_map/pallas_call | solution.py:253
  79.6 4.1 %collective-permute-start.16 = (bf16[24,512]{1,0:T(8,128)(2,1)S(1)}, bf16[24,512]{1,0:T(8,128)(2,1)S(1)}, u32[]{:S(2)}, u32[]{:S(2)}) collective-permute-start(bf16[24,512]{1,0:T(8,128)(2,1)S(1)} %get-tuple-element.121), channel_id=1, source_target_pairs={{0,32},{16,48},{32,0},{48,16},{64,96},{80,112},{96,64},{112,80},{1... | collective-permute-start | bytes 73736 | tf_op jit(solution)/shard_map/ppermute | solution.py:302
  83.8 3.6 %collective-permute-start.18 = (bf16[24,512]{1,0:T(8,128)(2,1)S(1)}, bf16[24,512]{1,0:T(8,128)(2,1)S(1)}, u32[]{:S(2)}, u32[]{:S(2)}) collective-permute-start(bf16[24,512]{1,0:T(8,128)(2,1)S(1)} %get-tuple-element.123), channel_id=1, source_target_pairs={{0,48},{16,0},{32,16},{48,32},{64,112},{80,64},{96,80},{112,96},{1... | collective-permute-start | bytes 73736 | tf_op jit(solution)/shard_map/ppermute | solution.py:302
  87.3 1.3 %shard_map.134 = bf16[512,512]{1,0:T(8,128)(2,1)} custom-call(s32[1]{0:T(128)} %bitcast.core_ref, bf16[384,128]{1,0:T(8,128)(2,1)S(1)} %get-tuple-element.82.mine_ref, bf16[384,128]{1,0:T(8,128)(2,1)S(1)} %collective-permute-done.9.other_ref, bf16[4,384,512]{2,1,0:T(8,128)(2,1)S(1)} %get-tuple-element.124.probs_ref), custom_call_target="tpu_custom_call" | custom-call | flops 1073741824 | bytes 1048576 | tf_op jit(solution)/shard_map/pallas_call | solution.py:253
  (49 shorter events, 7.6 us)
Async XLA Ops:
  0.7 12.5 %collective-permute-start.2 = (bf16[24,512]{1,0:T(8,128)(2,1)}, bf16[24,512]{1,0:T(8,128)(2,1)S(1)}, u32[]{:S(2)}, u32[]{:S(2)}) collective-permute-start(bf16[24,512]{1,0:T(8,128)(2,1)} %rows_ref), channel_id=1, source_target_pairs={{0,32},{16,48},{32,0},{48,16},{64,96},{80,112},{96,64},{112,80},{1... | collective-permute-start | bytes 73736 | tf_op jit(solution)/shard_map/ppermute | solution.py:302
  8.5 4.6 %collective-permute-start.1 = (bf16[24,512]{1,0:T(8,128)(2,1)}, bf16[24,512]{1,0:T(8,128)(2,1)S(1)}, u32[]{:S(2)}, u32[]{:S(2)}) collective-permute-start(bf16[24,512]{1,0:T(8,128)(2,1)} %rows_ref), channel_id=1, source_target_pairs={{0,48},{16,0},{32,16},{48,32},{64,112},{80,64},{96,80},{112,96},{1... | collective-permute-start | bytes 73736 | tf_op jit(solution)/shard_map/ppermute | solution.py:302
  8.5 5.1 %collective-permute-start = (bf16[24,512]{1,0:T(8,128)(2,1)}, bf16[24,512]{1,0:T(8,128)(2,1)S(1)}, u32[]{:S(2)}, u32[]{:S(2)}) collective-permute-start(bf16[24,512]{1,0:T(8,128)(2,1)} %rows_ref), channel_id=1, source_target_pairs={{0,16},{16,32},{32,48},{48,0},{64,80},{80,96},{96,112},{112,64},{1... | collective-permute-start | bytes 73736 | tf_op jit(solution)/shard_map/ppermute | solution.py:302
  10.8 11.8 %collective-permute-start.6 = (bf16[512,1024]{1,0:T(8,128)(2,1)}, bf16[512,1024]{1,0:T(8,128)(2,1)S(1)}, u32[]{:S(2)}, u32[]{:S(2)}) collective-permute-start(bf16[512,1024]{1,0:T(8,128)(2,1)} %bitcast.15), channel_id=1, source_target_pairs={{0,1},{1,0},{2,3},{3,2},{4,5},{5,4},{6,7},{7,6},{8,9},{9,8},{10,11... | collective-permute-start | bytes 3145736 | tf_op jit(solution)/shard_map/ppermute | solution.py:279
  12.4 10.3 %collective-permute-start.7 = (bf16[512,1024]{1,0:T(8,128)(2,1)}, bf16[512,1024]{1,0:T(8,128)(2,1)S(1)}, u32[]{:S(2)}, u32[]{:S(2)}) collective-permute-start(bf16[512,1024]{1,0:T(8,128)(2,1)} %bitcast.18), channel_id=1, source_target_pairs={{0,1},{1,0},{2,3},{3,2},{4,5},{5,4},{6,7},{7,6},{8,9},{9,8},{10,11... | collective-permute-start | bytes 3145736 | tf_op jit(solution)/shard_map/ppermute | solution.py:279
  13.1 12.8 %copy-start = (bf16[1,512,1024]{2,1,0:T(8,128)(2,1)S(1)}, bf16[1,512,1024]{2,1,0:T(8,128)(2,1)}, u32[]{:S(2)}) copy-start(bf16[1,512,1024]{2,1,0:T(8,128)(2,1)} %param.10) | copy-start | bytes 3145732
  13.1 12.8 %copy-start.1 = (bf16[1,512,1024]{2,1,0:T(8,128)(2,1)S(1)}, bf16[1,512,1024]{2,1,0:T(8,128)(2,1)}, u32[]{:S(2)}) copy-start(bf16[1,512,1024]{2,1,0:T(8,128)(2,1)} %param.11) | copy-start | bytes 3145732
  13.6 5.1 %collective-permute-start.5 = (bf16[4,24,512]{2,1,0:T(8,128)(2,1)S(1)}, bf16[4,24,512]{2,1,0:T(8,128)(2,1)S(1)}, u32[]{:S(2)}, u32[]{:S(2)}) collective-permute-start(bf16[4,24,512]{2,1,0:T(8,128)(2,1)S(1)} %shard_map.120.refs_0_), channel_id=1, source_target_pairs={{0,128},{16,144},{32,160},{48,176},{64,192},{80,208},{96,224},{112... | collective-permute-start | bytes 294920 | tf_op jit(solution)/shard_map/ppermute | solution.py:305
  16.6 3.5 %collective-permute-start.4 = (bf16[4,24,512]{2,1,0:T(8,128)(2,1)S(1)}, bf16[4,24,512]{2,1,0:T(8,128)(2,1)S(1)}, u32[]{:S(2)}, u32[]{:S(2)}) collective-permute-start(bf16[4,24,512]{2,1,0:T(8,128)(2,1)S(1)} %shard_map.120.refs_0_), channel_id=1, source_target_pairs={{0,192},{16,208},{32,224},{48,240},{64,0},{80,16},{96,32},{112,48}... | collective-permute-start | bytes 294920 | tf_op jit(solution)/shard_map/ppermute | solution.py:305
  17.4 5.2 %collective-permute-start.3 = (bf16[4,24,512]{2,1,0:T(8,128)(2,1)S(1)}, bf16[4,24,512]{2,1,0:T(8,128)(2,1)S(1)}, u32[]{:S(2)}, u32[]{:S(2)}) collective-permute-start(bf16[4,24,512]{2,1,0:T(8,128)(2,1)S(1)} %shard_map.120.refs_0_), channel_id=1, source_target_pairs={{0,64},{16,80},{32,96},{48,112},{64,128},{80,144},{96,160},{112,17... | collective-permute-start | bytes 294920 | tf_op jit(solution)/shard_map/ppermute | solution.py:305
  22.7 4.6 %collective-permute-start.8 = (bf16[384,512]{1,0:T(8,128)(2,1)S(1)}, bf16[384,512]{1,0:T(8,128)(2,1)S(1)}, u32[]{:S(2)}, u32[]{:S(2)}) collective-permute-start(bf16[384,512]{1,0:T(8,128)(2,1)S(1)} %bitcast.22), channel_id=1, source_target_pairs={{0,1},{1,0},{2,3},{3,2},{4,5},{5,4},{6,7},{7,6},{8,9},{9,8},{10,11... | collective-permute-start | bytes 1179656 | tf_op jit(solution)/shard_map/ppermute | solution.py:279
  27.9 17.2 %copy-start.4 = (f32[1,128]{1,0:T(1,128)S(1)}, f32[1,128]{1,0:T(1,128)}, u32[]{:S(2)}) copy-start(f32[1,128]{1,0:T(1,128)} %gain_ref.6) | copy-start | bytes 1540
  27.9 19.3 %copy-start.5 = (bf16[1,512,512]{2,1,0:T(8,128)(2,1)S(1)}, bf16[1,512,512]{2,1,0:T(8,128)(2,1)}, u32[]{:S(2)}) copy-start(bf16[1,512,512]{2,1,0:T(8,128)(2,1)} %param.9) | copy-start | bytes 1572868
  27.9 19.3 %copy-start.7 = (f32[1,128]{1,0:T(1,128)S(1)}, f32[1,128]{1,0:T(1,128)}, u32[]{:S(2)}) copy-start(f32[1,128]{1,0:T(1,128)} %gain_ref.7) | copy-start | bytes 1540
  45.3 2.8 %collective-permute-start.9 = (bf16[384,128]{1,0:T(8,128)(2,1)S(1)}, bf16[384,128]{1,0:T(8,128)(2,1)S(1)}, u32[]{:S(2)}, u32[]{:S(2)}) collective-permute-start(bf16[384,128]{1,0:T(8,128)(2,1)S(1)} %get-tuple-element.82.mine_ref), channel_id=1, source_target_pairs={{0,1},{1,0},{2,3},{3,2},{4,5},{5,4},{6,7},{7,6},{8,9},{9,8},{10,11... | collective-permute-start | bytes 294920 | tf_op jit(solution)/shard_map/ppermute | solution.py:279
  50.8 1.4 %collective-permute-start.10 = (bf16[384,128]{1,0:T(8,128)(2,1)S(1)}, bf16[384,128]{1,0:T(8,128)(2,1)S(1)}, u32[]{:S(2)}, u32[]{:S(2)}) collective-permute-start(bf16[384,128]{1,0:T(8,128)(2,1)S(1)} %get-tuple-element.91), channel_id=1, source_target_pairs={{0,1},{1,0},{2,3},{3,2},{4,5},{5,4},{6,7},{7,6},{8,9},{9,8},{10,11... | collective-permute-start | bytes 294920 | tf_op jit(solution)/shard_map/ppermute | solution.py:279
  68.3 2.6 %collective-permute-start.11 = (bf16[384,512]{1,0:T(8,128)(2,1)S(1)}, bf16[384,512]{1,0:T(8,128)(2,1)S(1)}, u32[]{:S(2)}, u32[]{:S(2)}) collective-permute-start(bf16[384,512]{1,0:T(8,128)(2,1)S(1)} %shard_map.128), channel_id=1, source_target_pairs={{0,1},{1,0},{2,3},{3,2},{4,5},{5,4},{6,7},{7,6},{8,9},{9,8},{10,11... | collective-permute-start | bytes 1179656 | tf_op jit(solution)/shard_map/ppermute | solution.py:279
  71.0 5.3 %collective-permute-start.15 = (bf16[8,384,128]{2,1,0:T(8,128)(2,1)S(1)}, bf16[8,384,128]{2,1,0:T(8,128)(2,1)S(1)}, u32[]{:S(2)}, u32[]{:S(2)}) collective-permute-start(bf16[8,384,128]{2,1,0:T(8,128)(2,1)S(1)} %all_to_all.11.grads_ref.mine_ref), channel_id=1, source_target_pairs={{0,1},{1,0},{2,3},{3,2},{4,5},{5,4},{6,7},{7,6},{8,9},{9,8},{10,11... | collective-permute-start | bytes 2359304 | tf_op jit(solution)/shard_map/ppermute | solution.py:279
  71.4 7.5 %collective-permute-start.12 = (bf16[4,24,512]{2,1,0:T(8,128)(2,1)S(1)}, bf16[4,24,512]{2,1,0:T(8,128)(2,1)S(1)}, u32[]{:S(2)}, u32[]{:S(2)}) collective-permute-start(bf16[4,24,512]{2,1,0:T(8,128)(2,1)S(1)} %get-tuple-element.105), channel_id=1, source_target_pairs={{0,128},{16,144},{32,160},{48,176},{64,192},{80,208},{96,224},{112... | collective-permute-start | bytes 294920 | tf_op jit(solution)/shard_map/ppermute | solution.py:305
  71.6 7.9 %collective-permute-start.13 = (bf16[4,24,512]{2,1,0:T(8,128)(2,1)S(1)}, bf16[4,24,512]{2,1,0:T(8,128)(2,1)S(1)}, u32[]{:S(2)}, u32[]{:S(2)}) collective-permute-start(bf16[4,24,512]{2,1,0:T(8,128)(2,1)S(1)} %get-tuple-element.106), channel_id=1, source_target_pairs={{0,64},{16,80},{32,96},{48,112},{64,128},{80,144},{96,160},{112,17... | collective-permute-start | bytes 294920 | tf_op jit(solution)/shard_map/ppermute | solution.py:305
  71.8 7.7 %collective-permute-start.14 = (bf16[4,24,512]{2,1,0:T(8,128)(2,1)S(1)}, bf16[4,24,512]{2,1,0:T(8,128)(2,1)S(1)}, u32[]{:S(2)}, u32[]{:S(2)}) collective-permute-start(bf16[4,24,512]{2,1,0:T(8,128)(2,1)S(1)} %get-tuple-element.107), channel_id=1, source_target_pairs={{0,192},{16,208},{32,224},{48,240},{64,0},{80,16},{96,32},{112,48}... | collective-permute-start | bytes 294920 | tf_op jit(solution)/shard_map/ppermute | solution.py:305
  79.6 9.0 %collective-permute-start.16 = (bf16[24,512]{1,0:T(8,128)(2,1)S(1)}, bf16[24,512]{1,0:T(8,128)(2,1)S(1)}, u32[]{:S(2)}, u32[]{:S(2)}) collective-permute-start(bf16[24,512]{1,0:T(8,128)(2,1)S(1)} %get-tuple-element.121), channel_id=1, source_target_pairs={{0,32},{16,48},{32,0},{48,16},{64,96},{80,112},{96,64},{112,80},{1... | collective-permute-start | bytes 73736 | tf_op jit(solution)/shard_map/ppermute | solution.py:302
  83.8 4.9 %collective-permute-start.17 = (bf16[24,512]{1,0:T(8,128)(2,1)S(1)}, bf16[24,512]{1,0:T(8,128)(2,1)S(1)}, u32[]{:S(2)}, u32[]{:S(2)}) collective-permute-start(bf16[24,512]{1,0:T(8,128)(2,1)S(1)} %get-tuple-element.122), channel_id=1, source_target_pairs={{0,16},{16,32},{32,48},{48,0},{64,80},{80,96},{96,112},{112,64},{1... | collective-permute-start | bytes 73736 | tf_op jit(solution)/shard_map/ppermute | solution.py:302
  83.8 4.9 %collective-permute-start.18 = (bf16[24,512]{1,0:T(8,128)(2,1)S(1)}, bf16[24,512]{1,0:T(8,128)(2,1)S(1)}, u32[]{:S(2)}, u32[]{:S(2)}) collective-permute-start(bf16[24,512]{1,0:T(8,128)(2,1)S(1)} %get-tuple-element.123), channel_id=1, source_target_pairs={{0,48},{16,0},{32,16},{48,32},{64,112},{80,64},{96,80},{112,96},{1... | collective-permute-start | bytes 73736 | tf_op jit(solution)/shard_map/ppermute | solution.py:302
  (3 other events, 6.5 us)

commit v10 on v9

--- a/solution.py
+++ b/solution.py
@@ -290,8 +290,6 @@
     pieces = (kv_heads, rows_total, head)
     square = (rows_total, head)
 
-    key_other = other_core(key_weight[0])
-    value_other = other_core(value_weight[0])
     block = (own_rows, features)
     column = (SIDE, *block)
     section = lax.axis_index("section").astype(jnp.int32)
@@ -314,7 +312,10 @@
         gather_z_kernel, [(column, bf16)], my_z, own, *others, scalar=True,
         cost=pl.CostEstimate(flops=2**34, bytes_accessed=2**25, transcendentals=0),
     )
+    rows_z, key_weight, value_weight = fence(rows_z, key_weight, value_weight)
     others = [along_y(rows_z, k) for k in STEPS[1:]]
+    key_other = other_core(key_weight[0])
+    value_other = other_core(value_weight[0])
     blocks = call(
         gather_y_kernel, [((sections, *block), bf16)], my_y, rows_z, *others, scalar=True
     )

time: 89.5 us -> 90.4 us (1.010)
    ppermute x6, waiting for transfers between devices: 0.46 us -> 1.98 us  [along_z(): return lax.ppermute(x, 'section', to)]
    ppermute x6, waiting for transfers between devices: 5.21 us -> 3.99 us  [along_y(): lax.ppermute(x, 'section', [(i, (i + k * SIDE) % sections) for i in range...]
    ppermute x6, starting transfers between devices: 7.34 us -> 8.31 us  [along_y(): lax.ppermute(x, 'section', [(i, (i + k * SIDE) % sections) for i in range...]
where the time goes in v10:
time: 90.4 us; the launch traced here: 90.2 us
  starting transfers between devices  34.7 us (38%)
  blocking collectives  32.4 us (36%)
  Pallas kernels  12.4 us (14%)
  waiting for transfers between devices  8.99 us (10%)
    all_to_all x2, blocking collectives, over_chips(): return lax.all_to_all(x, 'tp', 0, 0, axis_index_groups=same_core)  32.4 us
    ppermute x6, starting transfers between devices, along_z(): return lax.ppermute(x, 'section', to)  17.9 us
    pallas_call x17, Pallas kernels, call(): pl.pallas_call(kernel, out_shape=shapes if many else shapes[0], in_specs=...  12.4 us
    ppermute x7, starting transfers between devices, other_core(): return lax.ppermute(x, 'tp', swap)  8.51 us
    ppermute x6, starting transfers between devices, along_y(): lax.ppermute(x, 'section', [(i, (i + k * SIDE) % sections) for i in range...  8.31 us
    ppermute x6, waiting for transfers between devices, along_y(): lax.ppermute(x, 'section', [(i, (i + k * SIDE) % sections) for i in range...  3.99 us
    ppermute x7, waiting for transfers between devices, other_core(): return lax.ppermute(x, 'tp', swap)  3.02 us
    ppermute x6, waiting for transfers between devices, along_z(): return lax.ppermute(x, 'section', to)  1.98 us
  transfers between devices with their start and end apart: 19, of which 9 were waited for; matrix products, arithmetic and copies ran while one was open for 0% of the time, Pallas kernels for 8%

profile of v10, /device:TPU:1, one launch (start us, length us, event | category | flops | bytes accessed | tf_op | source)
XLA Modules:
  0.0 90.2 jit_solution(10254928002415903682)
XLA Ops:
  0.7 7.8 %collective-permute-start.2 = (bf16[24,512]{1,0:T(8,128)(2,1)}, bf16[24,512]{1,0:T(8,128)(2,1)S(1)}, u32[]{:S(2)}, u32[]{:S(2)}) collective-permute-start(bf16[24,512]{1,0:T(8,128)(2,1)} %rows_ref), channel_id=1, source_target_pairs={{0,32},{16,48},{32,0},{48,16},{64,96},{80,112},{96,64},{112,80},{1... | collective-permute-start | bytes 73736 | tf_op jit(solution)/shard_map/ppermute | solution.py:300
  8.5 2.4 %collective-permute-start = (bf16[24,512]{1,0:T(8,128)(2,1)}, bf16[24,512]{1,0:T(8,128)(2,1)S(1)}, u32[]{:S(2)}, u32[]{:S(2)}) collective-permute-start(bf16[24,512]{1,0:T(8,128)(2,1)} %rows_ref), channel_id=1, source_target_pairs={{0,16},{16,32},{32,48},{48,0},{64,80},{80,96},{96,112},{112,64},{1... | collective-permute-start | bytes 73736 | tf_op jit(solution)/shard_map/ppermute | solution.py:300
  10.9 0.8 copy-done.6
  12.3 1.3 %collective-permute-done.refs_1_ = bf16[24,512]{1,0:T(8,128)(2,1)S(1)} collective-permute-done((bf16[24,512]{1,0:T(8,128)(2,1)}, bf16[24,512]{1,0:T(8,128)(2,1)S(1)}, u32[]{:S(2)}, u32[]{:S(2)}) %collective-permute-start) | collective-permute-done | bytes 24608 | tf_op jit(solution)/shard_map/ppermute | solution.py:300
  13.6 2.1 %collective-permute-start.7 = (bf16[512,1024]{1,0:T(8,128)(2,1)S(1)}, bf16[512,1024]{1,0:T(8,128)(2,1)S(1)}, u32[]{:S(2)}, u32[]{:S(2)}) collective-permute-start(bf16[512,1024]{1,0:T(8,128)(2,1)S(1)} %bitcast.18), channel_id=1, source_target_pairs={{0,1},{1,0},{2,3},{3,2},{4,5},{5,4},{6,7},{7,6},{8,9},{9,8},{10,11... | collective-permute-start | bytes 3145736 | tf_op jit(solution)/shard_map/ppermute | solution.py:279
  15.8 2.9 %collective-permute-start.5 = (bf16[4,24,512]{2,1,0:T(8,128)(2,1)S(1)}, bf16[4,24,512]{2,1,0:T(8,128)(2,1)S(1)}, u32[]{:S(2)}, u32[]{:S(2)}) collective-permute-start(bf16[4,24,512]{2,1,0:T(8,128)(2,1)S(1)} %shard_map.120.refs_0_), channel_id=1, source_target_pairs={{0,128},{16,144},{32,160},{48,176},{64,192},{80,208},{96,224},{112... | collective-permute-start | bytes 294920 | tf_op jit(solution)/shard_map/ppermute | solution.py:303
  18.7 0.8 collective-permute-start.4
  20.2 1.1 %collective-permute-done.5.refs_3_ = bf16[4,24,512]{2,1,0:T(8,128)(2,1)S(1)} collective-permute-done((bf16[4,24,512]{2,1,0:T(8,128)(2,1)S(1)}, bf16[4,24,512]{2,1,0:T(8,128)(2,1)S(1)}, u32[]{:S(2)}, u32[]{:S(2)}) %collective-permute-start.5) | collective-permute-done | bytes 98336 | tf_op jit(solution)/shard_map/ppermute | solution.py:303
  21.3 2.4 %collective-permute-done.4.refs_2_ = bf16[4,24,512]{2,1,0:T(8,128)(2,1)S(1)} collective-permute-done((bf16[4,24,512]{2,1,0:T(8,128)(2,1)S(1)}, bf16[4,24,512]{2,1,0:T(8,128)(2,1)S(1)}, u32[]{:S(2)}, u32[]{:S(2)}) %collective-permute-start.4) | collective-permute-done | bytes 98336 | tf_op jit(solution)/shard_map/ppermute | solution.py:303
  24.2 2.2 %collective-permute-start.8 = (bf16[384,512]{1,0:T(8,128)(2,1)S(1)}, bf16[384,512]{1,0:T(8,128)(2,1)S(1)}, u32[]{:S(2)}, u32[]{:S(2)}) collective-permute-start(bf16[384,512]{1,0:T(8,128)(2,1)S(1)} %bitcast.22), channel_id=1, source_target_pairs={{0,1},{1,0},{2,3},{3,2},{4,5},{5,4},{6,7},{7,6},{8,9},{9,8},{10,11... | collective-permute-start | bytes 1179656 | tf_op jit(solution)/shard_map/ppermute | solution.py:279
  27.1 0.7 collective-permute-done.8.rows_ref
  28.5 17.1 %all_to_all.10.parts_ref = bf16[8,384,128]{2,1,0:T(8,128)(2,1)S(1)} all-to-all(bf16[8,384,128]{2,1,0:T(8,128)(2,1)S(1)} %shard_map.123), channel_id=1, replica_groups={{0,2,4,6,8,10,12,14},{1,3,5,7,9,11,13,15},{16,18,20,22,24,26,28,30},{17..., dimensions={0} | all-to-all | bytes 1572864 | tf_op jit(solution)/shard_map/all_to_all | solution.py:282
  45.8 1.9 %collective-permute-start.9 = (bf16[384,128]{1,0:T(8,128)(2,1)S(1)}, bf16[384,128]{1,0:T(8,128)(2,1)S(1)}, u32[]{:S(2)}, u32[]{:S(2)}) collective-permute-start(bf16[384,128]{1,0:T(8,128)(2,1)S(1)} %get-tuple-element.88.mine_ref), channel_id=1, source_target_pairs={{0,1},{1,0},{2,3},{3,2},{4,5},{5,4},{6,7},{7,6},{8,9},{9,8},{10,11... | collective-permute-start | bytes 294920 | tf_op jit(solution)/shard_map/ppermute | solution.py:279
  48.7 2.6 %shard_map.126 = (bf16[4,384,512]{2,1,0:T(8,128)(2,1)S(1)}, bf16[4,384,512]{2,1,0:T(8,128)(2,1)S(1)}, bf16[384,128]{1,0:T(8,128)(2,1)S(1)}, f32[384,128]{1,0:T(8,128)S(1)}) custom-call(s32[1]{0:T(128)} %bitcast.core_ref, bf16[384,128]{1,0:T(8,128)(2,1)S(1)} %get-tuple-element.88.mine_ref, bf16[384,128]{1,0:T(8,128)(2,1)S(1)} %collective-permute-done.9.other_ref, ...), custom_call_target="tpu_custom_call" | custom-call | tf_op jit(solution)/shard_map/pallas_call | solution.py:253
  51.8 0.9 %collective-permute-done.10.received_ref = bf16[384,128]{1,0:T(8,128)(2,1)S(1)} collective-permute-done((bf16[384,128]{1,0:T(8,128)(2,1)S(1)}, bf16[384,128]{1,0:T(8,128)(2,1)S(1)}, u32[]{:S(2)}, u32[]{:S(2)}) %collective-permute-start.10) | collective-permute-done | bytes 98336 | tf_op jit(solution)/shard_map/ppermute | solution.py:279
  52.9 15.3 %all_to_all.11.grads_ref.mine_ref = bf16[8,384,128]{2,1,0:T(8,128)(2,1)S(1)} all-to-all(bf16[8,384,128]{2,1,0:T(8,128)(2,1)S(1)} %shard_map.127), channel_id=1, replica_groups={{0,2,4,6,8,10,12,14},{1,3,5,7,9,11,13,15},{16,18,20,22,24,26,28,30},{17..., dimensions={0} | all-to-all | bytes 1572864 | tf_op jit(solution)/shard_map/all_to_all | solution.py:282
  68.8 1.3 %collective-permute-start.11 = (bf16[384,512]{1,0:T(8,128)(2,1)S(1)}, bf16[384,512]{1,0:T(8,128)(2,1)S(1)}, u32[]{:S(2)}, u32[]{:S(2)}) collective-permute-start(bf16[384,512]{1,0:T(8,128)(2,1)S(1)} %shard_map.128), channel_id=1, source_target_pairs={{0,1},{1,0},{2,3},{3,2},{4,5},{5,4},{6,7},{7,6},{8,9},{9,8},{10,11... | collective-permute-start | bytes 1179656 | tf_op jit(solution)/shard_map/ppermute | solution.py:279
  71.9 1.3 %collective-permute-start.12 = (bf16[4,24,512]{2,1,0:T(8,128)(2,1)S(1)}, bf16[4,24,512]{2,1,0:T(8,128)(2,1)S(1)}, u32[]{:S(2)}, u32[]{:S(2)}) collective-permute-start(bf16[4,24,512]{2,1,0:T(8,128)(2,1)S(1)} %get-tuple-element.111), channel_id=1, source_target_pairs={{0,128},{16,144},{32,160},{48,176},{64,192},{80,208},{96,224},{112... | collective-permute-start | bytes 294920 | tf_op jit(solution)/shard_map/ppermute | solution.py:303
  73.6 2.3 %collective-permute-start.14 = (bf16[4,24,512]{2,1,0:T(8,128)(2,1)S(1)}, bf16[4,24,512]{2,1,0:T(8,128)(2,1)S(1)}, u32[]{:S(2)}, u32[]{:S(2)}) collective-permute-start(bf16[4,24,512]{2,1,0:T(8,128)(2,1)S(1)} %get-tuple-element.113), channel_id=1, source_target_pairs={{0,192},{16,208},{32,224},{48,240},{64,0},{80,16},{96,32},{112,48}... | collective-permute-start | bytes 294920 | tf_op jit(solution)/shard_map/ppermute | solution.py:303
  75.9 1.9 %shard_map.132 = bf16[512,512]{1,0:T(8,128)(2,1)} custom-call(s32[1]{0:T(128)} %bitcast.core_ref, bf16[384,128]{1,0:T(8,128)(2,1)S(1)} %get-tuple-element.88.mine_ref, bf16[384,128]{1,0:T(8,128)(2,1)S(1)} %collective-permute-done.9.other_ref, bf16[512,512]{1,0:T(8,128)(2,1)S(1)} %bitcast.29, f32[1,128]{1,0:T(1,128)S(1)} %copy-done.7, ...), custom_call_target="tpu_custom_call" | custom-call | flops 1073741824 | bytes 1048576 | tf_op jit(solution)/shard_map/pallas_call | solution.py:253
  77.8 2.6 %shard_map.131 = (bf16[512,1024]{1,0:T(8,128)(2,1)}, bf16[512,1024]{1,0:T(8,128)(2,1)}) custom-call(s32[1]{0:T(128)} %bitcast.core_ref, bf16[384,512]{1,0:T(8,128)(2,1)S(1)} %bitcast.24, bf16[8,384,128]{2,1,0:T(8,128)(2,1)S(1)} %all_to_all.11.grads_ref.mine_ref, bf16[8,384,128]{2,1,0:T(8,128)(2,1)S(1)} %collective-permute-done.15.other_ref), custom_call_target="tpu_custom_call" | custom-call | flops 805306368 | bytes 4194304 | tf_op jit(solution)/shard_map/pallas_call | solution.py:253
  80.5 4.1 %collective-permute-start.16 = (bf16[24,512]{1,0:T(8,128)(2,1)S(1)}, bf16[24,512]{1,0:T(8,128)(2,1)S(1)}, u32[]{:S(2)}, u32[]{:S(2)}) collective-permute-start(bf16[24,512]{1,0:T(8,128)(2,1)S(1)} %get-tuple-element.127), channel_id=1, source_target_pairs={{0,32},{16,48},{32,0},{48,16},{64,96},{80,112},{96,64},{112,80},{1... | collective-permute-start | bytes 73736 | tf_op jit(solution)/shard_map/ppermute | solution.py:300
  84.7 3.6 %collective-permute-start.18 = (bf16[24,512]{1,0:T(8,128)(2,1)S(1)}, bf16[24,512]{1,0:T(8,128)(2,1)S(1)}, u32[]{:S(2)}, u32[]{:S(2)}) collective-permute-start(bf16[24,512]{1,0:T(8,128)(2,1)S(1)} %get-tuple-element.129), channel_id=1, source_target_pairs={{0,48},{16,0},{32,16},{48,32},{64,112},{80,64},{96,80},{112,96},{1... | collective-permute-start | bytes 73736 | tf_op jit(solution)/shard_map/ppermute | solution.py:300
  88.3 1.3 %shard_map.134 = bf16[512,512]{1,0:T(8,128)(2,1)} custom-call(s32[1]{0:T(128)} %bitcast.core_ref, bf16[384,128]{1,0:T(8,128)(2,1)S(1)} %get-tuple-element.88.mine_ref, bf16[384,128]{1,0:T(8,128)(2,1)S(1)} %collective-permute-done.9.other_ref, bf16[4,384,512]{2,1,0:T(8,128)(2,1)S(1)} %get-tuple-element.130.probs_ref), custom_call_target="tpu_custom_call" | custom-call | flops 1073741824 | bytes 1048576 | tf_op jit(solution)/shard_map/pallas_call | solution.py:253
  (49 shorter events, 8.6 us)
Async XLA Ops:
  0.7 11.0 %collective-permute-start.2 = (bf16[24,512]{1,0:T(8,128)(2,1)}, bf16[24,512]{1,0:T(8,128)(2,1)S(1)}, u32[]{:S(2)}, u32[]{:S(2)}) collective-permute-start(bf16[24,512]{1,0:T(8,128)(2,1)} %rows_ref), channel_id=1, source_target_pairs={{0,32},{16,48},{32,0},{48,16},{64,96},{80,112},{96,64},{112,80},{1... | collective-permute-start | bytes 73736 | tf_op jit(solution)/shard_map/ppermute | solution.py:300
  8.5 3.8 %collective-permute-start.1 = (bf16[24,512]{1,0:T(8,128)(2,1)}, bf16[24,512]{1,0:T(8,128)(2,1)S(1)}, u32[]{:S(2)}, u32[]{:S(2)}) collective-permute-start(bf16[24,512]{1,0:T(8,128)(2,1)} %rows_ref), channel_id=1, source_target_pairs={{0,48},{16,0},{32,16},{48,32},{64,112},{80,64},{96,80},{112,96},{1... | collective-permute-start | bytes 73736 | tf_op jit(solution)/shard_map/ppermute | solution.py:300
  8.5 5.1 %collective-permute-start = (bf16[24,512]{1,0:T(8,128)(2,1)}, bf16[24,512]{1,0:T(8,128)(2,1)S(1)}, u32[]{:S(2)}, u32[]{:S(2)}) collective-permute-start(bf16[24,512]{1,0:T(8,128)(2,1)} %rows_ref), channel_id=1, source_target_pairs={{0,16},{16,32},{32,48},{48,0},{64,80},{80,96},{96,112},{112,64},{1... | collective-permute-start | bytes 73736 | tf_op jit(solution)/shard_map/ppermute | solution.py:300
  11.6 4.1 %copy-start = (bf16[1,512,1024]{2,1,0:T(8,128)(2,1)S(1)}, bf16[1,512,1024]{2,1,0:T(8,128)(2,1)}, u32[]{:S(2)}) copy-start(bf16[1,512,1024]{2,1,0:T(8,128)(2,1)} %param.10) | copy-start | bytes 3145732
  13.6 10.6 %collective-permute-start.7 = (bf16[512,1024]{1,0:T(8,128)(2,1)S(1)}, bf16[512,1024]{1,0:T(8,128)(2,1)S(1)}, u32[]{:S(2)}, u32[]{:S(2)}) collective-permute-start(bf16[512,1024]{1,0:T(8,128)(2,1)S(1)} %bitcast.18), channel_id=1, source_target_pairs={{0,1},{1,0},{2,3},{3,2},{4,5},{5,4},{6,7},{7,6},{8,9},{9,8},{10,11... | collective-permute-start | bytes 3145736 | tf_op jit(solution)/shard_map/ppermute | solution.py:279
  15.7 8.5 %collective-permute-start.6 = (bf16[512,1024]{1,0:T(8,128)(2,1)S(1)}, bf16[512,1024]{1,0:T(8,128)(2,1)S(1)}, u32[]{:S(2)}, u32[]{:S(2)}) collective-permute-start(bf16[512,1024]{1,0:T(8,128)(2,1)S(1)} %bitcast.15), channel_id=1, source_target_pairs={{0,1},{1,0},{2,3},{3,2},{4,5},{5,4},{6,7},{7,6},{8,9},{9,8},{10,11... | collective-permute-start | bytes 3145736 | tf_op jit(solution)/shard_map/ppermute | solution.py:279
  15.8 5.5 %collective-permute-start.5 = (bf16[4,24,512]{2,1,0:T(8,128)(2,1)S(1)}, bf16[4,24,512]{2,1,0:T(8,128)(2,1)S(1)}, u32[]{:S(2)}, u32[]{:S(2)}) collective-permute-start(bf16[4,24,512]{2,1,0:T(8,128)(2,1)S(1)} %shard_map.120.refs_0_), channel_id=1, source_target_pairs={{0,128},{16,144},{32,160},{48,176},{64,192},{80,208},{96,224},{112... | collective-permute-start | bytes 294920 | tf_op jit(solution)/shard_map/ppermute | solution.py:303
  18.7 5.0 %collective-permute-start.4 = (bf16[4,24,512]{2,1,0:T(8,128)(2,1)S(1)}, bf16[4,24,512]{2,1,0:T(8,128)(2,1)S(1)}, u32[]{:S(2)}, u32[]{:S(2)}) collective-permute-start(bf16[4,24,512]{2,1,0:T(8,128)(2,1)S(1)} %shard_map.120.refs_0_), channel_id=1, source_target_pairs={{0,192},{16,208},{32,224},{48,240},{64,0},{80,16},{96,32},{112,48}... | collective-permute-start | bytes 294920 | tf_op jit(solution)/shard_map/ppermute | solution.py:303
  19.5 4.7 %collective-permute-start.3 = (bf16[4,24,512]{2,1,0:T(8,128)(2,1)S(1)}, bf16[4,24,512]{2,1,0:T(8,128)(2,1)S(1)}, u32[]{:S(2)}, u32[]{:S(2)}) collective-permute-start(bf16[4,24,512]{2,1,0:T(8,128)(2,1)S(1)} %shard_map.120.refs_0_), channel_id=1, source_target_pairs={{0,64},{16,80},{32,96},{48,112},{64,128},{80,144},{96,160},{112,17... | collective-permute-start | bytes 294920 | tf_op jit(solution)/shard_map/ppermute | solution.py:303
  24.2 3.5 %collective-permute-start.8 = (bf16[384,512]{1,0:T(8,128)(2,1)S(1)}, bf16[384,512]{1,0:T(8,128)(2,1)S(1)}, u32[]{:S(2)}, u32[]{:S(2)}) collective-permute-start(bf16[384,512]{1,0:T(8,128)(2,1)S(1)} %bitcast.22), channel_id=1, source_target_pairs={{0,1},{1,0},{2,3},{3,2},{4,5},{5,4},{6,7},{7,6},{8,9},{9,8},{10,11... | collective-permute-start | bytes 1179656 | tf_op jit(solution)/shard_map/ppermute | solution.py:279
  28.4 17.2 %copy-start.4 = (f32[1,128]{1,0:T(1,128)S(1)}, f32[1,128]{1,0:T(1,128)}, u32[]{:S(2)}) copy-start(f32[1,128]{1,0:T(1,128)} %gain_ref.6) | copy-start | bytes 1540
  28.4 19.3 %copy-start.5 = (bf16[1,512,512]{2,1,0:T(8,128)(2,1)S(1)}, bf16[1,512,512]{2,1,0:T(8,128)(2,1)}, u32[]{:S(2)}) copy-start(bf16[1,512,512]{2,1,0:T(8,128)(2,1)} %param.9) | copy-start | bytes 1572868
  28.4 19.3 %copy-start.7 = (f32[1,128]{1,0:T(1,128)S(1)}, f32[1,128]{1,0:T(1,128)}, u32[]{:S(2)}) copy-start(f32[1,128]{1,0:T(1,128)} %gain_ref.7) | copy-start | bytes 1540
  45.8 2.9 %copy-start.2 = (bf16[1,512,512]{2,1,0:T(8,128)(2,1)S(1)}, bf16[1,512,512]{2,1,0:T(8,128)(2,1)}, u32[]{:S(2)}) copy-start(bf16[1,512,512]{2,1,0:T(8,128)(2,1)} %param.15) | copy-start | bytes 1572868
  45.8 2.8 %collective-permute-start.9 = (bf16[384,128]{1,0:T(8,128)(2,1)S(1)}, bf16[384,128]{1,0:T(8,128)(2,1)S(1)}, u32[]{:S(2)}, u32[]{:S(2)}) collective-permute-start(bf16[384,128]{1,0:T(8,128)(2,1)S(1)} %get-tuple-element.88.mine_ref), channel_id=1, source_target_pairs={{0,1},{1,0},{2,3},{3,2},{4,5},{5,4},{6,7},{7,6},{8,9},{9,8},{10,11... | collective-permute-start | bytes 294920 | tf_op jit(solution)/shard_map/ppermute | solution.py:279
  51.3 1.4 %collective-permute-start.10 = (bf16[384,128]{1,0:T(8,128)(2,1)S(1)}, bf16[384,128]{1,0:T(8,128)(2,1)S(1)}, u32[]{:S(2)}, u32[]{:S(2)}) collective-permute-start(bf16[384,128]{1,0:T(8,128)(2,1)S(1)} %get-tuple-element.97), channel_id=1, source_target_pairs={{0,1},{1,0},{2,3},{3,2},{4,5},{5,4},{6,7},{7,6},{8,9},{9,8},{10,11... | collective-permute-start | bytes 294920 | tf_op jit(solution)/shard_map/ppermute | solution.py:279
  68.8 2.6 %collective-permute-start.11 = (bf16[384,512]{1,0:T(8,128)(2,1)S(1)}, bf16[384,512]{1,0:T(8,128)(2,1)S(1)}, u32[]{:S(2)}, u32[]{:S(2)}) collective-permute-start(bf16[384,512]{1,0:T(8,128)(2,1)S(1)} %shard_map.128), channel_id=1, source_target_pairs={{0,1},{1,0},{2,3},{3,2},{4,5},{5,4},{6,7},{7,6},{8,9},{9,8},{10,11... | collective-permute-start | bytes 1179656 | tf_op jit(solution)/shard_map/ppermute | solution.py:279
  71.5 6.3 %collective-permute-start.15 = (bf16[8,384,128]{2,1,0:T(8,128)(2,1)S(1)}, bf16[8,384,128]{2,1,0:T(8,128)(2,1)S(1)}, u32[]{:S(2)}, u32[]{:S(2)}) collective-permute-start(bf16[8,384,128]{2,1,0:T(8,128)(2,1)S(1)} %all_to_all.11.grads_ref.mine_ref), channel_id=1, source_target_pairs={{0,1},{1,0},{2,3},{3,2},{4,5},{5,4},{6,7},{7,6},{8,9},{9,8},{10,11... | collective-permute-start | bytes 2359304 | tf_op jit(solution)/shard_map/ppermute | solution.py:279
  71.9 8.5 %collective-permute-start.12 = (bf16[4,24,512]{2,1,0:T(8,128)(2,1)S(1)}, bf16[4,24,512]{2,1,0:T(8,128)(2,1)S(1)}, u32[]{:S(2)}, u32[]{:S(2)}) collective-permute-start(bf16[4,24,512]{2,1,0:T(8,128)(2,1)S(1)} %get-tuple-element.111), channel_id=1, source_target_pairs={{0,128},{16,144},{32,160},{48,176},{64,192},{80,208},{96,224},{112... | collective-permute-start | bytes 294920 | tf_op jit(solution)/shard_map/ppermute | solution.py:303
  73.2 7.3 %collective-permute-start.13 = (bf16[4,24,512]{2,1,0:T(8,128)(2,1)S(1)}, bf16[4,24,512]{2,1,0:T(8,128)(2,1)S(1)}, u32[]{:S(2)}, u32[]{:S(2)}) collective-permute-start(bf16[4,24,512]{2,1,0:T(8,128)(2,1)S(1)} %get-tuple-element.112), channel_id=1, source_target_pairs={{0,64},{16,80},{32,96},{48,112},{64,128},{80,144},{96,160},{112,17... | collective-permute-start | bytes 294920 | tf_op jit(solution)/shard_map/ppermute | solution.py:303
  73.6 6.9 %collective-permute-start.14 = (bf16[4,24,512]{2,1,0:T(8,128)(2,1)S(1)}, bf16[4,24,512]{2,1,0:T(8,128)(2,1)S(1)}, u32[]{:S(2)}, u32[]{:S(2)}) collective-permute-start(bf16[4,24,512]{2,1,0:T(8,128)(2,1)S(1)} %get-tuple-element.113), channel_id=1, source_target_pairs={{0,192},{16,208},{32,224},{48,240},{64,0},{80,16},{96,32},{112,48}... | collective-permute-start | bytes 294920 | tf_op jit(solution)/shard_map/ppermute | solution.py:303
  80.5 9.0 %collective-permute-start.16 = (bf16[24,512]{1,0:T(8,128)(2,1)S(1)}, bf16[24,512]{1,0:T(8,128)(2,1)S(1)}, u32[]{:S(2)}, u32[]{:S(2)}) collective-permute-start(bf16[24,512]{1,0:T(8,128)(2,1)S(1)} %get-tuple-element.127), channel_id=1, source_target_pairs={{0,32},{16,48},{32,0},{48,16},{64,96},{80,112},{96,64},{112,80},{1... | collective-permute-start | bytes 73736 | tf_op jit(solution)/shard_map/ppermute | solution.py:300
  84.7 4.9 %collective-permute-start.17 = (bf16[24,512]{1,0:T(8,128)(2,1)S(1)}, bf16[24,512]{1,0:T(8,128)(2,1)S(1)}, u32[]{:S(2)}, u32[]{:S(2)}) collective-permute-start(bf16[24,512]{1,0:T(8,128)(2,1)S(1)} %get-tuple-element.128), channel_id=1, source_target_pairs={{0,16},{16,32},{32,48},{48,0},{64,80},{80,96},{96,112},{112,64},{1... | collective-permute-start | bytes 73736 | tf_op jit(solution)/shard_map/ppermute | solution.py:300
  84.7 4.9 %collective-permute-start.18 = (bf16[24,512]{1,0:T(8,128)(2,1)S(1)}, bf16[24,512]{1,0:T(8,128)(2,1)S(1)}, u32[]{:S(2)}, u32[]{:S(2)}) collective-permute-start(bf16[24,512]{1,0:T(8,128)(2,1)S(1)} %get-tuple-element.129), channel_id=1, source_target_pairs={{0,48},{16,0},{32,16},{48,32},{64,112},{80,64},{96,80},{112,96},{1... | collective-permute-start | bytes 73736 | tf_op jit(solution)/shard_map/ppermute | solution.py:300
  (3 other events, 5.6 us)
